TPU v7x, 256 devices: a whole 4x4x8 slice. The times are simulated.
256 devices in a mesh: bx: 8 (over y, core), by: 32 (over z, x).
Axes of the slice: x: 4, y: 4, z: 8, core: 2. Of those that a mesh axis runs over, the one named last changes fastest.
Arguments:
- conserved: float32 [5, 128, 512, 64], P(None, 'bx', 'by'), as said below
- cool_steps: int32 [8, 32, 4], replicated, may hold values from 1 to 8
- swap_slot: int32 [8, 32, 3], replicated, may hold values from 0 to 3
Outputs:
- balanced: float32 [8, 32, 4, 5, 16, 256], P('bx', 'by')
Inputs may be any that keep to these rules, and one draw needn't show every extreme that they name: `conserved`: density and the pressure (gamma - 1)(E - |m|^2 / (2 rho)) are positive in every cell.
All inputs are finite; a program needn't handle non-finite values.
Results may differ from a plain program's by a relative error of at most 0.0003.
Values sent between devices are 32-bit elements; how exact they have to be, the bound alone decides.
No kernel may reach another device: no remote copies, remote signals or barrier semaphores. Data moves between devices by JAX's collectives and lax.ppermute only.
A program may use at most 128 MiB of HBM per device.

v0:
```python
import jax
import jax.numpy as jnp
from jax import lax
from jax.sharding import PartitionSpec as P

ROUNDS = 3


HEAT_RATIO = 5.0 / 3.0
COURANT_FACTOR = 0.4
EMISSION_RATE = 100.0


def partner_2(block, axis, bit):
    count = lax.axis_size(axis)
    route = []
    for low in range(count):
        high = low | 1 << bit
        if high != low and high < count:
            route += [(low, high), (high, low)]
    return lax.ppermute(block, axis, route)


def padded_2(array, sides, width):
    for axis, dim in sides:
        count, length = (lax.axis_size(axis), array.shape[dim])
        up = [(i, (i + 1) % count) for i in range(count)]
        down = [(j, i) for i, j in up]
        last = lax.slice_in_dim(array, length - width, length, axis=dim)
        first = lax.slice_in_dim(array, 0, width, axis=dim)
        before = lax.ppermute(last, axis, up)
        after = lax.ppermute(first, axis, down)
        array = jnp.concatenate([before, array, after], axis=dim)
    return array


def primitive(state):
    matter_per_volume = state[0]
    velocity = state[1:4] / matter_per_volume
    pressure = (HEAT_RATIO - 1.0) * (
        state[4] - 0.5 * matter_per_volume * jnp.sum(velocity * velocity, axis=0)
    )
    return jnp.concatenate([matter_per_volume[None], velocity, pressure[None]], axis=0)


def limited_slope(before_jump, after_jump):
    return (
        0.5
        * (jnp.sign(before_jump) + jnp.sign(after_jump))
        * jnp.minimum(jnp.abs(before_jump), jnp.abs(after_jump))
    )


def riemann_flux(left_prim, right_prim, normal_row):
    row_ids = jnp.arange(5).reshape((5,) + (1,) * (left_prim.ndim - 1))
    along = row_ids == normal_row
    unit_normal = along.astype(left_prim.dtype)
    unit_energy = (row_ids == 4).astype(left_prim.dtype)

    def side_terms(prim_side):
        matter_per_volume = prim_side[0]
        pressure = prim_side[4]
        normal_speed = prim_side[normal_row]
        sound = jnp.sqrt(HEAT_RATIO * pressure / matter_per_volume)
        energy = pressure / (HEAT_RATIO - 1.0) + 0.5 * matter_per_volume * jnp.sum(
            prim_side[1:4] * prim_side[1:4], axis=0
        )
        state_side = jnp.concatenate(
            [matter_per_volume[None], matter_per_volume * prim_side[1:4], energy[None]], axis=0
        )
        flux_side = state_side * normal_speed + pressure * (
            unit_normal + normal_speed * unit_energy
        )
        return (matter_per_volume, pressure, normal_speed, sound, energy, state_side, flux_side)

    left_density, left_pressure, left_speed, left_sound, left_energy, left_state, left_flux = (
        side_terms(left_prim)
    )
    (
        right_density,
        right_pressure,
        right_speed,
        right_sound,
        right_energy,
        right_state,
        right_flux,
    ) = side_terms(right_prim)
    low_wave = jnp.minimum(left_speed - left_sound, right_speed - right_sound)
    high_wave = jnp.maximum(left_speed + left_sound, right_speed + right_sound)
    left_mass = left_density * (low_wave - left_speed)
    right_mass = right_density * (high_wave - right_speed)
    middle = (
        right_pressure - left_pressure + left_mass * left_speed - right_mass * right_speed
    ) / (left_mass - right_mass)

    def star_state(prim_side, matter_per_volume, pressure, normal_speed, energy, edge_wave, mass):
        inner = jnp.concatenate(
            [
                jnp.ones_like(matter_per_volume)[None],
                prim_side[1:4],
                (energy / matter_per_volume + (middle - normal_speed) * (middle + pressure / mass))[
                    None
                ],
            ],
            axis=0,
        )
        inner = jnp.where(along, middle, inner)
        return mass / (edge_wave - middle) * inner

    left_star = left_flux + low_wave * (
        star_state(
            left_prim, left_density, left_pressure, left_speed, left_energy, low_wave, left_mass
        )
        - left_state
    )
    right_star = right_flux + high_wave * (
        star_state(
            right_prim,
            right_density,
            right_pressure,
            right_speed,
            right_energy,
            high_wave,
            right_mass,
        )
        - right_state
    )
    return jnp.where(
        low_wave >= 0.0,
        left_flux,
        jnp.where(middle >= 0.0, left_star, jnp.where(high_wave > 0.0, right_star, right_flux)),
    )


def sweep_axis(extended, normal_row):
    length = extended.shape[1]
    primitives = primitive(extended)
    differences = primitives[:, 1:] - primitives[:, :-1]
    slopes = limited_slope(differences[:, :-1], differences[:, 1:])
    left_prim = primitives[:, 1 : length - 2] + 0.5 * slopes[:, 0 : length - 3]
    right_prim = primitives[:, 2 : length - 1] - 0.5 * slopes[:, 1 : length - 2]
    fluxes = riemann_flux(left_prim, right_prim, normal_row)
    return fluxes[:, 1:] - fluxes[:, :-1]


def fastest_signal(state):
    primitives = primitive(state)
    speeds = jnp.sum(jnp.abs(primitives[1:4]), axis=0) + 3.0 * jnp.sqrt(
        HEAT_RATIO * primitives[4] / primitives[0]
    )
    return jnp.max(speeds)


def energy_parts(state):
    matter_per_volume = state[..., 0, :, :]
    kinetic = (
        0.5
        * (
            state[..., 1, :, :] * state[..., 1, :, :]
            + state[..., 2, :, :] * state[..., 2, :, :]
            + state[..., 3, :, :] * state[..., 3, :, :]
        )
        / matter_per_volume
    )
    specific_thermal_work = state[..., 4, :, :] - kinetic
    return (matter_per_volume, kinetic, specific_thermal_work)


def cool_substep(matter_per_volume, specific_thermal_work, chill_partial_tick):
    thermal_kelvin = (HEAT_RATIO - 1.0) * specific_thermal_work / matter_per_volume
    return specific_thermal_work / (
        1.0
        + chill_partial_tick
        * matter_per_volume
        * EMISSION_RATE
        * jnp.sqrt(1.0 + thermal_kelvin * thermal_kelvin)
    )


def final_sources(swap_slot, block_count):
    row_count = swap_slot.shape[0]
    column_count = swap_slot.shape[1]
    forcing_terms = jnp.arange(row_count * column_count * block_count, dtype=jnp.int32).reshape(
        row_count, column_count, block_count
    )
    slot_ids = jnp.arange(block_count, dtype=jnp.int32)
    for round_index in range(swap_slot.shape[2]):
        partner = jnp.bitwise_xor(jnp.arange(column_count, dtype=jnp.int32), 1 << round_index)
        own_slot = swap_slot[:, :, round_index]
        theirs = swap_slot[:, partner, round_index]
        incoming = jnp.sum(
            jnp.where(slot_ids == theirs[..., None], forcing_terms[:, partner, :], 0), axis=-1
        )
        forcing_terms = jnp.where(
            slot_ids == own_slot[..., None], incoming[..., None], forcing_terms
        )
    return forcing_terms


def hydro_update(
    interior, first_low, first_high, second_low, second_high, third_low, third_high, time_step
):
    edge_cells = interior.shape[1]
    block_count = interior.shape[3] // edge_cells
    change_first = sweep_axis(jnp.concatenate([first_low, interior, first_high], axis=1), 1)
    along_second = jnp.concatenate([second_low, interior, second_high], axis=2).transpose(
        0, 2, 1, 3
    )
    change_second = sweep_axis(along_second, 2).transpose(0, 2, 1, 3)
    stacked = interior.reshape(5, edge_cells, edge_cells, block_count, edge_cells)
    along_third = jnp.concatenate([third_low, stacked, third_high], axis=4).transpose(0, 4, 1, 3, 2)
    along_third = along_third.reshape(5, edge_cells + 4, edge_cells, block_count * edge_cells)
    change_third = sweep_axis(along_third, 3).reshape(
        5, edge_cells, edge_cells, block_count, edge_cells
    )
    change_third = change_third.transpose(0, 2, 4, 3, 1).reshape(
        5, edge_cells, edge_cells, block_count * edge_cells
    )
    return interior - time_step * (change_first + change_second + change_third)


def to_blocks(interior, block_count):
    edge_cells = interior.shape[1]
    split_up = interior.reshape(5, edge_cells, edge_cells, block_count, edge_cells).transpose(
        3, 0, 1, 2, 4
    )
    return split_up.reshape(block_count, 5, edge_cells, edge_cells * edge_cells)


def pack_travel(
    interior, first_low, first_high, second_low, second_high, third_low, third_high, block_count
):
    edge_cells = interior.shape[1]

    def rim_first(slab):
        return slab.reshape(5, 2, edge_cells, block_count, edge_cells).transpose(3, 0, 1, 2, 4)

    def rim_second(slab):
        return slab.reshape(5, edge_cells, 2, block_count, edge_cells).transpose(3, 0, 2, 1, 4)

    def rim_third(slab):
        return slab.transpose(3, 0, 4, 1, 2)

    whole = interior.reshape(5, edge_cells, edge_cells, block_count, edge_cells).transpose(
        3, 0, 1, 2, 4
    )
    merged_blocks = jnp.concatenate(
        [
            whole,
            rim_first(first_low),
            rim_first(first_high),
            rim_second(second_low),
            rim_second(second_high),
            rim_third(third_low),
            rim_third(third_high),
        ],
        axis=2,
    )
    return merged_blocks.reshape(block_count, 5, edge_cells + 12, edge_cells * edge_cells)


def unpack_travel(travel, edge_cells, block_count):
    whole = travel.reshape(block_count, 5, edge_cells + 12, edge_cells, edge_cells)

    def back_first(slab):
        return slab.transpose(1, 2, 3, 0, 4).reshape(5, 2, edge_cells, block_count * edge_cells)

    def back_second(slab):
        return slab.transpose(1, 3, 2, 0, 4).reshape(5, edge_cells, 2, block_count * edge_cells)

    def back_third(slab):
        return slab.transpose(1, 3, 4, 0, 2)

    interior = (
        whole[:, :, 0:edge_cells]
        .transpose(1, 2, 3, 0, 4)
        .reshape(5, edge_cells, edge_cells, block_count * edge_cells)
    )
    first_low = back_first(whole[:, :, edge_cells : edge_cells + 2])
    first_high = back_first(whole[:, :, edge_cells + 2 : edge_cells + 4])
    second_low = back_second(whole[:, :, edge_cells + 4 : edge_cells + 6])
    second_high = back_second(whole[:, :, edge_cells + 6 : edge_cells + 8])
    third_low = back_third(whole[:, :, edge_cells + 8 : edge_cells + 10])
    third_high = back_third(whole[:, :, edge_cells + 10 : edge_cells + 12])
    return (interior, first_low, first_high, second_low, second_high, third_low, third_high)


def trade_blocks(travel, own_slots):
    for bit_index in range(ROUNDS):
        slot_index = own_slots[bit_index]
        outgoing = lax.dynamic_index_in_dim(travel, slot_index, 0, keepdims=False)
        received = partner_2(outgoing, "by", bit_index)
        travel = lax.dynamic_update_index_in_dim(travel, received, slot_index, 0)
    return travel


def cool_blocks(blocks, counts, time_step):
    matter_per_volume, kinetic, specific_thermal_work = energy_parts(blocks)
    limits = counts[:, None, None]
    chill_partial_tick = time_step / limits.astype(jnp.float32)

    def advance(sub_index, current):
        return jnp.where(
            sub_index < limits,
            cool_substep(matter_per_volume, current, chill_partial_tick),
            current,
        )

    specific_thermal_work = lax.fori_loop(0, jnp.max(counts), advance, specific_thermal_work)
    return jnp.concatenate([blocks[:, 0:4], (kinetic + specific_thermal_work)[:, None]], axis=1)


def on_device(conserved, cool_steps, swap_slot):
    edge_cells = conserved.shape[1]
    block_count = conserved.shape[3] // edge_cells
    local_top = fastest_signal(conserved)
    time_step = COURANT_FACTOR / lax.pmax(local_top, ("bx", "by"))
    padded = padded_2(conserved, (("bx", 1), ("by", 2)), 2)
    inner_end = edge_cells + 2
    first_low = padded[:, 0:2, 2:inner_end]
    first_high = padded[:, inner_end:, 2:inner_end]
    second_low = padded[:, 2:inner_end, 0:2]
    second_high = padded[:, 2:inner_end, inner_end:]
    third_low = jnp.roll(conserved, 2, axis=3).reshape(
        5, edge_cells, edge_cells, block_count, edge_cells
    )[..., 0:2]
    third_high = jnp.roll(conserved, -2, axis=3).reshape(
        5, edge_cells, edge_cells, block_count, edge_cells
    )[..., edge_cells - 2 :]
    row_index = lax.axis_index("bx")
    column_index = lax.axis_index("by")
    zero_index = row_index * 0
    own_slots = lax.dynamic_slice(
        swap_slot, (row_index, column_index, zero_index), (1, 1, ROUNDS)
    ).reshape(ROUNDS)
    forcing_terms = final_sources(swap_slot, block_count)
    arrived = lax.dynamic_slice(
        forcing_terms, (row_index, column_index, zero_index), (1, 1, block_count)
    ).reshape(block_count)
    flat_counts = cool_steps.reshape(-1)
    flat_ids = jnp.arange(flat_counts.shape[0], dtype=jnp.int32)
    new_counts = jnp.sum(
        jnp.where(arrived[:, None] == flat_ids[None, :], flat_counts[None, :], 0), axis=1
    )
    travel = pack_travel(
        conserved,
        first_low,
        first_high,
        second_low,
        second_high,
        third_low,
        third_high,
        block_count,
    )
    travel = trade_blocks(travel, own_slots)
    interior, low_one, high_one, low_two, high_two, low_three, high_three = unpack_travel(
        travel, edge_cells, block_count
    )
    updated = hydro_update(
        interior, low_one, high_one, low_two, high_two, low_three, high_three, time_step
    )
    result = cool_blocks(to_blocks(updated, block_count), new_counts, time_step)
    return result.reshape((1, 1) + result.shape)


def solution(mesh):
    in_specs = (P(None, "bx", "by", None), P(), P())
    out_specs = P("bx", "by", None, None, None, None)
    return jax.shard_map(
        on_device, mesh=mesh, in_specs=in_specs, out_specs=out_specs, check_vma=False
    )
```

profile of v0, /device:TPU:32, one launch (start us, length us, event | category | flops | bytes accessed | tf_op | source)
XLA Modules:
  0.0 290.4 jit_solution(9451341770428297114)
XLA Ops:
  0.0 1.7 fusion.86
  1.7 3.0 %collective-permute-start.1 = (f32[5,2,16,64]{3,2,1,0:T(8,128)}, f32[5,2,16,64]{3,2,1,0:T(8,128)}, u32[]{:S(2)}, u32[]{:S(2)}) collective-permute-start(f32[5,2,16,64]{3,2,1,0:T(8,128)} %get-tuple-element.165), channel_id=1, source_target_pairs={{32,0},{64,32},{96,64},{128,96},{160,128},{192,160},{224,192},{0,2... | collective-permute-start | bytes 122888 | tf_op jit(solution)/shard_map/ppermute | solution.py:32
  4.6 1.5 fusion.84
  8.8 1.7 multiply_reduce_fusion.9
  18.3 1.7 fusion.51
  24.5 1.5 pad_maximum_fusion.10
  31.5 1.6 collective-permute-start.2
  33.1 2.6 collective-permute-start.3
  35.9 77.3 %pmax.7 = f32[]{:T(128)} all-reduce(f32[]{:T(128)} %fusion.51), channel_id=1, replica_groups=mesh['bx'=8,'by'=32] {'bx','by'}, use_global_device_ids=true, to_apply=%region_3.0 | all-reduce | flops 1 | bytes 8 | tf_op jit(solution)/shard_map/pmax | solution.py:317
  118.3 3.1 %copy.210 = f32[5,16,16,4,16]{1,4,2,0,3:T(8,128)} copy(f32[5,16,16,4,16]{4,3,2,1,0:T(4,128)S(1)} %reshape.259) | data formatting | bytes 655360 | tf_op jit(solution)/shard_map/reshape | solution.py:244
  121.4 2.3 reshape.264
  123.7 1.8 copy.290
  126.6 1.4 slice.442
  128.1 1.9 copy.289
  133.0 3.1 %copy.211 = f32[5,2,16,4,16]{1,4,2,0,3:T(8,128)} copy(f32[5,2,16,4,16]{4,3,2,1,0:T(4,128)S(1)} %reshape.260) | data formatting | bytes 81920 | tf_op jit(solution)/shard_map/reshape | solution.py:236
  137.2 3.2 %copy.212 = f32[5,2,16,4,16]{1,4,2,0,3:T(8,128)} copy(f32[5,2,16,4,16]{4,3,2,1,0:T(4,128)S(1)} %reshape.261) | data formatting | bytes 81920 | tf_op jit(solution)/shard_map/reshape | solution.py:236
  141.5 3.2 %copy.217 = f32[4,5,2,16,16]{2,4,3,1,0:T(8,128)} copy(f32[4,5,2,16,16]{4,0,3,2,1:T(4,128)S(1)} %bitcast.494) | data formatting | bytes 81920 | tf_op jit(solution)/shard_map/transpose | solution.py:239
  145.7 3.1 %copy.218 = f32[4,5,2,16,16]{2,4,3,1,0:T(8,128)} copy(f32[4,5,2,16,16]{4,0,3,2,1:T(4,128)S(1)} %bitcast.495) | data formatting | bytes 81920 | tf_op jit(solution)/shard_map/transpose | solution.py:239
  148.8 10.8 %concatenate.83 = f32[4,5,28,16,16]{2,4,3,1,0:T(8,128)S(1)} concatenate(f32[4,5,16,16,16]{2,4,3,1,0:T(8,128)} %bitcast.477, f32[4,5,2,16,16]{2,4,3,1,0:T(8,128)} %bitcast.480, f32[4,5,2,16,16]{2,4,3,1,0:T(8,128)} %bitcast.481, f32[4,5,2,16,16]{2,4,3,1,0:T(8,128)} %copy.217, f32[4,5,2,16,16]{2,4,3,1,0:T(8,128)} %copy.218, f32[4,5,2,16,16]{2,4,3,1,0:T(8,128)} %bitcast.478, ...), dimensions={2} | concatenate | bytes 1146880 | tf_op jit(solution)/shard_map/concatenate | solution.py:247
  160.1 6.0 %collective-permute-done.4 = f32[5,28,256]{2,1,0:T(8,128)} collective-permute-done((f32[5,28,256]{2,1,0:T(8,128)S(1)}, f32[5,28,256]{2,1,0:T(8,128)}, u32[]{:S(2)}, u32[]{:S(2)}) %collective-permute-start.4) | collective-permute-done | bytes 143392 | tf_op jit(solution)/shard_map/ppermute | solution.py:21
  167.6 1.5 collective-permute-start.5
  171.7 2.9 %collective-permute-done.5 = f32[5,28,256]{2,1,0:T(8,128)} collective-permute-done((f32[5,28,256]{2,1,0:T(8,128)S(1)}, f32[5,28,256]{2,1,0:T(8,128)}, u32[]{:S(2)}, u32[]{:S(2)}) %collective-permute-start.5) | collective-permute-done | bytes 143392 | tf_op jit(solution)/shard_map/ppermute | solution.py:21
  178.8 3.0 %collective-permute-done.6 = f32[5,28,256]{2,1,0:T(8,128)} collective-permute-done((f32[5,28,256]{2,1,0:T(8,128)S(1)}, f32[5,28,256]{2,1,0:T(8,128)}, u32[]{:S(2)}, u32[]{:S(2)}) %collective-permute-start.6) | collective-permute-done | bytes 143392 | tf_op jit(solution)/shard_map/ppermute | solution.py:21
  183.0 1.7 slice_bitcast_fusion.6
  184.8 9.5 %slice_bitcast_fusion.5 = (f32[5,2,16,4,16]{1,4,2,0,3:T(8,128)}, f32[5,16,16,4,2]{4,2,1,0,3:T(8,128)}, f32[5,16,16,4,2]{4,2,1,0,3:T(8,128)}, f32[5,16,2,4,16]{2,...) fusion(f32[4,5,28,16,16]{2,4,3,1,0:T(8,128)S(1)} %bitcast.476), kind=kLoop, calls=%fused_computation.14 | loop fusion | bytes 491520 | tf_op jit(solution)/shard_map/transpose | solution.py:266
  194.3 4.3 %copy.225 = f32[5,16,16,4,16]{4,3,2,1,0:T(4,128)} copy(f32[5,16,16,4,16]{1,4,2,0,3:T(8,128)} %slice_bitcast_fusion.6) | data formatting | bytes 655360 | tf_op jit(solution)/shard_map/transpose | solution.py:276
  198.7 3.6 %copy.237 = f32[5,16,16,4,2]{1,4,2,0,3:T(2,128)S(1)} copy(f32[5,16,16,4,2]{4,2,1,0,3:T(8,128)} %get-tuple-element.95) | data formatting | bytes 81920 | tf_op jit(solution)/shard_map/transpose | solution.py:272
  202.2 3.4 %copy.236 = f32[5,16,16,4,2]{1,4,2,0,3:T(2,128)S(1)} copy(f32[5,16,16,4,2]{4,2,1,0,3:T(8,128)} %get-tuple-element.96) | data formatting | bytes 81920 | tf_op jit(solution)/shard_map/transpose | solution.py:272
  206.5 1.9 copy-done.2
  212.0 2.4 fusion.80
  214.7 2.4 copy.267
  217.1 2.4 reshape.330
  221.1 1.7 divide_bitcast_fusion.1
  223.8 2.6 reshape.268
  226.4 3.6 %copy.266 = f32[5,16,2,4,16]{4,3,2,1,0:T(4,128)S(1)} copy(f32[5,16,2,4,16]{2,4,1,0,3:T(8,128)} %get-tuple-element.97) | data formatting | bytes 81920 | tf_op jit(solution)/shard_map/reshape | solution.py:269
  230.3 3.6 %copy.265 = f32[5,16,2,4,16]{4,3,2,1,0:T(4,128)S(1)} copy(f32[5,16,2,4,16]{2,4,1,0,3:T(8,128)} %get-tuple-element.98) | data formatting | bytes 81920 | tf_op jit(solution)/shard_map/reshape | solution.py:269
  235.7 1.4 divide_bitcast_fusion.3
  239.3 4.0 %copy.264 = f32[5,2,16,4,16]{4,3,1,2,0:T(4,128)} copy(f32[5,2,16,4,16]{1,4,2,0,3:T(8,128)} %get-tuple-element.99) | data formatting | bytes 81920 | tf_op jit(solution)/shard_map/reshape | solution.py:266
  243.3 1.8 reshape.327
  245.1 4.0 %copy.263 = f32[5,2,16,4,16]{4,3,1,2,0:T(4,128)} copy(f32[5,2,16,4,16]{1,4,2,0,3:T(8,128)} %get-tuple-element.94) | data formatting | bytes 81920 | tf_op jit(solution)/shard_map/reshape | solution.py:266
  249.1 1.8 reshape.326
  254.8 1.5 divide_bitcast_fusion.5
  260.2 2.6 reshape.273
  262.8 4.4 %copy.249 = f32[5,16,16,4,16]{1,3,4,2,0:T(4,128)} copy(f32[5,16,16,4,16]{4,3,1,2,0:T(4,128)} %reshape.273) | data formatting | bytes 655360 | tf_op jit(solution)/shard_map/reshape | solution.py:213
  267.2 2.9 %reshape.274 = f32[5,16,16,64]{3,2,1,0:T(8,128)S(1)} reshape(f32[5,16,16,4,16]{4,3,2,1,0:T(4,128)} %bitcast.483) | data formatting | bytes 655360 | tf_op jit(solution)/shard_map/reshape | solution.py:216
  278.3 1.8 copy.250
  280.0 2.6 reshape.276
  282.8 6.6 %while.10 = (s32[]{:T(128)}, f32[4,16,256]{2,1,0:T(8,128)S(1)}, s32[]{:T(128)}, s32[4,1,1]{0,2,1:T(1,128)S(1)}, f32[4,1,1]{0,2,1:T(1,128)S(1)}, /*index=5*/f32[4,16,256]{2,1,0:T(8,128)S(1)}, s32[]{:T(128)}) while((s32[]{:T(128)}, f32[4,16,256]{2,1,0:T(8,128)S(1)}, s32[]{:T(128)}, s32[4,1,1]{0,2,1:T(1,128)S(1)}, f32[4,1,1]{0,2,1:T(1,128)S(1)}, ...), condition=%wide.region_19.20_spmd, body=%wide.region_18.19_spmd.sunk | while | flops 163846 | bytes 196737 | solution.py:309
  (289 shorter events, 64.2 us)
Async XLA Ops:
  0.0 6.2 %copy-start = (f32[5,16,16,64]{3,2,1,0:T(8,128)S(1)}, f32[5,16,16,64]{3,2,1,0:T(8,128)}, u32[]{:S(2)}) copy-start(f32[5,16,16,64]{3,2,1,0:T(8,128)} %param.5) | copy-start | bytes 983044
  1.7 27.9 %collective-permute-start = (f32[5,2,16,64]{3,2,1,0:T(8,128)}, f32[5,2,16,64]{3,2,1,0:T(8,128)}, u32[]{:S(2)}, u32[]{:S(2)}) collective-permute-start(f32[5,2,16,64]{3,2,1,0:T(8,128)} %get-tuple-element.166), channel_id=1, source_target_pairs={{0,32},{32,64},{64,96},{96,128},{128,160},{160,192},{192,224},{224... | collective-permute-start | bytes 122888 | tf_op jit(solution)/shard_map/ppermute | solution.py:31
  1.7 5.9 %copy-start.63 = (s32[8,32,3]{1,0,2:T(8,128)S(1)}, s32[8,32,3]{1,0,2:T(8,128)}, u32[]{:S(2)}) copy-start(s32[8,32,3]{1,0,2:T(8,128)} %param.7) | copy-start | bytes 9220
  1.7 28.9 %collective-permute-start.1 = (f32[5,2,16,64]{3,2,1,0:T(8,128)}, f32[5,2,16,64]{3,2,1,0:T(8,128)}, u32[]{:S(2)}, u32[]{:S(2)}) collective-permute-start(f32[5,2,16,64]{3,2,1,0:T(8,128)} %get-tuple-element.165), channel_id=1, source_target_pairs={{32,0},{64,32},{96,64},{128,96},{160,128},{192,160},{224,192},{0,2... | collective-permute-start | bytes 122888 | tf_op jit(solution)/shard_map/ppermute | solution.py:32
  19.9 6.0 %copy-start.64 = (s32[32,8]{1,0:T(8,128)S(1)}, s32[32,8]{1,0:T(8,128)}, u32[]{:S(2)}) copy-start(s32[32,8]{1,0:T(8,128)} %gather_fusion) | copy-start | bytes 3076
  19.9 6.1 %copy-start.65 = (s32[8,32,4]{1,2,0:T(4,128)S(1)}, s32[8,32,4]{1,2,0:T(4,128)}, u32[]{:S(2)}) copy-start(s32[8,32,4]{1,2,0:T(4,128)} %param.6) | copy-start | bytes 12292
  31.5 108.8 %collective-permute-start.2 = (f32[5,20,2,64]{3,2,1,0:T(2,128)S(1)}, f32[5,20,2,64]{3,2,1,0:T(2,128)}, u32[]{:S(2)}, u32[]{:S(2)}) collective-permute-start(f32[5,20,2,64]{3,2,1,0:T(2,128)S(1)} %get-tuple-element.160), channel_id=1, source_target_pairs={{0,1},{1,2},{2,3},{3,4},{4,5},{5,6},{6,7},{7,8},{8,9},{9,10},{10,1... | collective-permute-start | bytes 153608 | tf_op jit(solution)/shard_map/ppermute | solution.py:31
  33.1 111.5 %collective-permute-start.3 = (f32[5,20,2,64]{3,2,1,0:T(2,128)S(1)}, f32[5,20,2,64]{3,2,1,0:T(2,128)}, u32[]{:S(2)}, u32[]{:S(2)}) collective-permute-start(f32[5,20,2,64]{3,2,1,0:T(2,128)S(1)} %get-tuple-element.159), channel_id=1, source_target_pairs={{1,0},{2,1},{3,2},{4,3},{5,4},{6,5},{7,6},{8,7},{9,8},{10,9},{11,1... | collective-permute-start | bytes 153608 | tf_op jit(solution)/shard_map/ppermute | solution.py:32
  35.9 141.6 %copy-start.71 = (s32[4]{0:T(128)}, s32[4]{0:T(128)S(1)}, u32[]{:S(2)}) copy-start(s32[4]{0:T(128)S(1)} %select_reduce_fusion) | copy-start | bytes 52
  123.7 1.8 copy-start.13
  159.9 6.1 %collective-permute-start.4 = (f32[5,28,256]{2,1,0:T(8,128)S(1)}, f32[5,28,256]{2,1,0:T(8,128)}, u32[]{:S(2)}, u32[]{:S(2)}) collective-permute-start(f32[5,28,256]{2,1,0:T(8,128)S(1)} %bitcast.498), channel_id=1, source_target_pairs={{0,1},{1,0},{2,3},{3,2},{4,5},{5,4},{6,7},{7,6},{8,9},{9,8},{10,11... | collective-permute-start | bytes 430088 | tf_op jit(solution)/shard_map/ppermute | solution.py:21
  167.6 7.0 %collective-permute-start.5 = (f32[5,28,256]{2,1,0:T(8,128)S(1)}, f32[5,28,256]{2,1,0:T(8,128)}, u32[]{:S(2)}, u32[]{:S(2)}) collective-permute-start(f32[5,28,256]{2,1,0:T(8,128)S(1)} %bitcast.496), channel_id=1, source_target_pairs={{0,2},{2,0},{1,3},{3,1},{4,6},{6,4},{5,7},{7,5},{8,10},{10,8},{9,1... | collective-permute-start | bytes 430088 | tf_op jit(solution)/shard_map/ppermute | solution.py:21
  176.1 5.7 %collective-permute-start.6 = (f32[5,28,256]{2,1,0:T(8,128)S(1)}, f32[5,28,256]{2,1,0:T(8,128)}, u32[]{:S(2)}, u32[]{:S(2)}) collective-permute-start(f32[5,28,256]{2,1,0:T(8,128)S(1)} %bitcast.497), channel_id=1, source_target_pairs={{0,4},{4,0},{1,5},{5,1},{2,6},{6,2},{3,7},{7,3},{8,12},{12,8},{9,1... | collective-permute-start | bytes 430088 | tf_op jit(solution)/shard_map/ppermute | solution.py:21
  198.7 7.0 %copy-start.1 = (f32[5,16,16,4,16]{1,4,2,0,3:T(8,128)S(1)}, f32[5,16,16,4,16]{1,4,2,0,3:T(8,128)}, u32[]{:S(2)}) copy-start(f32[5,16,16,4,16]{1,4,2,0,3:T(8,128)} %slice_bitcast_fusion.6) | copy-start | bytes 983044
  206.5 1.9 copy-start.2
  214.7 4.9 %copy-start.52 = (f32[20,16,64]{2,1,0:T(8,128)S(1)}, f32[20,16,64]{2,1,0:T(8,128)}, u32[]{:S(2)}) copy-start(f32[20,16,64]{2,1,0:T(8,128)} %div.298) | copy-start | bytes 245764
  217.1 2.6 copy-start.53
  221.0 1.7 copy-start.3
  226.4 7.7 %copy-start.9 = (f32[5,16,16,64]{3,2,1,0:T(8,128)}, f32[5,16,16,64]{3,2,1,0:T(8,128)S(1)}, u32[]{:S(2)}) copy-start(f32[5,16,16,64]{3,2,1,0:T(8,128)S(1)} %reshape.268) | copy-start | bytes 983044
  235.7 2.5 copy-start.10
  250.9 2.5 copy-start.12
  250.9 2.5 copy-start.17
  250.9 2.5 copy-start.18
  254.7 2.7 copy-start.5
  254.8 2.7 copy-start.7
  254.8 2.5 copy-start.48
  256.2 1.4 copy-start.46
  256.3 1.6 copy-start.14
  256.3 1.6 copy-start.44
  257.7 1.4 copy-start.34
  257.7 1.4 copy-start.57
  257.7 1.3 copy-start.58
  257.7 1.3 copy-start.59
  267.2 3.0 %copy-start.47 = (f32[17,16,64]{2,0,1:T(8,128)S(1)}, f32[17,16,64]{2,0,1:T(8,128)}, u32[]{:S(2)}) copy-start(f32[17,16,64]{2,0,1:T(8,128)} %get-tuple-element.133) | copy-start | bytes 208900
  267.2 3.1 %copy-start.45 = (f32[17,16,64]{2,0,1:T(8,128)S(1)}, f32[17,16,64]{2,0,1:T(8,128)}, u32[]{:S(2)}) copy-start(f32[17,16,64]{2,0,1:T(8,128)} %get-tuple-element.139) | copy-start | bytes 208900
  270.3 1.4 copy-start.8
  270.3 1.4 copy-start.50
  270.5 1.5 copy-start.15
  270.5 1.5 copy-start.16
  270.5 1.5 copy-start.49
  271.8 1.3 copy-start.42
  274.3 1.3 copy-start.25
  274.3 1.4 copy-start.26
  274.3 1.4 copy-start.54
  274.3 1.4 copy-start.55
  274.3 1.4 copy-start.56
  274.3 1.4 copy-start.66
  280.0 2.7 copy-start.72
  (32 other events, 38.1 us)
where the time goes:
time: 296 us; the launch traced here: 290 us
  local copies, waits for them, and re-layouts  139 us (47%)
  blocking collectives  77.3 us (26%)
  other arithmetic  38 us (13%)
  waiting for transfers between devices  12 us (4%)
  starting transfers between devices  9.73 us (3%)
  between operations  8.6 us (3%)
  loops' own time  5.87 us (2%)
    pmax x1, blocking collectives, on_device(): time_step = COURANT_FACTOR / lax.pmax(local_top, ('bx', 'by'))  77.3 us
    ppermute x3, waiting for transfers between devices, partner_2(): return lax.ppermute(block, axis, route)  11.9 us
    reshape x4, local copies, waits for them, and re-layouts, back_first(): slab.transpose(1, 2, 3, 0, 4)  11.6 us
    unnamed x152, local copies, waits for them, and re-layouts  11.2 us
    concatenate x1, local copies, waits for them, and re-layouts, pack_travel(): jnp.concatenate([whole, rim_first(first_low), rim_first(first_high), rim_...  10.8 us
    transpose x1, local copies, waits for them, and re-layouts, back_first(): slab.transpose(1, 2, 3, 0, 4)  9.53 us
    reshape x4, local copies, waits for them, and re-layouts, rim_first(): slab.reshape(5, 2, edge_cells, block_count, edge_cells)  8.45 us
    reshape x4, local copies, waits for them, and re-layouts, back_second(): slab.transpose(1, 3, 2, 0, 4)  7.63 us
  transfers between devices with their start and end apart: 7, of which 3 were waited for; matrix products, arithmetic and copies ran while one was open for 19% of the time, Pallas kernels for 0%

commit v1 on v0

v1 whole, which is shorter than its diff:
```python
import jax
import jax.numpy as jnp
from jax import lax
from jax.experimental import pallas as pl
from jax.experimental.pallas import tpu as pltpu
from jax.sharding import PartitionSpec as P

HEAT_RATIO = 5.0 / 3.0
COURANT_FACTOR = 0.4
EMISSION_RATE = 100.0
F32 = jnp.float32
TILE = (8, 128)
VMEM = pl.BlockSpec(memory_space=pltpu.VMEM)
SMEM = pl.BlockSpec(memory_space=pltpu.SMEM)


def shape(*dims):
    return jax.ShapeDtypeStruct(dims, F32)


def iota(axis):
    return lax.broadcasted_iota(jnp.int32, TILE, axis)


def half_minmod(a, b):
    return 0.5 * (jnp.maximum(jnp.minimum(a, b), 0.0) + jnp.minimum(jnp.maximum(a, b), 0.0))


def primitive(u):
    inverse = 1.0 / u[0]
    v1, v2, v3 = u[1] * inverse, u[2] * inverse, u[3] * inverse
    p = (HEAT_RATIO - 1.0) * (u[4] - 0.5 * u[0] * (v1 * v1 + v2 * v2 + v3 * v3))
    return [u[0], v1, v2, v3, p], inverse


def hllc(left, right, n):
    rl, ul, pl_ = left[0], left[n], left[4]
    rr, ur, pr = right[0], right[n], right[4]
    cl = jnp.sqrt(HEAT_RATIO * pl_ / rl)
    cr = jnp.sqrt(HEAT_RATIO * pr / rr)
    sl = jnp.minimum(ul - cl, ur - cr)
    sr = jnp.maximum(ul + cl, ur + cr)
    ml = rl * (sl - ul)
    mr = rr * (sr - ur)
    mid = (pr - pl_ + ml * ul - mr * ur) / (ml - mr)
    use_left = (sl >= 0.0) | (mid >= 0.0)
    rho, v1, v2, v3, p = [jnp.where(use_left, a, b) for a, b in zip(left, right)]
    edge = jnp.where(use_left, sl, sr)
    clip = jnp.where(use_left, jnp.minimum(sl, 0.0), jnp.maximum(sr, 0.0))
    v = [None, v1, v2, v3]
    u = v[n]
    energy = p * (1.0 / (HEAT_RATIO - 1.0)) + 0.5 * rho * (v1 * v1 + v2 * v2 + v3 * v3)
    gap = 1.0 / jnp.where(clip == 0.0, 1.0, edge - mid)
    ratio = (edge - u) * gap
    star_rho = rho * ratio
    star_energy = ratio * energy + (mid - u) * (star_rho * mid + p * gap)
    mass = rho * u
    f_rho = mass + clip * (star_rho - rho)
    out = [f_rho, f_rho * v1, f_rho * v2, f_rho * v3, None]
    out[n] = mass * u + p + clip * (star_rho * mid - mass)
    out[4] = (energy + p) * u + clip * (star_energy - energy)
    return out


def prep_kernel(cons, u_out, w_out, e_bx, o_bx, e_by, o_by):
    even_i = lax.axis_index("bx") % 2 == 0
    even_j = lax.axis_index("by") % 2 == 0
    lane = iota(1)
    bit0 = (lane // 16) % 2 == 0
    bit1 = (lane // 32) % 2 == 0
    row = iota(0)
    top = jnp.zeros(TILE, F32)
    for at in range(2):
        edge_pairs = {}
        for h in range(2):
            tiles = []
            for f in range(5):
                x = [cons[f, pl.ds(at * 128 + h * 8 + b, 8, stride=16), :] for b in range(8)]
                if h == 0:
                    edge_pairs.setdefault(0, []).append(jnp.concatenate([x[0], x[1]], axis=1))
                else:
                    edge_pairs.setdefault(1, []).append(jnp.concatenate([x[6], x[7]], axis=1))
                y = [jnp.concatenate([x[k], x[k + 4]], axis=1) for k in range(4)]
                z = [None] * 4
                for k in range(2):
                    z[k] = jnp.where(bit1, y[k], pltpu.roll(y[k + 2], 32, 1))
                    z[k + 2] = jnp.where(bit1, pltpu.roll(y[k], 96, 1), y[k + 2])
                t = [None] * 4
                for k in (0, 2):
                    t[k] = jnp.where(bit0, z[k], pltpu.roll(z[k + 1], 16, 1))
                    t[k + 1] = jnp.where(bit0, pltpu.roll(z[k], 112, 1), z[k + 1])
                tiles.append(t)
                for s in range(4):
                    u_out[s, f, at, h] = t[s]
            for s in range(4):
                w, inverse = primitive([tiles[f][s] for f in range(5)])
                speed = (
                    jnp.abs(w[1])
                    + jnp.abs(w[2])
                    + jnp.abs(w[3])
                    + 3.0 * jnp.sqrt(HEAT_RATIO * w[4] * inverse)
                )
                top = jnp.maximum(top, speed)
                for f in range(5):
                    w_out[s, f, at, h] = w[f]
        low, _ = primitive(edge_pairs[0])
        high, _ = primitive(edge_pairs[1])
        for f in range(5):
            e_by[f * 2 + at] = jnp.where(even_j, high[f], low[f])
            o_by[f * 2 + at] = jnp.where(even_j, low[f], high[f])
    for f in range(5):
        for h in range(2):
            low = jnp.zeros(TILE, F32)
            high = jnp.zeros(TILE, F32)
            for s in range(4):
                here = row // 2 == s
                low = jnp.where(here, pltpu.roll(w_out[s, f, 0, h], 2 * s, 0), low)
                high = jnp.where(here, pltpu.roll(w_out[s, f, 1, h], (2 * s + 2) % 8, 0), high)
            e_bx[f * 2 + h] = jnp.where(even_i, high, low)
            o_bx[f * 2 + h] = jnp.where(even_i, low, high)
    for ref in (e_bx, o_bx, e_by, o_by):
        ref[10] = top


def flux_kernel(
    slots, w, u, se_bx, so_bx, se_by, so_by, re_bx, ro_bx, re_by, ro_by,
    d, send_a, send_b, send_c, top_out,
    flux_a, high_a, halo_a, flux_b, high_b, halo_b, lefts, rights, fluxes,
):
    i, j = lax.axis_index("bx"), lax.axis_index("by")
    even_i, even_j = i % 2 == 0, j % 2 == 0
    row, lane = iota(0), iota(1)

    top = se_bx[10]
    for ref in (re_bx, ro_bx, re_by, ro_by):
        top = jnp.maximum(top, ref[10])
    top = jnp.max(top, axis=0, keepdims=True)
    top_out[...] = jnp.broadcast_to(top[None], top_out.shape)

    def pick(flag, a, b, index):
        return jnp.where(flag, a[index], b[index])

    def edges(near, far, own0, own1):
        left = [n + half_minmod(n - q, a - n) for n, q, a in zip(near, far, own0)]
        right = [a - half_minmod(a - n, b - a) for n, a, b in zip(near, own0, own1)]
        return left, right

    for h in range(2):
        tiles = range(h, 10, 2)
        own_low = [pick(even_i, so_bx, se_bx, t) for t in tiles]
        own_high = [pick(even_i, se_bx, so_bx, t) for t in tiles]
        low = [pick(even_i, ro_bx, re_bx, t) for t in tiles]
        high = [pick(even_i, re_bx, ro_bx, t) for t in tiles]
        back = lambda a: pltpu.roll(a, 1, 0)
        left, right = edges(low, [back(a) for a in low], [back(a) for a in own_low], own_low)
        f_low = hllc(left, right, 1)
        for f in range(5):
            n, q, a = high[f], pltpu.roll(high[f], 7, 0), pltpu.roll(own_high[f], 7, 0)
            flux_a[f, h] = f_low[f]
            high_a[f, h] = n - half_minmod(n - a, q - n)
            halo_a[0, f, h] = low[f]
            halo_a[1, f, h] = n
    for at in range(2):
        tiles = range(at, 10, 2)
        own_low = [pick(even_j, so_by, se_by, t) for t in tiles]
        own_high = [pick(even_j, se_by, so_by, t) for t in tiles]
        low = [pick(even_j, ro_by, re_by, t) for t in tiles]
        high = [pick(even_j, re_by, ro_by, t) for t in tiles]
        swap = lambda a: pltpu.roll(a, 64, 1)
        near = [swap(a) for a in low]
        left, right = edges(near, low, own_low, [swap(a) for a in own_low])
        f_low = hllc(left, right, 2)
        for f in range(5):
            n, q, a = high[f], swap(high[f]), swap(own_high[f])
            flux_b[f, at] = f_low[f]
            high_b[f, at] = n - half_minmod(n - a, q - n)
            halo_b[0, f, at] = near[f]
            halo_b[1, f, at] = n

    def sweep(n, load, low_fill, high_fill, high_state, low_flux, down, up, first, last):
        left, right = [[], []], [[], []]
        for f in range(5):
            a, b = load(f)
            da, db, ua, ub = down(a), down(b), up(a), up(b)
            a_prev = jnp.where(first, low_fill(f), da)
            b_prev = jnp.where(first, da, db)
            a_next = jnp.where(last, ub, ua)
            b_next = jnp.where(last, high_fill(f), ub)
            ha = half_minmod(a - a_prev, a_next - a)
            hb = half_minmod(b - b_prev, b_next - b)
            ra, rb = up(a - ha), up(b - hb)
            left[0].append(a + ha)
            left[1].append(b + hb)
            right[0].append(jnp.where(last, rb, ra))
            right[1].append(jnp.where(last, high_state(f), rb))
        fa = hllc(left[0], right[0], n)
        fb = hllc(left[1], right[1], n)
        out = []
        for f in range(5):
            da, db = down(fa[f]), down(fb[f])
            out.append(
                (
                    fa[f] - jnp.where(first, low_flux(f), da),
                    fb[f] - jnp.where(first, da, db),
                )
            )
        return out

    def along_first(k, _):
        s, h = k // 2, k % 2
        line = lambda ref, *index: jnp.broadcast_to(ref[index], TILE)
        out = sweep(
            1,
            lambda f: (w[s, f, 0, h], w[s, f, 1, h]),
            lambda f: line(halo_a, 0, f, h, pl.ds(2 * s + 1, 1)),
            lambda f: line(halo_a, 1, f, h, pl.ds(2 * s, 1)),
            lambda f: line(high_a, f, h, pl.ds(2 * s, 1)),
            lambda f: line(flux_a, f, h, pl.ds(2 * s + 1, 1)),
            lambda a: pltpu.roll(a, 1, 0),
            lambda a: pltpu.roll(a, 7, 0),
            row == 0,
            row == 7,
        )
        for f in range(5):
            d[s, f, 0, h], d[s, f, 1, h] = out[f]
        return 0

    def along_second(k, _):
        s, at = k // 2, k % 2
        to_low = (128 - 16 * s) % 128
        to_high = 112 - 16 * s
        out = sweep(
            2,
            lambda f: (w[s, f, at, 0], w[s, f, at, 1]),
            lambda f: pltpu.roll(halo_b[0, f, at], to_low, 1),
            lambda f: pltpu.roll(halo_b[1, f, at], to_high, 1),
            lambda f: pltpu.roll(high_b[f, at], to_high, 1),
            lambda f: pltpu.roll(flux_b[f, at], to_low, 1),
            lambda a: pltpu.roll(a, 16, 1),
            lambda a: pltpu.roll(a, 112, 1),
            lane < 16,
            lane >= 112,
        )
        for f in range(5):
            d[s, f, at, 0] += out[f][0]
            d[s, f, at, 1] += out[f][1]
        return 0

    first_c, last_c = lane % 16 == 0, lane % 16 == 15

    def previous(here, before):
        return jnp.where(first_c, pltpu.roll(before, 113, 1), pltpu.roll(here, 1, 1))

    def following(here, after):
        return jnp.where(last_c, pltpu.roll(after, 15, 1), pltpu.roll(here, 127, 1))

    def third_states(k, _):
        s, at = k // 2, k % 2
        before, after = (s + 3) % 4, (s + 1) % 4
        for h in range(2):
            for f in range(5):
                a = w[s, f, at, h]
                slope = half_minmod(
                    a - previous(a, w[before, f, at, h]), following(a, w[after, f, at, h]) - a
                )
                lefts[s, f, at, h] = a + slope
                rights[s, f, at, h] = a - slope
        return 0

    def third_fluxes(k, _):
        s, at = k // 2, k % 2
        after = (s + 1) % 4
        for h in range(2):
            out = hllc(
                [lefts[s, f, at, h] for f in range(5)],
                [following(rights[s, f, at, h], rights[after, f, at, h]) for f in range(5)],
                3,
            )
            for f in range(5):
                fluxes[s, f, at, h] = out[f]
        return 0

    def third_change(k, _):
        s, at = k // 2, k % 2
        before = (s + 3) % 4
        for h in range(2):
            for f in range(5):
                a = fluxes[s, f, at, h]
                d[s, f, at, h] += a - previous(a, fluxes[before, f, at, h])
        return 0

    for body in (along_first, along_second, third_states, third_fluxes, third_change):
        lax.fori_loop(0, 8, body, 0)

    for r, ref in enumerate((send_a, send_b, send_c)):
        slot = slots[i, j, r]
        ref[0] = u[slot]
        ref[1] = d[slot]


def tail_kernel(
    slots, counts, u, d, top, got1, got2, got3, got4, got5, got6, got7, out, energy, factor, tick
):
    i, j = lax.axis_index("bx"), lax.axis_index("by")
    speed = jnp.max(jnp.max(top[...], axis=0), axis=1, keepdims=True)
    step = COURANT_FACTOR / jnp.broadcast_to(speed, TILE)
    sw = lambda m, r: slots[i, j ^ m, r]

    def content(m, slot):
        second = slot == sw(m, 1)
        through = sw(m ^ 2, 1) == sw(m ^ 2, 0)
        first = slot == sw(m, 0)
        mask = jnp.where(second, jnp.where(through, 3, 2), jnp.where(first, 1, 0))
        index = jnp.where(
            second,
            jnp.where(through, sw(m ^ 3, 0), sw(m ^ 2, 1)),
            jnp.where(first, sw(m ^ 1, 0), slot),
        )
        return m ^ mask, index

    most = jnp.int32(0)
    limits = []
    for slot in range(4):
        is_last = sw(0, 2) == slot
        near, near_index = content(0, slot)
        far, far_index = content(4, sw(4, 2))
        mask = jnp.where(is_last, far, near)
        index = jnp.where(is_last, far_index, near_index)
        count = counts[i, j ^ mask, index]
        limits.append(count)
        most = jnp.maximum(most, count)

        def write(u_of, d_of):
            for at in range(2):
                for h in range(2):
                    new = [u_of(f, at, h) - step * d_of(f, at, h) for f in range(5)]
                    rho = new[0]
                    kinetic = 0.5 * (new[1] * new[1] + new[2] * new[2] + new[3] * new[3]) / rho
                    energy[slot, at, h] = new[4] - kinetic
                    factor[slot, at, h] = (HEAT_RATIO - 1.0) / rho
                    tick[slot, at, h] = (step / count.astype(F32)) * rho * EMISSION_RATE
                    new[4] = kinetic
                    for f in range(5):
                        out[slot, f, pl.ds(8 * at, 8), pl.ds(128 * h, 128)] = new[f]

        @pl.when(mask == 0)
        def _():
            write(lambda f, at, h: u[index, f, at, h], lambda f, at, h: d[index, f, at, h])

        for m, ref in enumerate((got1, got2, got3, got4, got5, got6, got7), 1):

            @pl.when(mask == m)
            def _():
                write(lambda f, at, h: ref[0, f, at, h], lambda f, at, h: ref[1, f, at, h])

    def advance(k, _):
        for slot in range(4):
            for at in range(2):
                for h in range(2):
                    now = energy[slot, at, h]
                    heat = now * factor[slot, at, h]
                    new = now / (1.0 + tick[slot, at, h] * jnp.sqrt(1.0 + heat * heat))
                    energy[slot, at, h] = jnp.where(k < limits[slot], new, now)
        return 0

    lax.fori_loop(0, most, advance, 0)
    for slot in range(4):
        for at in range(2):
            for h in range(2):
                place = (slot, 4, pl.ds(8 * at, 8), pl.ds(128 * h, 128))
                out[place] = out[place] + energy[slot, at, h]


def pair_even(count):
    return [(k, k ^ 1) for k in range(count)]


def pair_odd(count):
    return [(k, (k + 1) % count if k % 2 else (k - 1) % count) for k in range(count)]


def on_device(conserved, cool_steps, swap_slot):
    rows, columns = lax.axis_size("bx"), lax.axis_size("by")
    blocks = (4, 5, 2, 2) + TILE
    slab = (11,) + TILE
    u, w, *slabs = pl.pallas_call(
        prep_kernel,
        in_specs=[VMEM],
        out_specs=[VMEM] * 6,
        out_shape=[shape(*blocks)] * 2 + [shape(*slab)] * 4,
    )(conserved.reshape(5, 256, 64))
    e_bx, o_bx, e_by, o_by = slabs
    got_slabs = [
        lax.ppermute(e_bx, "bx", pair_even(rows)),
        lax.ppermute(o_bx, "bx", pair_odd(rows)),
        lax.ppermute(e_by, "by", pair_even(columns)),
        lax.ppermute(o_by, "by", pair_odd(columns)),
    ]
    groups = [
        [i * columns + j for i in range(rows) for j in range(columns) if (i + 2 * j) % 4 == r]
        for r in range(4)
    ]
    size = len(groups[0])
    travel = (2, 5, 2, 2) + TILE
    edge = (5, 2) + TILE
    d, send_a, send_b, send_c, top = pl.pallas_call(
        flux_kernel,
        in_specs=[SMEM] + [VMEM] * 10,
        out_specs=[VMEM] * 5,
        out_shape=[shape(*blocks)] + [shape(*travel)] * 3 + [shape(size, 1, 128)],
        scratch_shapes=[
            pltpu.VMEM(edge, F32),
            pltpu.VMEM(edge, F32),
            pltpu.VMEM((2,) + edge, F32),
            pltpu.VMEM(edge, F32),
            pltpu.VMEM(edge, F32),
            pltpu.VMEM((2,) + edge, F32),
            pltpu.VMEM(blocks, F32),
            pltpu.VMEM(blocks, F32),
            pltpu.VMEM(blocks, F32),
        ],
    )(swap_slot, w, u, *slabs, *got_slabs)
    sends = {1: send_a, 2: send_b, 3: send_a, 4: send_c, 5: send_a, 6: send_b, 7: send_a}
    got = [
        lax.ppermute(sends[m], "by", [(k, k ^ m) for k in range(columns)]) for m in range(1, 8)
    ]
    top = lax.all_to_all(top, ("bx", "by"), 0, 0, axis_index_groups=groups)
    state = (4, 2, 2) + TILE
    result = pl.pallas_call(
        tail_kernel,
        in_specs=[SMEM] * 2 + [VMEM] * 10,
        out_specs=VMEM,
        out_shape=shape(4, 5, 16, 256),
        scratch_shapes=[pltpu.VMEM(state, F32)] * 3,
    )(swap_slot, cool_steps, u, d, top, *got)
    return result.reshape((1, 1) + result.shape)


def solution(mesh):
    in_specs = (P(None, "bx", "by", None), P(), P())
    out_specs = P("bx", "by", None, None, None, None)
    return jax.shard_map(
        on_device, mesh=mesh, in_specs=in_specs, out_specs=out_specs, check_vma=False
    )
```

time: 296 us -> 68.7 us (0.23)
  the two profiles are of different devices: /device:TPU:32 before, /device:TPU:2 now
where the time goes in v1:
time: 68.7 us; the launch traced here: 68.5 us
  starting transfers between devices  34.4 us (50%)
  Pallas kernels  18.4 us (27%)
  waiting for transfers between devices  12.5 us (18%)
  local copies, waits for them, and re-layouts  3.03 us (4%)
    ppermute x7, starting transfers between devices, on_device(): lax.ppermute(sends[m], 'by', [(k, k ^ m) for k in range(columns)])  16.8 us
    all_to_all x1, starting transfers between devices, on_device(): top = lax.all_to_all(top, ('bx', 'by'), 0, 0, axis_index_groups=groups)  11.7 us
    all_to_all x1, waiting for transfers between devices, on_device(): top = lax.all_to_all(top, ('bx', 'by'), 0, 0, axis_index_groups=groups)  11.1 us
    pallas_call x1, Pallas kernels, on_device(): pl.pallas_call(flux_kernel, in_specs=[SMEM] + [VMEM] * 10, out_specs=[VME...  9.59 us
    pallas_call x1, Pallas kernels, on_device(): pl.pallas_call(tail_kernel, in_specs=[SMEM] * 2 + [VMEM] * 10, out_specs=...  6.35 us
    ppermute x1, starting transfers between devices, on_device(): lax.ppermute(o_bx, 'bx', pair_odd(rows))  3.13 us
    unnamed x30, local copies, waits for them, and re-layouts  3.03 us
    pallas_call x1, Pallas kernels, on_device(): pl.pallas_call(prep_kernel, in_specs=[VMEM], out_specs=[VMEM] * 6, out_sh...  2.47 us
  transfers between devices with their start and end apart: 12, of which 3 were waited for; matrix products, arithmetic and copies ran while one was open for 2% of the time, Pallas kernels for 0%

profile of v1, /device:TPU:2, one launch (start us, length us, event | category | flops | bytes accessed | tf_op | source)
XLA Modules:
  0.0 68.5 jit_solution(1557028157422438342)
XLA Ops:
  0.0 2.5 %shard_map.37 = (f32[4,5,2,2,8,128]{5,4,3,2,1,0:T(8,128)}, f32[4,5,2,2,8,128]{5,4,3,2,1,0:T(8,128)}, f32[11,8,128]{2,1,0:T(8,128)}, f32[11,8,128]{2,1,0:T(8,128)...) custom-call(f32[5,256,64]{2,1,0:T(8,128)} %bitcast.2), custom_call_target="tpu_custom_call" | custom-call | tf_op jit(solution)/shard_map/pallas_call | solution.py:386
  2.5 0.0 collective-permute-start
  2.5 3.1 %collective-permute-start.1 = (f32[11,8,128]{2,1,0:T(8,128)}, f32[11,8,128]{2,1,0:T(8,128)S(1)}, u32[]{:S(2)}, u32[]{:S(2)}) collective-permute-start(f32[11,8,128]{2,1,0:T(8,128)} %get-tuple-element.19.so_bx), channel_id=1, source_target_pairs={{0,224},{32,64},{64,32},{96,128},{128,96},{160,192},{192,160},{224... | collective-permute-start | bytes 135176 | tf_op jit(solution)/shard_map/ppermute | solution.py:395
  5.6 0.5 collective-permute-start.2
  6.1 2.2 %collective-permute-start.3 = (f32[11,8,128]{2,1,0:T(8,128)}, f32[11,8,128]{2,1,0:T(8,128)S(1)}, u32[]{:S(2)}, u32[]{:S(2)}) collective-permute-start(f32[11,8,128]{2,1,0:T(8,128)} %get-tuple-element.21.so_by), channel_id=1, source_target_pairs={{0,31},{1,2},{2,1},{3,4},{4,3},{5,6},{6,5},{7,8},{8,7},{9,10},{10,... | collective-permute-start | bytes 135176 | tf_op jit(solution)/shard_map/ppermute | solution.py:397
  8.3 0.0 copy-done.13
  8.3 0.8 %copy.5.slots = s32[8,32,3]{2,1,0:T(8,128)} copy(s32[8,32,3]{1,0,2:T(8,128)S(1)} %copy-done.13) | data formatting | bytes 6144 | tf_op args[2]
  9.1 0.0 collective-permute-done.re_bx
  9.1 0.0 collective-permute-done.1.ro_bx
  9.1 0.0 copy-start.9
  9.1 0.8 %collective-permute-done.2.re_by = f32[11,8,128]{2,1,0:T(8,128)S(1)} collective-permute-done((f32[11,8,128]{2,1,0:T(8,128)}, f32[11,8,128]{2,1,0:T(8,128)S(1)}, u32[]{:S(2)}, u32[]{:S(2)}) %collective-permute-start.2) | collective-permute-done | bytes 45088 | tf_op jit(solution)/shard_map/ppermute | solution.py:396
  9.9 0.7 collective-permute-done.3.ro_by
  10.5 0.0 copy-done.8
  10.5 0.0 copy-done.9
  10.5 0.0 copy-done.10
  10.5 0.6 copy-done.11
  11.2 9.6 %shard_map.38 = (f32[4,5,2,2,8,128]{5,4,3,2,1,0:T(8,128)}, f32[2,5,2,2,8,128]{5,4,3,2,1,0:T(8,128)}, f32[2,5,2,2,8,128]{5,4,3,2,1,0:T(8,128)}, f32[2,5,2,2,8,128]{5,4,3,2,1,0:T(8,128)}, f32[64,1,128]{2,1,0:T(1,128)}) custom-call(s32[8,32,3]{2,1,0:T(8,128)} %copy.5.slots, f32[4,5,2,2,8,128]{5,4,3,2,1,0:T(8,128)} %get-tuple-element.17.w, ...), custom_call_target="tpu_custom_call" | custom-call | tf_op jit(solution)/shard_map/pallas_call | solution.py:406
  20.7 1.9 %collective-permute-start.7 = (f32[2,5,2,2,8,128]{5,4,3,2,1,0:T(8,128)}, f32[2,5,2,2,8,128]{5,4,3,2,1,0:T(8,128)S(1)}, u32[]{:S(2)}, u32[]{:S(2)}) collective-permute-start(f32[2,5,2,2,8,128]{5,4,3,2,1,0:T(8,128)} %get-tuple-element.26), channel_id=1, source_target_pairs={{0,4},{1,5},{2,6},{3,7},{4,0},{5,1},{6,2},{7,3},{8,12},{9,13},{10,... | collective-permute-start | bytes 491528 | tf_op jit(solution)/shard_map/ppermute | solution.py:425
  22.7 3.9 %collective-permute-start.9 = (f32[2,5,2,2,8,128]{5,4,3,2,1,0:T(8,128)}, f32[2,5,2,2,8,128]{5,4,3,2,1,0:T(8,128)S(1)}, u32[]{:S(2)}, u32[]{:S(2)}) collective-permute-start(f32[2,5,2,2,8,128]{5,4,3,2,1,0:T(8,128)} %get-tuple-element.25), channel_id=1, source_target_pairs={{0,6},{1,7},{2,4},{3,5},{4,2},{5,3},{6,0},{7,1},{8,14},{9,15},{10,... | collective-permute-start | bytes 491528 | tf_op jit(solution)/shard_map/ppermute | solution.py:425
  26.6 0.5 collective-permute-start.5
  27.1 3.3 %collective-permute-start.10 = (f32[2,5,2,2,8,128]{5,4,3,2,1,0:T(8,128)}, f32[2,5,2,2,8,128]{5,4,3,2,1,0:T(8,128)S(1)}, u32[]{:S(2)}, u32[]{:S(2)}) collective-permute-start(f32[2,5,2,2,8,128]{5,4,3,2,1,0:T(8,128)} %get-tuple-element.24), channel_id=1, source_target_pairs={{0,7},{1,6},{2,5},{3,4},{4,3},{5,2},{6,1},{7,0},{8,15},{9,14},{10,... | collective-permute-start | bytes 491528 | tf_op jit(solution)/shard_map/ppermute | solution.py:425
  30.4 1.8 %collective-permute-start.8 = (f32[2,5,2,2,8,128]{5,4,3,2,1,0:T(8,128)}, f32[2,5,2,2,8,128]{5,4,3,2,1,0:T(8,128)S(1)}, u32[]{:S(2)}, u32[]{:S(2)}) collective-permute-start(f32[2,5,2,2,8,128]{5,4,3,2,1,0:T(8,128)} %get-tuple-element.24), channel_id=1, source_target_pairs={{0,5},{1,4},{2,7},{3,6},{4,1},{5,0},{6,3},{7,2},{8,13},{9,12},{10,... | collective-permute-start | bytes 491528 | tf_op jit(solution)/shard_map/ppermute | solution.py:425
  32.2 0.0 collective-permute-done.7.got4
  32.2 3.8 %collective-permute-start.6 = (f32[2,5,2,2,8,128]{5,4,3,2,1,0:T(8,128)}, f32[2,5,2,2,8,128]{5,4,3,2,1,0:T(8,128)S(1)}, u32[]{:S(2)}, u32[]{:S(2)}) collective-permute-start(f32[2,5,2,2,8,128]{5,4,3,2,1,0:T(8,128)} %get-tuple-element.24), channel_id=1, source_target_pairs={{0,3},{1,2},{2,1},{3,0},{4,7},{5,6},{6,5},{7,4},{8,11},{9,10},{10,... | collective-permute-start | bytes 491528 | tf_op jit(solution)/shard_map/ppermute | solution.py:425
  36.0 0.0 collective-permute-done.9.got6
  36.0 1.6 %collective-permute-start.4 = (f32[2,5,2,2,8,128]{5,4,3,2,1,0:T(8,128)}, f32[2,5,2,2,8,128]{5,4,3,2,1,0:T(8,128)S(1)}, u32[]{:S(2)}, u32[]{:S(2)}) collective-permute-start(f32[2,5,2,2,8,128]{5,4,3,2,1,0:T(8,128)} %get-tuple-element.24), channel_id=1, source_target_pairs={{0,1},{1,0},{2,3},{3,2},{4,5},{5,4},{6,7},{7,6},{8,9},{9,8},{10,11... | collective-permute-start | bytes 491528 | tf_op jit(solution)/shard_map/ppermute | solution.py:425
  37.6 11.7 %all-to-all-start = ((f32[64,1,128]{2,1,0:T(1,128)}), f32[64,1,128]{2,1,0:T(1,128)S(1)}, u32[]{:S(2)}, u32[]{:S(2)}) async-start(f32[64,1,128]{2,1,0:T(1,128)} %get-tuple-element.23), calls=%async_computation | async-start | bytes 65536 | tf_op jit(solution)/shard_map/all_to_all | solution.py:427
  49.3 0.0 copy-done.12
  49.3 0.8 %copy.6.counts = s32[8,32,4]{2,1,0:T(8,128)} copy(s32[8,32,4]{1,2,0:T(4,128)S(1)} %copy-done.12) | data formatting | bytes 8192 | tf_op args[1]
  50.1 11.1 %all-to-all-done.top = f32[64,1,128]{2,1,0:T(1,128)S(1)} async-done(((f32[64,1,128]{2,1,0:T(1,128)}), f32[64,1,128]{2,1,0:T(1,128)S(1)}, u32[]{:S(2)}, u32[]{:S(2)}) %all-to-all-start) | async-done | bytes 32800 | tf_op jit(solution)/shard_map/all_to_all | solution.py:427
  61.2 0.0 collective-permute-done.5.got2
  61.2 0.0 collective-permute-done.10.got7
  61.2 0.0 copy-start.3
  61.2 0.0 collective-permute-done.8.got5
  61.2 0.0 copy-start.4
  61.2 0.0 collective-permute-done.6.got3
  61.2 0.0 copy-start.5
  61.2 0.0 collective-permute-done.4.got1
  61.2 0.0 copy-start.6
  61.3 0.0 copy-done
  61.3 0.0 copy-done.1
  61.3 0.5 copy-done.7
  61.8 0.1 copy-done.2
  61.9 0.1 copy-done.3
  61.9 0.1 copy-done.4
  62.0 0.1 copy-done.5
  62.0 0.1 copy-done.6
  62.1 6.4 %shard_map.39 = f32[4,5,16,256]{3,2,1,0:T(8,128)} custom-call(s32[8,32,3]{2,1,0:T(8,128)} %copy.5.slots, s32[8,32,4]{2,1,0:T(8,128)} %copy.6.counts, f32[4,5,2,2,8,128]{5,4,3,2,1,0:T(8,128)} %get-tuple-element.16.u, f32[4,5,2,2,8,128]{5,4,3,2,1,0:T(8,128)} %get-tuple-element.22.d, f32[64,1,128]{2,1,0:T(1,128)} %copy-done.7, ...), custom_call_target="tpu_custom_call" | custom-call | tf_op jit(solution)/shard_map/pallas_call | solution.py:429
  (9 shorter events, 0.0 us)
Async XLA Ops:
  0.0 8.3 %copy-start.13 = (s32[8,32,3]{1,0,2:T(8,128)S(1)}, s32[8,32,3]{1,0,2:T(8,128)}, u32[]{:S(2)}) copy-start(s32[8,32,3]{1,0,2:T(8,128)} %param.5) | copy-start | bytes 9220
  2.5 6.6 %collective-permute-start = (f32[11,8,128]{2,1,0:T(8,128)}, f32[11,8,128]{2,1,0:T(8,128)S(1)}, u32[]{:S(2)}, u32[]{:S(2)}) collective-permute-start(f32[11,8,128]{2,1,0:T(8,128)} %get-tuple-element.18.se_bx), channel_id=1, source_target_pairs={{0,32},{32,0},{64,96},{96,64},{128,160},{160,128},{192,224},{224,1... | collective-permute-start | bytes 135176 | tf_op jit(solution)/shard_map/ppermute | solution.py:394
  2.5 6.6 %collective-permute-start.1 = (f32[11,8,128]{2,1,0:T(8,128)}, f32[11,8,128]{2,1,0:T(8,128)S(1)}, u32[]{:S(2)}, u32[]{:S(2)}) collective-permute-start(f32[11,8,128]{2,1,0:T(8,128)} %get-tuple-element.19.so_bx), channel_id=1, source_target_pairs={{0,224},{32,64},{64,32},{96,128},{128,96},{160,192},{192,160},{224... | collective-permute-start | bytes 135176 | tf_op jit(solution)/shard_map/ppermute | solution.py:395
  5.6 4.3 %collective-permute-start.2 = (f32[11,8,128]{2,1,0:T(8,128)}, f32[11,8,128]{2,1,0:T(8,128)S(1)}, u32[]{:S(2)}, u32[]{:S(2)}) collective-permute-start(f32[11,8,128]{2,1,0:T(8,128)} %get-tuple-element.20.se_by), channel_id=1, source_target_pairs={{0,1},{1,0},{2,3},{3,2},{4,5},{5,4},{6,7},{7,6},{8,9},{9,8},{10,11... | collective-permute-start | bytes 135176 | tf_op jit(solution)/shard_map/ppermute | solution.py:396
  6.1 4.4 %collective-permute-start.3 = (f32[11,8,128]{2,1,0:T(8,128)}, f32[11,8,128]{2,1,0:T(8,128)S(1)}, u32[]{:S(2)}, u32[]{:S(2)}) collective-permute-start(f32[11,8,128]{2,1,0:T(8,128)} %get-tuple-element.21.so_by), channel_id=1, source_target_pairs={{0,31},{1,2},{2,1},{3,4},{4,3},{5,6},{6,5},{7,8},{8,7},{9,10},{10,... | collective-permute-start | bytes 135176 | tf_op jit(solution)/shard_map/ppermute | solution.py:397
  9.1 1.5 %copy-start.8 = (f32[11,8,128]{2,1,0:T(8,128)}, f32[11,8,128]{2,1,0:T(8,128)S(1)}, u32[]{:S(2)}) copy-start(f32[11,8,128]{2,1,0:T(8,128)S(1)} %collective-permute-done.re_bx) | copy-start | bytes 135172
  9.1 1.4 %copy-start.9 = (f32[11,8,128]{2,1,0:T(8,128)}, f32[11,8,128]{2,1,0:T(8,128)S(1)}, u32[]{:S(2)}) copy-start(f32[11,8,128]{2,1,0:T(8,128)S(1)} %collective-permute-done.1.ro_bx) | copy-start | bytes 135172
  9.9 0.7 copy-start.10
  10.5 0.6 copy-start.11
  20.7 11.5 %collective-permute-start.7 = (f32[2,5,2,2,8,128]{5,4,3,2,1,0:T(8,128)}, f32[2,5,2,2,8,128]{5,4,3,2,1,0:T(8,128)S(1)}, u32[]{:S(2)}, u32[]{:S(2)}) collective-permute-start(f32[2,5,2,2,8,128]{5,4,3,2,1,0:T(8,128)} %get-tuple-element.26), channel_id=1, source_target_pairs={{0,4},{1,5},{2,6},{3,7},{4,0},{5,1},{6,2},{7,3},{8,12},{9,13},{10,... | collective-permute-start | bytes 491528 | tf_op jit(solution)/shard_map/ppermute | solution.py:425
  22.7 13.3 %collective-permute-start.9 = (f32[2,5,2,2,8,128]{5,4,3,2,1,0:T(8,128)}, f32[2,5,2,2,8,128]{5,4,3,2,1,0:T(8,128)S(1)}, u32[]{:S(2)}, u32[]{:S(2)}) collective-permute-start(f32[2,5,2,2,8,128]{5,4,3,2,1,0:T(8,128)} %get-tuple-element.25), channel_id=1, source_target_pairs={{0,6},{1,7},{2,4},{3,5},{4,2},{5,3},{6,0},{7,1},{8,14},{9,15},{10,... | collective-permute-start | bytes 491528 | tf_op jit(solution)/shard_map/ppermute | solution.py:425
  26.6 34.6 %collective-permute-start.5 = (f32[2,5,2,2,8,128]{5,4,3,2,1,0:T(8,128)}, f32[2,5,2,2,8,128]{5,4,3,2,1,0:T(8,128)S(1)}, u32[]{:S(2)}, u32[]{:S(2)}) collective-permute-start(f32[2,5,2,2,8,128]{5,4,3,2,1,0:T(8,128)} %get-tuple-element.25), channel_id=1, source_target_pairs={{0,2},{1,3},{2,0},{3,1},{4,6},{5,7},{6,4},{7,5},{8,10},{9,11},{10,... | collective-permute-start | bytes 491528 | tf_op jit(solution)/shard_map/ppermute | solution.py:425
  27.1 34.1 %collective-permute-start.10 = (f32[2,5,2,2,8,128]{5,4,3,2,1,0:T(8,128)}, f32[2,5,2,2,8,128]{5,4,3,2,1,0:T(8,128)S(1)}, u32[]{:S(2)}, u32[]{:S(2)}) collective-permute-start(f32[2,5,2,2,8,128]{5,4,3,2,1,0:T(8,128)} %get-tuple-element.24), channel_id=1, source_target_pairs={{0,7},{1,6},{2,5},{3,4},{4,3},{5,2},{6,1},{7,0},{8,15},{9,14},{10,... | collective-permute-start | bytes 491528 | tf_op jit(solution)/shard_map/ppermute | solution.py:425
  30.4 30.8 %collective-permute-start.8 = (f32[2,5,2,2,8,128]{5,4,3,2,1,0:T(8,128)}, f32[2,5,2,2,8,128]{5,4,3,2,1,0:T(8,128)S(1)}, u32[]{:S(2)}, u32[]{:S(2)}) collective-permute-start(f32[2,5,2,2,8,128]{5,4,3,2,1,0:T(8,128)} %get-tuple-element.24), channel_id=1, source_target_pairs={{0,5},{1,4},{2,7},{3,6},{4,1},{5,0},{6,3},{7,2},{8,13},{9,12},{10,... | collective-permute-start | bytes 491528 | tf_op jit(solution)/shard_map/ppermute | solution.py:425
  32.2 29.1 %copy-start = (f32[2,5,2,2,8,128]{5,4,3,2,1,0:T(8,128)}, f32[2,5,2,2,8,128]{5,4,3,2,1,0:T(8,128)S(1)}, u32[]{:S(2)}) copy-start(f32[2,5,2,2,8,128]{5,4,3,2,1,0:T(8,128)S(1)} %collective-permute-done.7.got4) | copy-start | bytes 491524
  32.2 29.0 %collective-permute-start.6 = (f32[2,5,2,2,8,128]{5,4,3,2,1,0:T(8,128)}, f32[2,5,2,2,8,128]{5,4,3,2,1,0:T(8,128)S(1)}, u32[]{:S(2)}, u32[]{:S(2)}) collective-permute-start(f32[2,5,2,2,8,128]{5,4,3,2,1,0:T(8,128)} %get-tuple-element.24), channel_id=1, source_target_pairs={{0,3},{1,2},{2,1},{3,0},{4,7},{5,6},{6,5},{7,4},{8,11},{9,10},{10,... | collective-permute-start | bytes 491528 | tf_op jit(solution)/shard_map/ppermute | solution.py:425
  36.0 25.3 %copy-start.1 = (f32[2,5,2,2,8,128]{5,4,3,2,1,0:T(8,128)}, f32[2,5,2,2,8,128]{5,4,3,2,1,0:T(8,128)S(1)}, u32[]{:S(2)}) copy-start(f32[2,5,2,2,8,128]{5,4,3,2,1,0:T(8,128)S(1)} %collective-permute-done.9.got6) | copy-start | bytes 491524
  36.0 25.2 %collective-permute-start.4 = (f32[2,5,2,2,8,128]{5,4,3,2,1,0:T(8,128)}, f32[2,5,2,2,8,128]{5,4,3,2,1,0:T(8,128)S(1)}, u32[]{:S(2)}, u32[]{:S(2)}) collective-permute-start(f32[2,5,2,2,8,128]{5,4,3,2,1,0:T(8,128)} %get-tuple-element.24), channel_id=1, source_target_pairs={{0,1},{1,0},{2,3},{3,2},{4,5},{5,4},{6,7},{7,6},{8,9},{9,8},{10,11... | collective-permute-start | bytes 491528 | tf_op jit(solution)/shard_map/ppermute | solution.py:425
  37.6 11.7 %copy-start.12 = (s32[8,32,4]{1,2,0:T(4,128)S(1)}, s32[8,32,4]{1,2,0:T(4,128)}, u32[]{:S(2)}) copy-start(s32[8,32,4]{1,2,0:T(4,128)} %param.4) | copy-start | bytes 12292
  37.6 23.6 %all-to-all-start = ((f32[64,1,128]{2,1,0:T(1,128)}), f32[64,1,128]{2,1,0:T(1,128)S(1)}, u32[]{:S(2)}, u32[]{:S(2)}) async-start(f32[64,1,128]{2,1,0:T(1,128)} %get-tuple-element.23), calls=%async_computation | async-start | bytes 65536 | tf_op jit(solution)/shard_map/all_to_all | solution.py:427
  61.2 0.6 copy-start.7
  61.2 0.7 copy-start.2
  61.2 0.7 %copy-start.3 = (f32[2,5,2,2,8,128]{5,4,3,2,1,0:T(8,128)}, f32[2,5,2,2,8,128]{5,4,3,2,1,0:T(8,128)S(1)}, u32[]{:S(2)}) copy-start(f32[2,5,2,2,8,128]{5,4,3,2,1,0:T(8,128)S(1)} %collective-permute-done.10.got7) | copy-start | bytes 491524
  61.2 0.8 %copy-start.4 = (f32[2,5,2,2,8,128]{5,4,3,2,1,0:T(8,128)}, f32[2,5,2,2,8,128]{5,4,3,2,1,0:T(8,128)S(1)}, u32[]{:S(2)}) copy-start(f32[2,5,2,2,8,128]{5,4,3,2,1,0:T(8,128)S(1)} %collective-permute-done.8.got5) | copy-start | bytes 491524
  61.2 0.8 %copy-start.5 = (f32[2,5,2,2,8,128]{5,4,3,2,1,0:T(8,128)}, f32[2,5,2,2,8,128]{5,4,3,2,1,0:T(8,128)S(1)}, u32[]{:S(2)}) copy-start(f32[2,5,2,2,8,128]{5,4,3,2,1,0:T(8,128)S(1)} %collective-permute-done.6.got3) | copy-start | bytes 491524
  61.2 0.8 %copy-start.6 = (f32[2,5,2,2,8,128]{5,4,3,2,1,0:T(8,128)}, f32[2,5,2,2,8,128]{5,4,3,2,1,0:T(8,128)S(1)}, u32[]{:S(2)}) copy-start(f32[2,5,2,2,8,128]{5,4,3,2,1,0:T(8,128)S(1)} %collective-permute-done.4.got1) | copy-start | bytes 491524

commit v2 on v1

v2 whole, which is shorter than its diff:
```python
import jax
import jax.numpy as jnp
from jax import lax
from jax.experimental import pallas as pl
from jax.experimental.pallas import tpu as pltpu
from jax.sharding import PartitionSpec as P

HEAT_RATIO = 5.0 / 3.0
COURANT_FACTOR = 0.4
EMISSION_RATE = 100.0
F32 = jnp.float32
TILE = (8, 128)
BLOCKS = (4, 5, 2, 2) + TILE
TRAVEL = (2, 5, 2, 2) + TILE
VMEM = pl.BlockSpec(memory_space=pltpu.VMEM)
SMEM = pl.BlockSpec(memory_space=pltpu.SMEM)
PARAMS = pltpu.CompilerParams(vmem_limit_bytes=16 * 1024 * 1024)
BIG = 3e38
SMALL = 1e-37


def shape(*dims):
    return jax.ShapeDtypeStruct(dims, F32)


def iota(axis):
    return lax.broadcasted_iota(jnp.int32, TILE, axis)


def invert(x):
    r = pl.reciprocal(x, approx=True)
    return r * (2.0 - x * r)


def root(x):
    x = jnp.maximum(x, SMALL)
    return x * lax.rsqrt(x)


def half_minmod(a, b):
    return 0.5 * (jnp.maximum(jnp.minimum(a, b), 0.0) + jnp.minimum(jnp.maximum(a, b), 0.0))


def primitive(u):
    inverse = invert(u[0])
    v1, v2, v3 = u[1] * inverse, u[2] * inverse, u[3] * inverse
    p = (HEAT_RATIO - 1.0) * (u[4] - 0.5 * u[0] * (v1 * v1 + v2 * v2 + v3 * v3))
    return [u[0], v1, v2, v3, p], inverse


def hllc(left, right, n):
    rl, ul, pl_ = left[0], left[n], left[4]
    rr, ur, pr = right[0], right[n], right[4]
    cl = root(HEAT_RATIO * pl_ * invert(rl))
    cr = root(HEAT_RATIO * pr * invert(rr))
    sl = jnp.minimum(ul - cl, ur - cr)
    sr = jnp.maximum(ul + cl, ur + cr)
    ml = rl * (sl - ul)
    mr = rr * (sr - ur)
    mid = (pr - pl_ + ml * ul - mr * ur) * invert(ml - mr)
    use_left = (sl >= 0.0) | (mid >= 0.0)
    rho, v1, v2, v3, p = [jnp.where(use_left, a, b) for a, b in zip(left, right)]
    edge = jnp.where(use_left, sl, sr)
    clip = jnp.where(use_left, jnp.minimum(sl, 0.0), jnp.maximum(sr, 0.0))
    u = (None, v1, v2, v3)[n]
    energy = p * (1.0 / (HEAT_RATIO - 1.0)) + 0.5 * rho * (v1 * v1 + v2 * v2 + v3 * v3)
    gap = invert(jnp.where(clip == 0.0, 1.0, edge - mid))
    ratio = (edge - u) * gap
    star_rho = rho * ratio
    star_energy = ratio * energy + (mid - u) * (star_rho * mid + p * gap)
    mass = rho * u
    f_rho = mass + clip * (star_rho - rho)
    out = [f_rho, f_rho * v1, f_rho * v2, f_rho * v3, None]
    out[n] = mass * u + p + clip * (star_rho * mid - mass)
    out[4] = (energy + p) * u + clip * (star_energy - energy)
    return out


def prep_kernel(cons, u_out, w_out, e_bx, o_bx, e_by, o_by, in_bx, in_by):
    even_i = lax.axis_index("bx") % 2 == 0
    even_j = lax.axis_index("by") % 2 == 0
    lane = iota(1)
    bit0 = (lane // 16) % 2 == 0
    bit1 = (lane // 32) % 2 == 0
    row = iota(0)
    top = jnp.zeros(TILE, F32)
    for at in range(2):
        low, high, inner = [], [], []
        for h in range(2):
            tiles = []
            for f in range(5):
                x = [cons[f, pl.ds(at * 128 + h * 8 + b, 8, stride=16), :] for b in range(8)]
                if h == 0:
                    low.append(jnp.concatenate([x[0], x[1]], axis=1))
                    inner.append(x[2])
                else:
                    high.append(jnp.concatenate([x[6], x[7]], axis=1))
                    inner[f] = jnp.concatenate([x[5], inner[f]], axis=1)
                y = [jnp.concatenate([x[k], x[k + 4]], axis=1) for k in range(4)]
                z = [None] * 4
                for k in range(2):
                    z[k] = jnp.where(bit1, y[k], pltpu.roll(y[k + 2], 32, 1))
                    z[k + 2] = jnp.where(bit1, pltpu.roll(y[k], 96, 1), y[k + 2])
                t = [None] * 4
                for k in (0, 2):
                    t[k] = jnp.where(bit0, z[k], pltpu.roll(z[k + 1], 16, 1))
                    t[k + 1] = jnp.where(bit0, pltpu.roll(z[k], 112, 1), z[k + 1])
                tiles.append(t)
                for s in range(4):
                    u_out[s, f, at, h] = t[s]
            for s in range(4):
                w, inverse = primitive([tiles[f][s] for f in range(5)])
                speed = (
                    jnp.abs(w[1])
                    + jnp.abs(w[2])
                    + jnp.abs(w[3])
                    + 3.0 * root(HEAT_RATIO * w[4] * inverse)
                )
                top = jnp.maximum(top, speed)
                for f in range(5):
                    w_out[s, f, at, h] = w[f]
        low, _ = primitive(low)
        high, _ = primitive(high)
        inner, _ = primitive(inner)
        for f in range(5):
            e_by[f * 2 + at] = jnp.where(even_j, high[f], low[f])
            o_by[f * 2 + at] = jnp.where(even_j, low[f], high[f])
            in_by[f * 2 + at] = inner[f]
    for f in range(5):
        for h in range(2):
            low = jnp.zeros(TILE, F32)
            high = jnp.zeros(TILE, F32)
            inner = jnp.zeros(TILE, F32)
            for s in range(4):
                here = row // 2 == s
                a, b = w_out[s, f, 0, h], w_out[s, f, 1, h]
                low = jnp.where(here, pltpu.roll(a, 2 * s, 0), low)
                high = jnp.where(here, pltpu.roll(b, (2 * s + 2) % 8, 0), high)
                inner = jnp.where(row == 2 * s, pltpu.roll(b, (2 * s + 3) % 8, 0), inner)
                inner = jnp.where(row == 2 * s + 1, pltpu.roll(a, (2 * s + 7) % 8, 0), inner)
            e_bx[f * 2 + h] = jnp.where(even_i, high, low)
            o_bx[f * 2 + h] = jnp.where(even_i, low, high)
            in_bx[f * 2 + h] = inner
    for ref in (e_bx, o_bx, e_by, o_by):
        ref[10] = top


def inner_kernel(w, d, lefts, rights, fluxes):
    row, lane = iota(0), iota(1)

    def sweep(n, load, down, up, first, last, no_first, no_last):
        left, right = [[], []], [[], []]
        for f in range(5):
            a, b = load(f)
            da, ub = down(a), up(b)
            a_prev, b_prev = da, jnp.where(first, da, down(b))
            a_next, b_next = jnp.where(last, ub, up(a)), ub
            ha = half_minmod(a - a_prev, a_next - a)
            hb = half_minmod(b - b_prev, b_next - b)
            ra, rb = up(a - ha), up(b - hb)
            left[0].append(a + ha)
            left[1].append(b + hb)
            right[0].append(jnp.where(last, rb, ra))
            right[1].append(rb)
        fa = hllc(left[0], right[0], n)
        fb = hllc(left[1], right[1], n)
        out = []
        for f in range(5):
            a = jnp.where(no_first, 0.0, fa[f])
            b = jnp.where(no_last, 0.0, fb[f])
            da = down(a)
            out.append((a - jnp.where(first, 0.0, da), b - jnp.where(first, da, down(b))))
        return out

    def along_first(k, _):
        s, h = k // 2, k % 2
        out = sweep(
            1,
            lambda f: (w[s, f, 0, h], w[s, f, 1, h]),
            lambda a: pltpu.roll(a, 1, 0),
            lambda a: pltpu.roll(a, 7, 0),
            row == 0,
            row == 7,
            row == 0,
            row >= 6,
        )
        for f in range(5):
            d[s, f, 0, h], d[s, f, 1, h] = out[f]
        return 0

    def along_second(k, _):
        s, at = k // 2, k % 2
        out = sweep(
            2,
            lambda f: (w[s, f, at, 0], w[s, f, at, 1]),
            lambda a: pltpu.roll(a, 16, 1),
            lambda a: pltpu.roll(a, 112, 1),
            lane < 16,
            lane >= 112,
            lane < 16,
            lane >= 96,
        )
        for f in range(5):
            d[s, f, at, 0] += out[f][0]
            d[s, f, at, 1] += out[f][1]
        return 0

    first_c, last_c = lane % 16 == 0, lane % 16 == 15

    def previous(here, before):
        return jnp.where(first_c, pltpu.roll(before, 113, 1), pltpu.roll(here, 1, 1))

    def following(here, after):
        return jnp.where(last_c, pltpu.roll(after, 15, 1), pltpu.roll(here, 127, 1))

    def third_states(k, _):
        s, at = k // 2, k % 2
        before, after = (s + 3) % 4, (s + 1) % 4
        for h in range(2):
            for f in range(5):
                a = w[s, f, at, h]
                slope = half_minmod(
                    a - previous(a, w[before, f, at, h]), following(a, w[after, f, at, h]) - a
                )
                lefts[s, f, at, h] = a + slope
                rights[s, f, at, h] = a - slope
        return 0

    def third_fluxes(k, _):
        s, at = k // 2, k % 2
        after = (s + 1) % 4
        for h in range(2):
            out = hllc(
                [lefts[s, f, at, h] for f in range(5)],
                [following(rights[s, f, at, h], rights[after, f, at, h]) for f in range(5)],
                3,
            )
            for f in range(5):
                fluxes[s, f, at, h] = out[f]
        return 0

    def third_change(k, _):
        s, at = k // 2, k % 2
        before = (s + 3) % 4
        for h in range(2):
            for f in range(5):
                a = fluxes[s, f, at, h]
                d[s, f, at, h] += a - previous(a, fluxes[before, f, at, h])
        return 0

    for body in (along_first, along_second, third_states, third_fluxes, third_change):
        lax.fori_loop(0, 8, body, 0, unroll=2)


def edge_kernel(
    slots, u, d_in, se_bx, so_bx, se_by, so_by, in_bx, in_by, re_bx, ro_bx, re_by, ro_by,
    d, send_a, send_b, top_out,
):
    i, j = lax.axis_index("bx"), lax.axis_index("by")
    even_i, even_j = i % 2 == 0, j % 2 == 0
    row, lane = iota(0), iota(1)

    top = se_bx[10]
    for ref in (re_bx, ro_bx, re_by, ro_by):
        top = jnp.maximum(top, ref[10])
    top = jnp.max(top, axis=0, keepdims=True)
    top_out[...] = jnp.broadcast_to(top[None], top_out.shape)

    def faces(n, own_low, own_high, low, high, inner, back, ahead, zero):
        left, right, left2, right2 = [], [], [], []
        for o, q, a, b, w in zip(own_low, own_high, low, high, inner):
            c = jnp.where(zero, ahead(a), back(o))
            left.append(c + half_minmod(c - a, o - c))
            right.append(o - half_minmod(o - c, jnp.where(zero, ahead(o), w) - o))
            e = jnp.where(zero, ahead(q), back(b))
            left2.append(q + half_minmod(q - jnp.where(zero, w, back(q)), e - q))
            right2.append(e - half_minmod(e - q, b - e))
        low_flux = hllc(left, right, n)
        high_flux = hllc(left2, right2, n)
        return (
            [jnp.where(zero, ahead(f) - f, -f) for f in low_flux],
            [jnp.where(zero, f, f - back(f)) for f in high_flux],
        )

    def picked(flag, a, b, index):
        return [jnp.where(flag, a[t], b[t]) for t in range(index, 10, 2)]

    d[...] = d_in[...]
    for h in range(2):
        low, high = faces(
            1,
            picked(even_i, so_bx, se_bx, h),
            picked(even_i, se_bx, so_bx, h),
            picked(even_i, ro_bx, re_bx, h),
            picked(even_i, re_bx, ro_bx, h),
            [in_bx[t] for t in range(h, 10, 2)],
            lambda a: pltpu.roll(a, 1, 0),
            lambda a: pltpu.roll(a, 7, 0),
            row % 2 == 0,
        )
        for f in range(5):
            for s in range(4):
                d[s, f, 0, h] += jnp.where(row < 2, pltpu.roll(low[f], (8 - 2 * s) % 8, 0), 0.0)
                d[s, f, 1, h] += jnp.where(row >= 6, pltpu.roll(high[f], 6 - 2 * s, 0), 0.0)
    for at in range(2):
        turn = lambda a: pltpu.roll(a, 64, 1)
        low, high = faces(
            2,
            picked(even_j, so_by, se_by, at),
            picked(even_j, se_by, so_by, at),
            picked(even_j, ro_by, re_by, at),
            picked(even_j, re_by, ro_by, at),
            [in_by[t] for t in range(at, 10, 2)],
            turn,
            turn,
            lane < 64,
        )
        for f in range(5):
            for s in range(4):
                one = pltpu.roll(low[f], (128 - 16 * s) % 128, 1)
                two = pltpu.roll(low[f], 80 - 16 * s, 1)
                d[s, f, at, 0] += jnp.where(lane < 16, one, jnp.where(lane < 32, two, 0.0))
                one = pltpu.roll(high[f], 96 - 16 * s, 1)
                two = pltpu.roll(high[f], 48 - 16 * s, 1)
                d[s, f, at, 1] += jnp.where(lane >= 112, two, jnp.where(lane >= 96, one, 0.0))

    for r, ref in enumerate((send_a, send_b)):
        slot = slots[r, i, j]
        ref[0] = u[slot]
        ref[1] = d[slot]


def content(slots, i, j, slot):
    sw = lambda m, r: slots[r, i, j ^ m]
    second = slot == sw(0, 1)
    through = sw(2, 1) == sw(2, 0)
    first = slot == sw(0, 0)
    mask = jnp.where(second, jnp.where(through, 3, 2), jnp.where(first, 1, 0))
    index = jnp.where(
        second,
        jnp.where(through, sw(3, 0), sw(2, 1)),
        jnp.where(first, sw(1, 0), slot),
    )
    return mask, index


def relay_kernel(slots, u, d, got1, got2, got3, send):
    i, j = lax.axis_index("bx"), lax.axis_index("by")
    mask, index = content(slots, i, j, slots[2, i, j])

    @pl.when(mask == 0)
    def _():
        send[0] = u[index]
        send[1] = d[index]

    for m, ref in enumerate((got1, got2, got3), 1):

        @pl.when(mask == m)
        def _():
            send[...] = ref[...]


def tail_kernel(
    slots, counts, u, d, top, got1, got2, got3, got4, out, stage, energy, factor, tick
):
    i, j = lax.axis_index("bx"), lax.axis_index("by")
    speed = jnp.max(jnp.max(top[...], axis=0), axis=1, keepdims=True)
    step = COURANT_FACTOR / jnp.broadcast_to(speed, TILE)

    def count_of(slot):
        is_last = slots[2, i, j] == slot
        column = jnp.where(is_last, j ^ 4, j)
        mask, index = content(slots, i, column, jnp.where(is_last, slots[2, i, j ^ 4], slot))
        return jnp.where(is_last, 4, mask), index, counts[i, index, column ^ mask]

    def load(slot, _):
        mask, index, count = count_of(slot)

        @pl.when(mask == 0)
        def _():
            stage[0] = u[index]
            stage[1] = d[index]

        for m, ref in enumerate((got1, got2, got3, got4), 1):

            @pl.when(mask == m)
            def _():
                stage[...] = ref[...]

        chill = step / count.astype(F32)
        for at in range(2):
            for h in range(2):
                new = [stage[0, f, at, h] - step * stage[1, f, at, h] for f in range(5)]
                inverse = invert(new[0])
                squares = new[1] * new[1] + new[2] * new[2] + new[3] * new[3]
                kinetic = 0.5 * squares * inverse
                energy[slot, at, h] = new[4] - kinetic
                factor[slot, at, h] = (HEAT_RATIO - 1.0) * inverse
                tick[slot, at, h] = chill * new[0] * EMISSION_RATE
                new[4] = kinetic
                for f in range(5):
                    out[slot, f, pl.ds(8 * at, 8), pl.ds(128 * h, 128)] = new[f]
        return 0

    lax.fori_loop(0, 4, load, 0)
    limits = [count_of(slot)[2] for slot in range(4)]
    most = jnp.maximum(jnp.maximum(limits[0], limits[1]), jnp.maximum(limits[2], limits[3]))

    def advance(k, _):
        for slot in range(4):
            for at in range(2):
                for h in range(2):
                    now = energy[slot, at, h]
                    heat = now * factor[slot, at, h]
                    loss = tick[slot, at, h] * root(jnp.minimum(1.0 + heat * heat, BIG))
                    new = now * invert(jnp.minimum(1.0 + loss, BIG))
                    energy[slot, at, h] = jnp.where(k < limits[slot], new, now)
        return 0

    lax.fori_loop(0, most, advance, 0)
    for slot in range(4):
        for at in range(2):
            for h in range(2):
                place = (slot, 4, pl.ds(8 * at, 8), pl.ds(128 * h, 128))
                out[place] = out[place] + energy[slot, at, h]


def pair_even(count):
    return [(k, k ^ 1) for k in range(count)]


def pair_odd(count):
    return [(k, (k + 1) % count if k % 2 else (k - 1) % count) for k in range(count)]


def call(kernel, inputs, outputs, scratch=(), smem=0):
    return pl.pallas_call(
        kernel,
        in_specs=[SMEM] * smem + [VMEM] * (len(inputs) - smem),
        out_specs=[VMEM] * len(outputs),
        out_shape=[shape(*dims) for dims in outputs],
        scratch_shapes=[pltpu.VMEM(dims, F32) for dims in scratch],
        compiler_params=PARAMS,
    )(*inputs)


def on_device(conserved, cool_steps, swap_slot):
    rows, columns = lax.axis_size("bx"), lax.axis_size("by")
    slots = swap_slot.transpose(2, 0, 1)
    counts = cool_steps.transpose(0, 2, 1)
    slab = (11,) + TILE
    inner = (10,) + TILE
    u, w, *slabs = call(
        prep_kernel, [conserved.reshape(5, 256, 64)], [BLOCKS] * 2 + [slab] * 4 + [inner] * 2
    )
    e_bx, o_bx, e_by, o_by = slabs[:4]
    got_slabs = [
        lax.ppermute(e_bx, "bx", pair_even(rows)),
        lax.ppermute(o_bx, "bx", pair_odd(rows)),
        lax.ppermute(e_by, "by", pair_even(columns)),
        lax.ppermute(o_by, "by", pair_odd(columns)),
    ]
    (d,) = call(inner_kernel, [w], [BLOCKS], [BLOCKS] * 3)
    groups = [
        [i * columns + j for i in range(rows) for j in range(columns) if (i + 2 * j) % 4 == r]
        for r in range(4)
    ]
    size = len(groups[0])
    d, send_a, send_b, top = call(
        edge_kernel,
        [slots, u, d, *slabs, *got_slabs],
        [BLOCKS] + [TRAVEL] * 2 + [(size, 1, 128)],
        smem=1,
    )
    sends = {1: send_a, 2: send_b, 3: send_a}
    trade = lambda m, block: lax.ppermute(block, "by", [(k, k ^ m) for k in range(columns)])
    got = [trade(m, block) for m, block in sends.items()]
    top = lax.all_to_all(top, ("bx", "by"), 0, 0, axis_index_groups=groups)
    (send_c,) = call(relay_kernel, [slots, u, d, *got], [TRAVEL], smem=1)
    got.append(trade(4, send_c))
    (result,) = call(
        tail_kernel,
        [slots, counts, u, d, top, *got],
        [(4, 5, 16, 256)],
        [TRAVEL] + [(4, 2, 2) + TILE] * 3,
        smem=2,
    )
    return result.reshape((1, 1) + result.shape)


def solution(mesh):
    in_specs = (P(None, "bx", "by", None), P(), P())
    out_specs = P("bx", "by", None, None, None, None)
    return jax.shard_map(
        on_device, mesh=mesh, in_specs=in_specs, out_specs=out_specs, check_vma=False
    )
```

time: 68.7 us -> 51.8 us (0.75)
  blocking collectives: 0 us -> 22.3 us
  starting transfers between devices: 34.4 us -> 14.3 us
  Pallas kernels: 18.4 us -> 8.44 us
  waiting for transfers between devices: 12.5 us -> 5.36 us
  local copies, waits for them, and re-layouts: 3.03 us -> 1.1 us
    all_to_all x0 -> x1, blocking collectives: none -> 22.3 us  [on_device(): top = lax.all_to_all(top, ('bx', 'by'), 0, 0, axis_index_groups=groups)]
    all_to_all x1 -> x0, starting transfers between devices: 11.7 us -> none  [on_device(): top = lax.all_to_all(top, ('bx', 'by'), 0, 0, axis_index_groups=groups)]
    all_to_all x1 -> x0, waiting for transfers between devices: 11.1 us -> none  [on_device(): top = lax.all_to_all(top, ('bx', 'by'), 0, 0, axis_index_groups=groups)]
    pallas_call x3 -> x5, Pallas kernels: 18.4 us -> 8.44 us  [call(): pl.pallas_call(kernel, in_specs=[SMEM] * smem + [VMEM] * (len(inputs) - s...]
    ppermute x7 -> x4, starting transfers between devices: 16.8 us -> 8.37 us  [on_device(): lax.ppermute(block, 'by', [(k, k ^ m) for k in range(columns)])]
    ppermute x7 -> x4, waiting for transfers between devices: 0.02 us -> 5.34 us  [on_device(): lax.ppermute(block, 'by', [(k, k ^ m) for k in range(columns)])]
    unnamed x30 -> x6, local copies, waits for them, and re-layouts: 3.03 us -> 1.1 us
    ppermute x1, waiting for transfers between devices: 0.76 us -> 0.01 us  [on_device(): lax.ppermute(e_by, 'by', pair_even(columns))]
  transfers between devices with their start and end apart: 12 -> 8, of which waited for: 3 -> 2; matrix products, arithmetic and copies ran while one was open for 2% -> 0% of each run, Pallas kernels for 0% -> 7%
where the time goes in v2:
time: 51.8 us; the launch traced here: 51.5 us
  blocking collectives  22.3 us (43%)
  starting transfers between devices  14.3 us (28%)
  Pallas kernels  8.44 us (16%)
  waiting for transfers between devices  5.36 us (10%)
  local copies, waits for them, and re-layouts  1.1 us (2%)
    all_to_all x1, blocking collectives, on_device(): top = lax.all_to_all(top, ('bx', 'by'), 0, 0, axis_index_groups=groups)  22.3 us
    pallas_call x5, Pallas kernels, call(): pl.pallas_call(kernel, in_specs=[SMEM] * smem + [VMEM] * (len(inputs) - s...  8.44 us
    ppermute x4, starting transfers between devices, on_device(): lax.ppermute(block, 'by', [(k, k ^ m) for k in range(columns)])  8.37 us
    ppermute x4, waiting for transfers between devices, on_device(): lax.ppermute(block, 'by', [(k, k ^ m) for k in range(columns)])  5.34 us
    ppermute x1, starting transfers between devices, on_device(): lax.ppermute(o_bx, 'bx', pair_odd(rows))  3.12 us
    ppermute x1, starting transfers between devices, on_device(): lax.ppermute(o_by, 'by', pair_odd(columns))  2.15 us
    unnamed x6, local copies, waits for them, and re-layouts  1.1 us
  transfers between devices with their start and end apart: 8, of which 2 were waited for; matrix products, arithmetic and copies ran while one was open for 0% of the time, Pallas kernels for 7%

profile of v2, /device:TPU:2, one launch (start us, length us, event | category | flops | bytes accessed | tf_op | source)
XLA Modules:
  0.0 51.5 jit_solution(4889077174192402543)
XLA Ops:
  0.0 0.0 copy-start
  0.0 1.1 %copy-done = f32[5,16,16,64]{3,2,1,0:T(8,128)S(1)} copy-done((f32[5,16,16,64]{3,2,1,0:T(8,128)S(1)}, f32[5,16,16,64]{3,2,1,0:T(8,128)}, u32[]{:S(2)}) %copy-start) | copy-done | bytes 327704
  1.1 0.6 %shard_map.37 = (f32[4,5,2,2,8,128]{5,4,3,2,1,0:T(8,128)S(1)}, f32[4,5,2,2,8,128]{5,4,3,2,1,0:T(8,128)S(1)}, f32[11,8,128]{2,1,0:T(8,128)S(1)}, f32[11,8,128]{2,...) custom-call(f32[5,256,64]{2,1,0:T(8,128)S(1)} %bitcast.4), custom_call_target="tpu_custom_call" | custom-call | tf_op jit(solution)/shard_map/pallas_call | solution.py:437
  1.7 0.1 collective-permute-start
  1.8 3.1 %collective-permute-start.1 = (f32[11,8,128]{2,1,0:T(8,128)S(1)}, f32[11,8,128]{2,1,0:T(8,128)S(1)}, u32[]{:S(2)}, u32[]{:S(2)}) collective-permute-start(f32[11,8,128]{2,1,0:T(8,128)S(1)} %get-tuple-element.20.so_bx), channel_id=1, source_target_pairs={{0,224},{32,64},{64,32},{96,128},{128,96},{160,192},{192,160},{224... | collective-permute-start | bytes 135176 | tf_op jit(solution)/shard_map/ppermute | solution.py:459
  4.9 0.5 %collective-permute-start.2 = (f32[11,8,128]{2,1,0:T(8,128)S(1)}, f32[11,8,128]{2,1,0:T(8,128)S(1)}, u32[]{:S(2)}, u32[]{:S(2)}) collective-permute-start(f32[11,8,128]{2,1,0:T(8,128)S(1)} %get-tuple-element.21.se_by), channel_id=1, source_target_pairs={{0,1},{1,0},{2,3},{3,2},{4,5},{5,4},{6,7},{7,6},{8,9},{9,8},{10,11... | collective-permute-start | bytes 135176 | tf_op jit(solution)/shard_map/ppermute | solution.py:460
  5.5 2.2 %collective-permute-start.3 = (f32[11,8,128]{2,1,0:T(8,128)S(1)}, f32[11,8,128]{2,1,0:T(8,128)S(1)}, u32[]{:S(2)}, u32[]{:S(2)}) collective-permute-start(f32[11,8,128]{2,1,0:T(8,128)S(1)} %get-tuple-element.22.so_by), channel_id=1, source_target_pairs={{0,31},{1,2},{2,1},{3,4},{4,3},{5,6},{6,5},{7,8},{8,7},{9,10},{10,... | collective-permute-start | bytes 135176 | tf_op jit(solution)/shard_map/ppermute | solution.py:461
  7.6 0.0 copy-start.1
  7.6 3.5 %shard_map.38.d_in = f32[4,5,2,2,8,128]{5,4,3,2,1,0:T(8,128)S(1)} custom-call(f32[4,5,2,2,8,128]{5,4,3,2,1,0:T(8,128)S(1)} %get-tuple-element.18.w), custom_call_target="tpu_custom_call" | custom-call | tf_op jit(solution)/shard_map/pallas_call | solution.py:437
  11.2 0.0 collective-permute-done.re_bx
  11.2 0.0 collective-permute-done.1.ro_bx
  11.2 0.0 collective-permute-done.2.re_by
  11.2 0.0 collective-permute-done.3.ro_by
  11.2 0.0 copy-done.1
  11.2 1.2 %shard_map.39 = (f32[4,5,2,2,8,128]{5,4,3,2,1,0:T(8,128)S(1)}, f32[2,5,2,2,8,128]{5,4,3,2,1,0:T(8,128)S(1)}, f32[2,5,2,2,8,128]{5,4,3,2,1,0:T(8,128)S(1)}, f32[64,1,128]{2,1,0:T(1,128)S(1)}) custom-call(s32[3,8,32]{2,1,0:T(8,128)S(1)} %bitcast.5, f32[4,5,2,2,8,128]{5,4,3,2,1,0:T(8,128)S(1)} %get-tuple-element.17.u, ...), custom_call_target="tpu_custom_call" | custom-call | tf_op jit(solution)/shard_map/pallas_call | solution.py:437
  12.4 2.9 %collective-permute-start.5 = (f32[2,5,2,2,8,128]{5,4,3,2,1,0:T(8,128)S(1)}, f32[2,5,2,2,8,128]{5,4,3,2,1,0:T(8,128)S(1)}, u32[]{:S(2)}, u32[]{:S(2)}) collective-permute-start(f32[2,5,2,2,8,128]{5,4,3,2,1,0:T(8,128)S(1)} %get-tuple-element.28), channel_id=1, source_target_pairs={{0,2},{1,3},{2,0},{3,1},{4,6},{5,7},{6,4},{7,5},{8,10},{9,11},{10,... | collective-permute-start | bytes 491528 | tf_op jit(solution)/shard_map/ppermute | solution.py:476
  15.3 5.4 %collective-permute-start.6 = (f32[2,5,2,2,8,128]{5,4,3,2,1,0:T(8,128)S(1)}, f32[2,5,2,2,8,128]{5,4,3,2,1,0:T(8,128)S(1)}, u32[]{:S(2)}, u32[]{:S(2)}) collective-permute-start(f32[2,5,2,2,8,128]{5,4,3,2,1,0:T(8,128)S(1)} %get-tuple-element.27), channel_id=1, source_target_pairs={{0,3},{1,2},{2,1},{3,0},{4,7},{5,6},{6,5},{7,4},{8,11},{9,10},{10,... | collective-permute-start | bytes 491528 | tf_op jit(solution)/shard_map/ppermute | solution.py:476
  20.7 0.0 collective-permute-start.4
  20.7 0.0 collective-permute-done.5.got2
  20.7 3.5 %collective-permute-done.6.got3 = f32[2,5,2,2,8,128]{5,4,3,2,1,0:T(8,128)S(1)} collective-permute-done((f32[2,5,2,2,8,128]{5,4,3,2,1,0:T(8,128)S(1)}, f32[2,5,2,2,8,128]{5,4,3,2,1,0:T(8,128)S(1)}, u32[]{:S(2)}, u32[]{:S(2)}) %collective-permute-start.6) | collective-permute-done | bytes 163872 | tf_op jit(solution)/shard_map/ppermute | solution.py:476
  24.2 1.8 %collective-permute-done.4.got1 = f32[2,5,2,2,8,128]{5,4,3,2,1,0:T(8,128)S(1)} collective-permute-done((f32[2,5,2,2,8,128]{5,4,3,2,1,0:T(8,128)S(1)}, f32[2,5,2,2,8,128]{5,4,3,2,1,0:T(8,128)S(1)}, u32[]{:S(2)}, u32[]{:S(2)}) %collective-permute-start.4) | collective-permute-done | bytes 163872 | tf_op jit(solution)/shard_map/ppermute | solution.py:476
  26.0 0.8 %shard_map.40 = f32[2,5,2,2,8,128]{5,4,3,2,1,0:T(8,128)S(1)} custom-call(s32[3,8,32]{2,1,0:T(8,128)S(1)} %bitcast.6, f32[4,5,2,2,8,128]{5,4,3,2,1,0:T(8,128)S(1)} %get-tuple-element.17.u, f32[4,5,2,2,8,128]{5,4,3,2,1,0:T(8,128)S(1)} %get-tuple-element.25.d, f32[2,5,2,2,8,128]{5,4,3,2,1,0:T(8,128)S(1)} %collective-permute-done.4.got1, ...), custom_call_target="tpu_custom_call" | custom-call | tf_op jit(solution)/shard_map/pallas_call | solution.py:437
  26.8 0.1 collective-permute-start.7
  26.9 0.0 copy-start.2
  26.9 22.3 %all_to_all.5.top = f32[64,1,128]{2,1,0:T(1,128)S(1)} all-to-all(f32[64,1,128]{2,1,0:T(1,128)S(1)} %get-tuple-element.26), channel_id=1, replica_groups={{0,2,4,6,8,10,12,14,16,18,20,22,24,26,28,30,65,67,69,71,73,75,77,79,81,..., dimensions={0} | all-to-all | bytes 65536 | tf_op jit(solution)/shard_map/all_to_all | solution.py:478
  49.2 0.0 collective-permute-done.7.got4
  49.2 0.0 copy-done.2
  49.2 2.3 %shard_map.41 = f32[4,5,16,256]{3,2,1,0:T(8,128)} custom-call(s32[3,8,32]{2,1,0:T(8,128)S(1)} %bitcast.7, s32[8,4,32]{2,1,0:T(4,128)S(1)} %bitcast.8, f32[4,5,2,2,8,128]{5,4,3,2,1,0:T(8,128)S(1)} %get-tuple-element.17.u, f32[4,5,2,2,8,128]{5,4,3,2,1,0:T(8,128)S(1)} %get-tuple-element.25.d, f32[64,1,128]{2,1,0:T(1,128)S(1)} %all_to_all.5.top, ...), custom_call_target="tpu_custom_call" | custom-call | tf_op jit(solution)/shard_map/pallas_call | solution.py:437
Async XLA Ops:
  0.0 1.1 %copy-start = (f32[5,16,16,64]{3,2,1,0:T(8,128)S(1)}, f32[5,16,16,64]{3,2,1,0:T(8,128)}, u32[]{:S(2)}) copy-start(f32[5,16,16,64]{3,2,1,0:T(8,128)} %param.3) | copy-start | bytes 983044
  1.7 9.4 %collective-permute-start = (f32[11,8,128]{2,1,0:T(8,128)S(1)}, f32[11,8,128]{2,1,0:T(8,128)S(1)}, u32[]{:S(2)}, u32[]{:S(2)}) collective-permute-start(f32[11,8,128]{2,1,0:T(8,128)S(1)} %get-tuple-element.19.se_bx), channel_id=1, source_target_pairs={{0,32},{32,0},{64,96},{96,64},{128,160},{160,128},{192,224},{224,1... | collective-permute-start | bytes 135176 | tf_op jit(solution)/shard_map/ppermute | solution.py:458
  1.8 9.4 %collective-permute-start.1 = (f32[11,8,128]{2,1,0:T(8,128)S(1)}, f32[11,8,128]{2,1,0:T(8,128)S(1)}, u32[]{:S(2)}, u32[]{:S(2)}) collective-permute-start(f32[11,8,128]{2,1,0:T(8,128)S(1)} %get-tuple-element.20.so_bx), channel_id=1, source_target_pairs={{0,224},{32,64},{64,32},{96,128},{128,96},{160,192},{192,160},{224... | collective-permute-start | bytes 135176 | tf_op jit(solution)/shard_map/ppermute | solution.py:459
  4.9 6.2 %collective-permute-start.2 = (f32[11,8,128]{2,1,0:T(8,128)S(1)}, f32[11,8,128]{2,1,0:T(8,128)S(1)}, u32[]{:S(2)}, u32[]{:S(2)}) collective-permute-start(f32[11,8,128]{2,1,0:T(8,128)S(1)} %get-tuple-element.21.se_by), channel_id=1, source_target_pairs={{0,1},{1,0},{2,3},{3,2},{4,5},{5,4},{6,7},{7,6},{8,9},{9,8},{10,11... | collective-permute-start | bytes 135176 | tf_op jit(solution)/shard_map/ppermute | solution.py:460
  5.5 5.7 %collective-permute-start.3 = (f32[11,8,128]{2,1,0:T(8,128)S(1)}, f32[11,8,128]{2,1,0:T(8,128)S(1)}, u32[]{:S(2)}, u32[]{:S(2)}) collective-permute-start(f32[11,8,128]{2,1,0:T(8,128)S(1)} %get-tuple-element.22.so_by), channel_id=1, source_target_pairs={{0,31},{1,2},{2,1},{3,4},{4,3},{5,6},{6,5},{7,8},{8,7},{9,10},{10,... | collective-permute-start | bytes 135176 | tf_op jit(solution)/shard_map/ppermute | solution.py:461
  7.6 3.6 %copy-start.1 = (s32[8,32,3]{1,0,2:T(8,128)S(1)}, s32[8,32,3]{1,0,2:T(8,128)}, u32[]{:S(2)}) copy-start(s32[8,32,3]{1,0,2:T(8,128)} %param.5) | copy-start | bytes 9220
  12.4 8.3 %collective-permute-start.5 = (f32[2,5,2,2,8,128]{5,4,3,2,1,0:T(8,128)S(1)}, f32[2,5,2,2,8,128]{5,4,3,2,1,0:T(8,128)S(1)}, u32[]{:S(2)}, u32[]{:S(2)}) collective-permute-start(f32[2,5,2,2,8,128]{5,4,3,2,1,0:T(8,128)S(1)} %get-tuple-element.28), channel_id=1, source_target_pairs={{0,2},{1,3},{2,0},{3,1},{4,6},{5,7},{6,4},{7,5},{8,10},{9,11},{10,... | collective-permute-start | bytes 491528 | tf_op jit(solution)/shard_map/ppermute | solution.py:476
  15.3 8.9 %collective-permute-start.6 = (f32[2,5,2,2,8,128]{5,4,3,2,1,0:T(8,128)S(1)}, f32[2,5,2,2,8,128]{5,4,3,2,1,0:T(8,128)S(1)}, u32[]{:S(2)}, u32[]{:S(2)}) collective-permute-start(f32[2,5,2,2,8,128]{5,4,3,2,1,0:T(8,128)S(1)} %get-tuple-element.27), channel_id=1, source_target_pairs={{0,3},{1,2},{2,1},{3,0},{4,7},{5,6},{6,5},{7,4},{8,11},{9,10},{10,... | collective-permute-start | bytes 491528 | tf_op jit(solution)/shard_map/ppermute | solution.py:476
  20.7 5.3 %collective-permute-start.4 = (f32[2,5,2,2,8,128]{5,4,3,2,1,0:T(8,128)S(1)}, f32[2,5,2,2,8,128]{5,4,3,2,1,0:T(8,128)S(1)}, u32[]{:S(2)}, u32[]{:S(2)}) collective-permute-start(f32[2,5,2,2,8,128]{5,4,3,2,1,0:T(8,128)S(1)} %get-tuple-element.27), channel_id=1, source_target_pairs={{0,1},{1,0},{2,3},{3,2},{4,5},{5,4},{6,7},{7,6},{8,9},{9,8},{10,11... | collective-permute-start | bytes 491528 | tf_op jit(solution)/shard_map/ppermute | solution.py:476
  26.8 22.4 %collective-permute-start.7 = (f32[2,5,2,2,8,128]{5,4,3,2,1,0:T(8,128)S(1)}, f32[2,5,2,2,8,128]{5,4,3,2,1,0:T(8,128)S(1)}, u32[]{:S(2)}, u32[]{:S(2)}) collective-permute-start(f32[2,5,2,2,8,128]{5,4,3,2,1,0:T(8,128)S(1)} %shard_map.40), channel_id=1, source_target_pairs={{0,4},{1,5},{2,6},{3,7},{4,0},{5,1},{6,2},{7,3},{8,12},{9,13},{10,... | collective-permute-start | bytes 491528 | tf_op jit(solution)/shard_map/ppermute | solution.py:476
  26.9 22.3 %copy-start.2 = (s32[8,32,4]{1,2,0:T(4,128)S(1)}, s32[8,32,4]{1,2,0:T(4,128)}, u32[]{:S(2)}) copy-start(s32[8,32,4]{1,2,0:T(4,128)} %param.4) | copy-start | bytes 12292

commit v3 on v2

--- a/solution.py
+++ b/solution.py
@@ -76,7 +76,7 @@
     return out
 
 
-def prep_kernel(cons, u_out, w_out, e_bx, o_bx, e_by, o_by, in_bx, in_by):
+def prep_kernel(cons, u_out, w_out, e_bx, o_bx, e_by, o_by, in_bx, in_by, top_out):
     even_i = lax.axis_index("bx") % 2 == 0
     even_j = lax.axis_index("by") % 2 == 0
     lane = iota(1)
@@ -141,8 +141,9 @@
             e_bx[f * 2 + h] = jnp.where(even_i, high, low)
             o_bx[f * 2 + h] = jnp.where(even_i, low, high)
             in_bx[f * 2 + h] = inner
-    for ref in (e_bx, o_bx, e_by, o_by):
+    for ref in (e_by, o_by):
         ref[10] = top
+    top_out[...] = top
 
 
 def inner_kernel(w, d, lefts, rights, fluxes):
@@ -253,18 +254,17 @@
 
 
 def edge_kernel(
-    slots, u, d_in, se_bx, so_bx, se_by, so_by, in_bx, in_by, re_bx, ro_bx, re_by, ro_by,
+    slots, u, d_in, se_bx, so_bx, se_by, so_by, in_bx, in_by, top, re_bx, ro_bx, re_by, ro_by, top2,
     d, send_a, send_b, top_out,
 ):
     i, j = lax.axis_index("bx"), lax.axis_index("by")
     even_i, even_j = i % 2 == 0, j % 2 == 0
     row, lane = iota(0), iota(1)
 
-    top = se_bx[10]
-    for ref in (re_bx, ro_bx, re_by, ro_by):
-        top = jnp.maximum(top, ref[10])
-    top = jnp.max(top, axis=0, keepdims=True)
-    top_out[...] = jnp.broadcast_to(top[None], top_out.shape)
+    top = jnp.maximum(jnp.maximum(top[...], top2[...]), jnp.maximum(re_by[10], ro_by[10]))
+    top = jnp.broadcast_to(jnp.max(top, axis=0, keepdims=True), TILE)
+    for k in range(top_out.shape[0]):
+        top_out[k] = top
 
     def faces(n, own_low, own_high, low, high, inner, back, ahead, zero):
         left, right, left2, right2 = [], [], [], []
@@ -364,7 +364,7 @@
     slots, counts, u, d, top, got1, got2, got3, got4, out, stage, energy, factor, tick
 ):
     i, j = lax.axis_index("bx"), lax.axis_index("by")
-    speed = jnp.max(jnp.max(top[...], axis=0), axis=1, keepdims=True)
+    speed = jnp.max(jnp.max(jnp.max(top[...], axis=0), axis=0, keepdims=True), axis=1, keepdims=True)
     step = COURANT_FACTOR / jnp.broadcast_to(speed, TILE)
 
     def count_of(slot):
@@ -449,9 +449,11 @@
     slots = swap_slot.transpose(2, 0, 1)
     counts = cool_steps.transpose(0, 2, 1)
     slab = (11,) + TILE
-    inner = (10,) + TILE
+    face = (10,) + TILE
     u, w, *slabs = call(
-        prep_kernel, [conserved.reshape(5, 256, 64)], [BLOCKS] * 2 + [slab] * 4 + [inner] * 2
+        prep_kernel,
+        [conserved.reshape(5, 256, 64)],
+        [BLOCKS] * 2 + [face] * 2 + [slab] * 2 + [face] * 2 + [TILE],
     )
     e_bx, o_bx, e_by, o_by = slabs[:4]
     got_slabs = [
@@ -459,23 +461,25 @@
         lax.ppermute(o_bx, "bx", pair_odd(rows)),
         lax.ppermute(e_by, "by", pair_even(columns)),
         lax.ppermute(o_by, "by", pair_odd(columns)),
+        lax.ppermute(slabs[-1], "by", [(k, k ^ 2) for k in range(columns)]),
     ]
     (d,) = call(inner_kernel, [w], [BLOCKS], [BLOCKS] * 3)
     groups = [
-        [i * columns + j for i in range(rows) for j in range(columns) if (i + 2 * j) % 4 == r]
-        for r in range(4)
+        [i * columns + j for i in range(rows) for j in range(x, columns, 4)] for x in range(4)
     ]
     size = len(groups[0])
     d, send_a, send_b, top = call(
         edge_kernel,
         [slots, u, d, *slabs, *got_slabs],
-        [BLOCKS] + [TRAVEL] * 2 + [(size, 1, 128)],
+        [BLOCKS] + [TRAVEL] * 2 + [(size // 2,) + TILE],
         smem=1,
     )
     sends = {1: send_a, 2: send_b, 3: send_a}
     trade = lambda m, block: lax.ppermute(block, "by", [(k, k ^ m) for k in range(columns)])
     got = [trade(m, block) for m, block in sends.items()]
+    top = top.reshape(size, 4, 128)
     top = lax.all_to_all(top, ("bx", "by"), 0, 0, axis_index_groups=groups)
+    top = top.reshape((size // 2,) + TILE)
     (send_c,) = call(relay_kernel, [slots, u, d, *got], [TRAVEL], smem=1)
     got.append(trade(4, send_c))
     (result,) = call(

time: 51.8 us -> 43.1 us (0.83)
  blocking collectives: 22.3 us -> 0 us
  starting transfers between devices: 14.3 us -> 23.8 us
  waiting for transfers between devices: 5.36 us -> 8.73 us
  Pallas kernels: 8.44 us -> 9.34 us
    all_to_all x1 -> x0, blocking collectives: 22.3 us -> none  [on_device(): top = lax.all_to_all(top, ('bx', 'by'), 0, 0, axis_index_groups=groups)]
    all_to_all x0 -> x1, waiting for transfers between devices: none -> 8.7 us  [on_device(): top = lax.all_to_all(top, ('bx', 'by'), 0, 0, axis_index_groups=groups)]
    all_to_all x0 -> x1, starting transfers between devices: none -> 5.96 us  [on_device(): top = lax.all_to_all(top, ('bx', 'by'), 0, 0, axis_index_groups=groups)]
    ppermute x4, waiting for transfers between devices: 5.34 us -> 0.01 us  [on_device(): lax.ppermute(block, 'by', [(k, k ^ m) for k in range(columns)])]
    ppermute x0 -> x1, starting transfers between devices: none -> 2.76 us  [on_device(): lax.ppermute(slabs[-1], 'by', [(k, k ^ 2) for k in range(columns)])]
    ppermute x1, starting transfers between devices: 0.53 us -> 2.36 us  [on_device(): lax.ppermute(e_by, 'by', pair_even(columns))]
    ppermute x1, starting transfers between devices: 2.15 us -> 0.42 us  [on_device(): lax.ppermute(o_by, 'by', pair_odd(columns))]
    pallas_call x5, Pallas kernels: 8.44 us -> 9.34 us  [call(): pl.pallas_call(kernel, in_specs=[SMEM] * smem + [VMEM] * (len(inputs) - s...]
  transfers between devices with their start and end apart: 8 -> 10, of which waited for: 2 -> 1; matrix products, arithmetic and copies ran while one was open for 0% -> 0% of each run, Pallas kernels for 7% -> 10%
where the time goes in v3:
time: 43.1 us
  starting transfers between devices  23.8 us (55%)
  Pallas kernels  9.34 us (22%)
  waiting for transfers between devices  8.73 us (20%)
  local copies, waits for them, and re-layouts  1.1 us (3%)
    pallas_call x5, Pallas kernels, call(): pl.pallas_call(kernel, in_specs=[SMEM] * smem + [VMEM] * (len(inputs) - s...  9.34 us
    ppermute x4, starting transfers between devices, on_device(): lax.ppermute(block, 'by', [(k, k ^ m) for k in range(columns)])  9.16 us
    all_to_all x1, waiting for transfers between devices, on_device(): top = lax.all_to_all(top, ('bx', 'by'), 0, 0, axis_index_groups=groups)  8.7 us
    all_to_all x1, starting transfers between devices, on_device(): top = lax.all_to_all(top, ('bx', 'by'), 0, 0, axis_index_groups=groups)  5.96 us
    ppermute x1, starting transfers between devices, on_device(): lax.ppermute(o_bx, 'bx', pair_odd(rows))  3.13 us
    ppermute x1, starting transfers between devices, on_device(): lax.ppermute(slabs[-1], 'by', [(k, k ^ 2) for k in range(columns)])  2.76 us
    ppermute x1, starting transfers between devices, on_device(): lax.ppermute(e_by, 'by', pair_even(columns))  2.36 us
    unnamed x6, local copies, waits for them, and re-layouts  1.1 us
  transfers between devices with their start and end apart: 10, of which 1 were waited for; matrix products, arithmetic and copies ran while one was open for 0% of the time, Pallas kernels for 10%

profile of v3, /device:TPU:2, one launch (start us, length us, event | category | flops | bytes accessed | tf_op | source)
XLA Modules:
  0.0 43.1 jit_solution(14506619020473976154)
XLA Ops:
  0.0 0.0 copy-start
  0.0 1.1 %copy-done = f32[5,16,16,64]{3,2,1,0:T(8,128)S(1)} copy-done((f32[5,16,16,64]{3,2,1,0:T(8,128)S(1)}, f32[5,16,16,64]{3,2,1,0:T(8,128)}, u32[]{:S(2)}) %copy-start) | copy-done | bytes 327704
  1.1 0.6 %shard_map.37 = (f32[4,5,2,2,8,128]{5,4,3,2,1,0:T(8,128)S(1)}, f32[4,5,2,2,8,128]{5,4,3,2,1,0:T(8,128)S(1)}, f32[10,8,128]{2,1,0:T(8,128)S(1)}, f32[10,8,128]{2,...) custom-call(f32[5,256,64]{2,1,0:T(8,128)S(1)} %bitcast.6), custom_call_target="tpu_custom_call" | custom-call | tf_op jit(solution)/shard_map/pallas_call | solution.py:437
  1.7 2.4 %collective-permute-start.2 = (f32[11,8,128]{2,1,0:T(8,128)S(1)}, f32[11,8,128]{2,1,0:T(8,128)S(1)}, u32[]{:S(2)}, u32[]{:S(2)}) collective-permute-start(f32[11,8,128]{2,1,0:T(8,128)S(1)} %get-tuple-element.22.se_by), channel_id=1, source_target_pairs={{0,1},{1,0},{2,3},{3,2},{4,5},{5,4},{6,7},{7,6},{8,9},{9,8},{10,11... | collective-permute-start | bytes 135176 | tf_op jit(solution)/shard_map/ppermute | solution.py:462
  4.1 0.4 collective-permute-start.3
  4.5 0.0 collective-permute-start
  4.5 3.1 %collective-permute-start.1 = (f32[10,8,128]{2,1,0:T(8,128)S(1)}, f32[10,8,128]{2,1,0:T(8,128)S(1)}, u32[]{:S(2)}, u32[]{:S(2)}) collective-permute-start(f32[10,8,128]{2,1,0:T(8,128)S(1)} %get-tuple-element.21.so_bx), channel_id=1, source_target_pairs={{0,224},{32,64},{64,32},{96,128},{128,96},{160,192},{192,160},{224... | collective-permute-start | bytes 122888 | tf_op jit(solution)/shard_map/ppermute | solution.py:461
  7.6 2.8 %collective-permute-start.4 = (f32[8,128]{1,0:T(8,128)S(1)}, f32[8,128]{1,0:T(8,128)S(1)}, u32[]{:S(2)}, u32[]{:S(2)}) collective-permute-start(f32[8,128]{1,0:T(8,128)S(1)} %get-tuple-element.26.top), channel_id=1, source_target_pairs={{0,2},{1,3},{2,0},{3,1},{4,6},{5,7},{6,4},{7,5},{8,10},{9,11},{10,... | collective-permute-start | bytes 12296 | tf_op jit(solution)/shard_map/ppermute | solution.py:464
  10.4 0.0 copy-start.1
  10.4 3.5 %shard_map.38.d_in = f32[4,5,2,2,8,128]{5,4,3,2,1,0:T(8,128)S(1)} custom-call(f32[4,5,2,2,8,128]{5,4,3,2,1,0:T(8,128)S(1)} %get-tuple-element.19.w), custom_call_target="tpu_custom_call" | custom-call | tf_op jit(solution)/shard_map/pallas_call | solution.py:437
  13.9 0.0 collective-permute-done.4.top2
  13.9 0.0 collective-permute-done.re_bx
  13.9 0.0 collective-permute-done.1.ro_bx
  13.9 0.0 collective-permute-done.2.re_by
  14.0 0.0 collective-permute-done.3.ro_by
  14.0 0.0 copy-done.1
  14.0 1.8 %shard_map.39 = (f32[4,5,2,2,8,128]{5,4,3,2,1,0:T(8,128)S(1)}, f32[2,5,2,2,8,128]{5,4,3,2,1,0:T(8,128)S(1)}, f32[2,5,2,2,8,128]{5,4,3,2,1,0:T(8,128)S(1)}, f32[32,8,128]{2,1,0:T(8,128)}) custom-call(s32[3,8,32]{2,1,0:T(8,128)S(1)} %bitcast.8, f32[4,5,2,2,8,128]{5,4,3,2,1,0:T(8,128)S(1)} %get-tuple-element.18.u, f32[4,5,2,2,8,128]{5,4,3,2,1,0:T(8,128)S(1)} %shard_map.38.d_in, ...), custom_call_target="tpu_custom_call" | custom-call | tf_op jit(solution)/shard_map/pallas_call | solution.py:437
  15.8 1.5 %collective-permute-start.6 = (f32[2,5,2,2,8,128]{5,4,3,2,1,0:T(8,128)S(1)}, f32[2,5,2,2,8,128]{5,4,3,2,1,0:T(8,128)S(1)}, u32[]{:S(2)}, u32[]{:S(2)}) collective-permute-start(f32[2,5,2,2,8,128]{5,4,3,2,1,0:T(8,128)S(1)} %get-tuple-element.30), channel_id=1, source_target_pairs={{0,2},{1,3},{2,0},{3,1},{4,6},{5,7},{6,4},{7,5},{8,10},{9,11},{10,... | collective-permute-start | bytes 491528 | tf_op jit(solution)/shard_map/ppermute | solution.py:478
  17.4 5.4 %collective-permute-start.7 = (f32[2,5,2,2,8,128]{5,4,3,2,1,0:T(8,128)S(1)}, f32[2,5,2,2,8,128]{5,4,3,2,1,0:T(8,128)S(1)}, u32[]{:S(2)}, u32[]{:S(2)}) collective-permute-start(f32[2,5,2,2,8,128]{5,4,3,2,1,0:T(8,128)S(1)} %get-tuple-element.29), channel_id=1, source_target_pairs={{0,3},{1,2},{2,1},{3,0},{4,7},{5,6},{6,5},{7,4},{8,11},{9,10},{10,... | collective-permute-start | bytes 491528 | tf_op jit(solution)/shard_map/ppermute | solution.py:478
  22.8 0.5 %collective-permute-start.5 = (f32[2,5,2,2,8,128]{5,4,3,2,1,0:T(8,128)S(1)}, f32[2,5,2,2,8,128]{5,4,3,2,1,0:T(8,128)S(1)}, u32[]{:S(2)}, u32[]{:S(2)}) collective-permute-start(f32[2,5,2,2,8,128]{5,4,3,2,1,0:T(8,128)S(1)} %get-tuple-element.29), channel_id=1, source_target_pairs={{0,1},{1,0},{2,3},{3,2},{4,5},{5,4},{6,7},{7,6},{8,9},{9,8},{10,11... | collective-permute-start | bytes 491528 | tf_op jit(solution)/shard_map/ppermute | solution.py:478
  23.3 6.0 %all-to-all-start = ((f32[64,4,128]{2,1,0:T(4,128)}), f32[64,4,128]{2,1,0:T(4,128)S(1)}, u32[]{:S(2)}, u32[]{:S(2)}) async-start(f32[64,4,128]{2,1,0:T(4,128)} %bitcast.3), calls=%async_computation | async-start | bytes 262144 | tf_op jit(solution)/shard_map/all_to_all | solution.py:481
  29.3 0.0 collective-permute-done.6.got2
  29.3 0.0 collective-permute-done.7.got3
  29.3 0.0 collective-permute-done.5.got1
  29.3 0.0 copy-start.2
  29.3 0.8 %shard_map.40 = f32[2,5,2,2,8,128]{5,4,3,2,1,0:T(8,128)S(1)} custom-call(s32[3,8,32]{2,1,0:T(8,128)S(1)} %bitcast.9, f32[4,5,2,2,8,128]{5,4,3,2,1,0:T(8,128)S(1)} %get-tuple-element.18.u, f32[4,5,2,2,8,128]{5,4,3,2,1,0:T(8,128)S(1)} %get-tuple-element.27.d, f32[2,5,2,2,8,128]{5,4,3,2,1,0:T(8,128)S(1)} %collective-permute-done.5.got1, ...), custom_call_target="tpu_custom_call" | custom-call | tf_op jit(solution)/shard_map/pallas_call | solution.py:437
  30.1 1.7 %collective-permute-start.8 = (f32[2,5,2,2,8,128]{5,4,3,2,1,0:T(8,128)S(1)}, f32[2,5,2,2,8,128]{5,4,3,2,1,0:T(8,128)S(1)}, u32[]{:S(2)}, u32[]{:S(2)}) collective-permute-start(f32[2,5,2,2,8,128]{5,4,3,2,1,0:T(8,128)S(1)} %shard_map.40), channel_id=1, source_target_pairs={{0,4},{1,5},{2,6},{3,7},{4,0},{5,1},{6,2},{7,3},{8,12},{9,13},{10,... | collective-permute-start | bytes 491528 | tf_op jit(solution)/shard_map/ppermute | solution.py:478
  31.8 8.7 %all-to-all-done = f32[64,4,128]{2,1,0:T(4,128)S(1)} async-done(((f32[64,4,128]{2,1,0:T(4,128)}), f32[64,4,128]{2,1,0:T(4,128)S(1)}, u32[]{:S(2)}, u32[]{:S(2)}) %all-to-all-start) | async-done | bytes 131104 | tf_op jit(solution)/shard_map/all_to_all | solution.py:481
  40.5 0.0 collective-permute-done.8.got4
  40.5 0.0 copy-done.2
  40.5 2.6 %shard_map.41 = f32[4,5,16,256]{3,2,1,0:T(8,128)} custom-call(s32[3,8,32]{2,1,0:T(8,128)S(1)} %bitcast.10, s32[8,4,32]{2,1,0:T(4,128)S(1)} %bitcast.11, f32[4,5,2,2,8,128]{5,4,3,2,1,0:T(8,128)S(1)} %get-tuple-element.18.u, f32[4,5,2,2,8,128]{5,4,3,2,1,0:T(8,128)S(1)} %get-tuple-element.27.d, f32[32,8,128]{2,1,0:T(8,128)S(1)} %bitcast.7, ...), custom_call_target="tpu_custom_call" | custom-call | tf_op jit(solution)/shard_map/pallas_call | solution.py:437
Async XLA Ops:
  0.0 1.1 %copy-start = (f32[5,16,16,64]{3,2,1,0:T(8,128)S(1)}, f32[5,16,16,64]{3,2,1,0:T(8,128)}, u32[]{:S(2)}) copy-start(f32[5,16,16,64]{3,2,1,0:T(8,128)} %param.3) | copy-start | bytes 983044
  1.7 12.2 %collective-permute-start.2 = (f32[11,8,128]{2,1,0:T(8,128)S(1)}, f32[11,8,128]{2,1,0:T(8,128)S(1)}, u32[]{:S(2)}, u32[]{:S(2)}) collective-permute-start(f32[11,8,128]{2,1,0:T(8,128)S(1)} %get-tuple-element.22.se_by), channel_id=1, source_target_pairs={{0,1},{1,0},{2,3},{3,2},{4,5},{5,4},{6,7},{7,6},{8,9},{9,8},{10,11... | collective-permute-start | bytes 135176 | tf_op jit(solution)/shard_map/ppermute | solution.py:462
  4.1 9.9 %collective-permute-start.3 = (f32[11,8,128]{2,1,0:T(8,128)S(1)}, f32[11,8,128]{2,1,0:T(8,128)S(1)}, u32[]{:S(2)}, u32[]{:S(2)}) collective-permute-start(f32[11,8,128]{2,1,0:T(8,128)S(1)} %get-tuple-element.23.so_by), channel_id=1, source_target_pairs={{0,31},{1,2},{2,1},{3,4},{4,3},{5,6},{6,5},{7,8},{8,7},{9,10},{10,... | collective-permute-start | bytes 135176 | tf_op jit(solution)/shard_map/ppermute | solution.py:463
  4.5 9.4 %collective-permute-start = (f32[10,8,128]{2,1,0:T(8,128)S(1)}, f32[10,8,128]{2,1,0:T(8,128)S(1)}, u32[]{:S(2)}, u32[]{:S(2)}) collective-permute-start(f32[10,8,128]{2,1,0:T(8,128)S(1)} %get-tuple-element.20.se_bx), channel_id=1, source_target_pairs={{0,32},{32,0},{64,96},{96,64},{128,160},{160,128},{192,224},{224,1... | collective-permute-start | bytes 122888 | tf_op jit(solution)/shard_map/ppermute | solution.py:460
  4.5 9.4 %collective-permute-start.1 = (f32[10,8,128]{2,1,0:T(8,128)S(1)}, f32[10,8,128]{2,1,0:T(8,128)S(1)}, u32[]{:S(2)}, u32[]{:S(2)}) collective-permute-start(f32[10,8,128]{2,1,0:T(8,128)S(1)} %get-tuple-element.21.so_bx), channel_id=1, source_target_pairs={{0,224},{32,64},{64,32},{96,128},{128,96},{160,192},{192,160},{224... | collective-permute-start | bytes 122888 | tf_op jit(solution)/shard_map/ppermute | solution.py:461
  7.6 6.3 %collective-permute-start.4 = (f32[8,128]{1,0:T(8,128)S(1)}, f32[8,128]{1,0:T(8,128)S(1)}, u32[]{:S(2)}, u32[]{:S(2)}) collective-permute-start(f32[8,128]{1,0:T(8,128)S(1)} %get-tuple-element.26.top), channel_id=1, source_target_pairs={{0,2},{1,3},{2,0},{3,1},{4,6},{5,7},{6,4},{7,5},{8,10},{9,11},{10,... | collective-permute-start | bytes 12296 | tf_op jit(solution)/shard_map/ppermute | solution.py:464
  10.4 3.6 %copy-start.1 = (s32[8,32,3]{1,0,2:T(8,128)S(1)}, s32[8,32,3]{1,0,2:T(8,128)}, u32[]{:S(2)}) copy-start(s32[8,32,3]{1,0,2:T(8,128)} %param.5) | copy-start | bytes 9220
  15.8 13.5 %collective-permute-start.6 = (f32[2,5,2,2,8,128]{5,4,3,2,1,0:T(8,128)S(1)}, f32[2,5,2,2,8,128]{5,4,3,2,1,0:T(8,128)S(1)}, u32[]{:S(2)}, u32[]{:S(2)}) collective-permute-start(f32[2,5,2,2,8,128]{5,4,3,2,1,0:T(8,128)S(1)} %get-tuple-element.30), channel_id=1, source_target_pairs={{0,2},{1,3},{2,0},{3,1},{4,6},{5,7},{6,4},{7,5},{8,10},{9,11},{10,... | collective-permute-start | bytes 491528 | tf_op jit(solution)/shard_map/ppermute | solution.py:478
  17.4 11.9 %collective-permute-start.7 = (f32[2,5,2,2,8,128]{5,4,3,2,1,0:T(8,128)S(1)}, f32[2,5,2,2,8,128]{5,4,3,2,1,0:T(8,128)S(1)}, u32[]{:S(2)}, u32[]{:S(2)}) collective-permute-start(f32[2,5,2,2,8,128]{5,4,3,2,1,0:T(8,128)S(1)} %get-tuple-element.29), channel_id=1, source_target_pairs={{0,3},{1,2},{2,1},{3,0},{4,7},{5,6},{6,5},{7,4},{8,11},{9,10},{10,... | collective-permute-start | bytes 491528 | tf_op jit(solution)/shard_map/ppermute | solution.py:478
  22.8 6.5 %collective-permute-start.5 = (f32[2,5,2,2,8,128]{5,4,3,2,1,0:T(8,128)S(1)}, f32[2,5,2,2,8,128]{5,4,3,2,1,0:T(8,128)S(1)}, u32[]{:S(2)}, u32[]{:S(2)}) collective-permute-start(f32[2,5,2,2,8,128]{5,4,3,2,1,0:T(8,128)S(1)} %get-tuple-element.29), channel_id=1, source_target_pairs={{0,1},{1,0},{2,3},{3,2},{4,5},{5,4},{6,7},{7,6},{8,9},{9,8},{10,11... | collective-permute-start | bytes 491528 | tf_op jit(solution)/shard_map/ppermute | solution.py:478
  23.3 17.2 %all-to-all-start = ((f32[64,4,128]{2,1,0:T(4,128)}), f32[64,4,128]{2,1,0:T(4,128)S(1)}, u32[]{:S(2)}, u32[]{:S(2)}) async-start(f32[64,4,128]{2,1,0:T(4,128)} %bitcast.3), calls=%async_computation | async-start | bytes 262144 | tf_op jit(solution)/shard_map/all_to_all | solution.py:481
  29.3 11.2 %copy-start.2 = (s32[8,32,4]{1,2,0:T(4,128)S(1)}, s32[8,32,4]{1,2,0:T(4,128)}, u32[]{:S(2)}) copy-start(s32[8,32,4]{1,2,0:T(4,128)} %param.4) | copy-start | bytes 12292
  30.1 10.4 %collective-permute-start.8 = (f32[2,5,2,2,8,128]{5,4,3,2,1,0:T(8,128)S(1)}, f32[2,5,2,2,8,128]{5,4,3,2,1,0:T(8,128)S(1)}, u32[]{:S(2)}, u32[]{:S(2)}) collective-permute-start(f32[2,5,2,2,8,128]{5,4,3,2,1,0:T(8,128)S(1)} %shard_map.40), channel_id=1, source_target_pairs={{0,4},{1,5},{2,6},{3,7},{4,0},{5,1},{6,2},{7,3},{8,12},{9,13},{10,... | collective-permute-start | bytes 491528 | tf_op jit(solution)/shard_map/ppermute | solution.py:478

commit v4 on v3

--- a/solution.py
+++ b/solution.py
@@ -13,8 +13,9 @@
 BLOCKS = (4, 5, 2, 2) + TILE
 TRAVEL = (2, 5, 2, 2) + TILE
 VMEM = pl.BlockSpec(memory_space=pltpu.VMEM)
-SMEM = pl.BlockSpec(memory_space=pltpu.SMEM)
+ANY = pl.BlockSpec(memory_space=pl.ANY)
 PARAMS = pltpu.CompilerParams(vmem_limit_bytes=16 * 1024 * 1024)
+PLAN = jax.ShapeDtypeStruct((16, 128), jnp.int32)
 BIG = 3e38
 SMALL = 1e-37
 
@@ -28,17 +29,15 @@
 
 
 def invert(x):
-    r = pl.reciprocal(x, approx=True)
-    return r * (2.0 - x * r)
+    return pl.reciprocal(x, approx=True)
 
 
 def root(x):
-    x = jnp.maximum(x, SMALL)
-    return x * lax.rsqrt(x)
+    return x * lax.rsqrt(jnp.maximum(x, SMALL))
 
 
 def half_minmod(a, b):
-    return 0.5 * (jnp.maximum(jnp.minimum(a, b), 0.0) + jnp.minimum(jnp.maximum(a, b), 0.0))
+    return 0.5 * jnp.maximum(jnp.minimum(a, b), jnp.minimum(jnp.maximum(a, b), 0.0))
 
 
 def primitive(u):
@@ -58,7 +57,7 @@
     ml = rl * (sl - ul)
     mr = rr * (sr - ur)
     mid = (pr - pl_ + ml * ul - mr * ur) * invert(ml - mr)
-    use_left = (sl >= 0.0) | (mid >= 0.0)
+    use_left = jnp.maximum(sl, mid) >= 0.0
     rho, v1, v2, v3, p = [jnp.where(use_left, a, b) for a, b in zip(left, right)]
     edge = jnp.where(use_left, sl, sr)
     clip = jnp.where(use_left, jnp.minimum(sl, 0.0), jnp.maximum(sr, 0.0))
@@ -76,7 +75,9 @@
     return out
 
 
-def prep_kernel(cons, u_out, w_out, e_bx, o_bx, e_by, o_by, in_bx, in_by, top_out):
+def prep_kernel(
+    cons, u_out, w_out, e_bx, o_bx, e_by, o_by, in_bx, in_by, top_out
+):
     even_i = lax.axis_index("bx") % 2 == 0
     even_j = lax.axis_index("by") % 2 == 0
     lane = iota(1)
@@ -146,7 +147,65 @@
     top_out[...] = top
 
 
-def inner_kernel(w, d, lefts, rights, fluxes):
+def make_plan(slots, counts, plan):
+    i, j = lax.axis_index("bx"), lax.axis_index("by")
+    row = iota(0)
+    here = lax.broadcasted_iota(jnp.int32, (8, 32), 1) == jnp.bitwise_xor(
+        lax.broadcasted_iota(jnp.int32, (8, 32), 0), j
+    )
+
+    def columns(line):
+        line = jnp.broadcast_to(line.astype(F32), (8, 32))
+        value = jnp.sum(jnp.where(here, line, 0.0), axis=1, keepdims=True)
+        return jnp.broadcast_to(value, TILE)
+
+    def across(a, mask):
+        for bit in (1, 2, 4):
+            if mask & bit:
+                a = jnp.where(row & bit == 0, pltpu.roll(a, 8 - bit, 0), pltpu.roll(a, bit, 0))
+        return a
+
+    give = [columns(slots[r, pl.ds(i, 1), :]) for r in range(3)]
+    loads = [columns(counts[i, pl.ds(k, 1), :]) for k in range(4)]
+    through = across(give[1], 2) == across(give[0], 2)
+    from_one, from_two, from_three = across(give[0], 1), across(give[1], 2), across(give[0], 3)
+
+    def content(slot):
+        second, first = slot == give[1], slot == give[0]
+        mask = jnp.where(second, jnp.where(through, 3.0, 2.0), jnp.where(first, 1.0, 0.0))
+        index = jnp.where(
+            second,
+            jnp.where(through, from_three, from_two),
+            jnp.where(first, from_one, slot),
+        )
+        return mask, index
+
+    relay_mask, relay_index = content(give[2])
+    entries = [give[0], give[1], relay_mask, relay_index]
+    far_mask, far_index = across(relay_mask, 4) + 4.0, across(relay_index, 4)
+    for slot in range(4):
+        is_last = give[2] == float(slot)
+        mask, index = content(jnp.full(TILE, slot, F32))
+        source = jnp.where(is_last, far_mask, mask)
+        index = jnp.where(is_last, far_index, index)
+        source0 = jnp.broadcast_to(source[0:1], TILE)
+        index0 = jnp.broadcast_to(index[0:1], TILE)
+        count = jnp.zeros(TILE, F32)
+        for k in range(4):
+            hit = (row.astype(F32) == source0) & (index0 == float(k))
+            count += jnp.where(hit, loads[k], 0.0)
+        count = jnp.sum(count, axis=0, keepdims=True)
+        entries += [jnp.where(is_last, 4.0, mask), index, count]
+    for e, value in enumerate(entries):
+        plan[pl.ds(e, 1), :] = value[0:1].astype(jnp.int32)
+
+
+def entry(plan, e):
+    return plan[pl.ds(e, 1), :][0, 0]
+
+
+def inner_kernel(slots, counts, w, d, plan, lefts, rights, fluxes):
+    make_plan(slots, counts, plan)
     row, lane = iota(0), iota(1)
 
     def sweep(n, load, down, up, first, last, no_first, no_last):
@@ -250,12 +309,12 @@
         return 0
 
     for body in (along_first, along_second, third_states, third_fluxes, third_change):
-        lax.fori_loop(0, 8, body, 0, unroll=2)
+        lax.fori_loop(0, 8, body, 0, unroll=4)
 
 
 def edge_kernel(
-    slots, u, d_in, se_bx, so_bx, se_by, so_by, in_bx, in_by, top, re_bx, ro_bx, re_by, ro_by, top2,
-    d, send_a, send_b, top_out,
+    plan, u, d_in, se_bx, so_bx, se_by, so_by, in_bx, in_by, top, re_bx, ro_bx, re_by, ro_by, top2,
+    d, send_a, send_b, top_out, spread, sent,
 ):
     i, j = lax.axis_index("bx"), lax.axis_index("by")
     even_i, even_j = i % 2 == 0, j % 2 == 0
@@ -263,8 +322,10 @@
 
     top = jnp.maximum(jnp.maximum(top[...], top2[...]), jnp.maximum(re_by[10], ro_by[10]))
     top = jnp.broadcast_to(jnp.max(top, axis=0, keepdims=True), TILE)
-    for k in range(top_out.shape[0]):
-        top_out[k] = top
+    for k in range(spread.shape[0]):
+        spread[k] = top
+    copy = pltpu.make_async_copy(spread, top_out, sent)
+    copy.start()
 
     def faces(n, own_low, own_high, low, high, inner, back, ahead, zero):
         left, right, left2, right2 = [], [], [], []
@@ -325,28 +386,14 @@
                 d[s, f, at, 1] += jnp.where(lane >= 112, two, jnp.where(lane >= 96, one, 0.0))
 
     for r, ref in enumerate((send_a, send_b)):
-        slot = slots[r, i, j]
+        slot = entry(plan, r)
         ref[0] = u[slot]
         ref[1] = d[slot]
-
-
-def content(slots, i, j, slot):
-    sw = lambda m, r: slots[r, i, j ^ m]
-    second = slot == sw(0, 1)
-    through = sw(2, 1) == sw(2, 0)
-    first = slot == sw(0, 0)
-    mask = jnp.where(second, jnp.where(through, 3, 2), jnp.where(first, 1, 0))
-    index = jnp.where(
-        second,
-        jnp.where(through, sw(3, 0), sw(2, 1)),
-        jnp.where(first, sw(1, 0), slot),
-    )
-    return mask, index
-
-
-def relay_kernel(slots, u, d, got1, got2, got3, send):
-    i, j = lax.axis_index("bx"), lax.axis_index("by")
-    mask, index = content(slots, i, j, slots[2, i, j])
+    copy.wait()
+
+
+def relay_kernel(plan, u, d, got1, got2, got3, send):
+    mask, index = entry(plan, 2), entry(plan, 3)
 
     @pl.when(mask == 0)
     def _():
@@ -361,36 +408,20 @@
 
 
 def tail_kernel(
-    slots, counts, u, d, top, got1, got2, got3, got4, out, stage, energy, factor, tick
+    plan, u, d, top, got1, got2, got3, got4, result, out, energy, factor, tick, sent, last
 ):
-    i, j = lax.axis_index("bx"), lax.axis_index("by")
-    speed = jnp.max(jnp.max(jnp.max(top[...], axis=0), axis=0, keepdims=True), axis=1, keepdims=True)
+    speed = jnp.max(jnp.max(top[...], axis=0), axis=0, keepdims=True)
+    speed = jnp.max(speed, axis=1, keepdims=True)
     step = COURANT_FACTOR / jnp.broadcast_to(speed, TILE)
-
-    def count_of(slot):
-        is_last = slots[2, i, j] == slot
-        column = jnp.where(is_last, j ^ 4, j)
-        mask, index = content(slots, i, column, jnp.where(is_last, slots[2, i, j ^ 4], slot))
-        return jnp.where(is_last, 4, mask), index, counts[i, index, column ^ mask]
+    tiles = [(at, h) for at in range(2) for h in range(2)]
 
     def load(slot, _):
-        mask, index, count = count_of(slot)
-
-        @pl.when(mask == 0)
-        def _():
-            stage[0] = u[index]
-            stage[1] = d[index]
-
-        for m, ref in enumerate((got1, got2, got3, got4), 1):
-
-            @pl.when(mask == m)
-            def _():
-                stage[...] = ref[...]
-
+        mask, index, count = [entry(plan, 4 + 3 * slot + k) for k in range(3)]
         chill = step / count.astype(F32)
-        for at in range(2):
-            for h in range(2):
-                new = [stage[0, f, at, h] - step * stage[1, f, at, h] for f in range(5)]
+
+        def update(u_of, d_of):
+            for at, h in tiles:
+                new = [u_of(f, at, h) - step * d_of(f, at, h) for f in range(5)]
                 inverse = invert(new[0])
                 squares = new[1] * new[1] + new[2] * new[2] + new[3] * new[3]
                 kinetic = 0.5 * squares * inverse
@@ -400,29 +431,48 @@
                 new[4] = kinetic
                 for f in range(5):
                     out[slot, f, pl.ds(8 * at, 8), pl.ds(128 * h, 128)] = new[f]
+
+        @pl.when(mask == 0)
+        def _():
+            update(lambda f, at, h: u[index, f, at, h], lambda f, at, h: d[index, f, at, h])
+
+        for m, ref in enumerate((got1, got2, got3, got4), 1):
+
+            @pl.when(mask == m)
+            def _():
+                update(lambda f, at, h: ref[0, f, at, h], lambda f, at, h: ref[1, f, at, h])
+
+        place = (slot, pl.ds(0, 4))
+        pltpu.make_async_copy(out.at[place], result.at[place], sent.at[slot]).start()
         return 0
 
     lax.fori_loop(0, 4, load, 0)
-    limits = [count_of(slot)[2] for slot in range(4)]
+    limits = [entry(plan, 6 + 3 * slot) for slot in range(4)]
     most = jnp.maximum(jnp.maximum(limits[0], limits[1]), jnp.maximum(limits[2], limits[3]))
-
-    def advance(k, _):
-        for slot in range(4):
-            for at in range(2):
-                for h in range(2):
-                    now = energy[slot, at, h]
-                    heat = now * factor[slot, at, h]
-                    loss = tick[slot, at, h] * root(jnp.minimum(1.0 + heat * heat, BIG))
-                    new = now * invert(jnp.minimum(1.0 + loss, BIG))
-                    energy[slot, at, h] = jnp.where(k < limits[slot], new, now)
-        return 0
-
-    lax.fori_loop(0, most, advance, 0)
+    places = [(slot, at, h) for slot in range(4) for at, h in tiles]
+
+    def advance(k, state):
+        after = []
+        for now, place in zip(state, places):
+            heat = now * factor[place]
+            loss = tick[place] * root(jnp.minimum(1.0 + heat * heat, BIG))
+            new = now * invert(jnp.minimum(1.0 + loss, BIG))
+            after.append(jnp.where(k < limits[place[0]], new, now))
+        return tuple(after)
+
+    state = lax.fori_loop(0, most, advance, tuple(energy[place] for place in places))
+    for left, (slot, at, h) in zip(state, places):
+        place = (slot, 4, pl.ds(8 * at, 8), pl.ds(128 * h, 128))
+        out[place] = out[place] + left
+    copies = []
     for slot in range(4):
-        for at in range(2):
-            for h in range(2):
-                place = (slot, 4, pl.ds(8 * at, 8), pl.ds(128 * h, 128))
-                out[place] = out[place] + energy[slot, at, h]
+        place = (slot, pl.ds(4, 1))
+        copies.append(pltpu.make_async_copy(out.at[place], result.at[place], last.at[slot]))
+        copies[-1].start()
+    for slot in range(4):
+        place = (slot, pl.ds(0, 4))
+        pltpu.make_async_copy(out.at[place], result.at[place], sent.at[slot]).wait()
+        copies[slot].wait()
 
 
 def pair_even(count):
@@ -433,13 +483,13 @@
     return [(k, (k + 1) % count if k % 2 else (k - 1) % count) for k in range(count)]
 
 
-def call(kernel, inputs, outputs, scratch=(), smem=0):
+def call(kernel, inputs, outputs, scratch=(), hbm_out=0, plan=0):
     return pl.pallas_call(
         kernel,
-        in_specs=[SMEM] * smem + [VMEM] * (len(inputs) - smem),
-        out_specs=[VMEM] * len(outputs),
-        out_shape=[shape(*dims) for dims in outputs],
-        scratch_shapes=[pltpu.VMEM(dims, F32) for dims in scratch],
+        in_specs=[VMEM] * len(inputs),
+        out_specs=[VMEM] * (len(outputs) - hbm_out) + [ANY] * hbm_out + [VMEM] * plan,
+        out_shape=[shape(*dims) for dims in outputs] + [PLAN] * plan,
+        scratch_shapes=[pltpu.VMEM(x, F32) if isinstance(x, tuple) else x for x in scratch],
         compiler_params=PARAMS,
     )(*inputs)
 
@@ -463,16 +513,17 @@
         lax.ppermute(o_by, "by", pair_odd(columns)),
         lax.ppermute(slabs[-1], "by", [(k, k ^ 2) for k in range(columns)]),
     ]
-    (d,) = call(inner_kernel, [w], [BLOCKS], [BLOCKS] * 3)
+    d, plan = call(inner_kernel, [slots, counts, w], [BLOCKS], [BLOCKS] * 3, plan=1)
     groups = [
         [i * columns + j for i in range(rows) for j in range(x, columns, 4)] for x in range(4)
     ]
     size = len(groups[0])
     d, send_a, send_b, top = call(
         edge_kernel,
-        [slots, u, d, *slabs, *got_slabs],
+        [plan, u, d, *slabs, *got_slabs],
         [BLOCKS] + [TRAVEL] * 2 + [(size // 2,) + TILE],
-        smem=1,
+        [(size // 2,) + TILE, pltpu.SemaphoreType.DMA],
+        hbm_out=1,
     )
     sends = {1: send_a, 2: send_b, 3: send_a}
     trade = lambda m, block: lax.ppermute(block, "by", [(k, k ^ m) for k in range(columns)])
@@ -480,14 +531,14 @@
     top = top.reshape(size, 4, 128)
     top = lax.all_to_all(top, ("bx", "by"), 0, 0, axis_index_groups=groups)
     top = top.reshape((size // 2,) + TILE)
-    (send_c,) = call(relay_kernel, [slots, u, d, *got], [TRAVEL], smem=1)
+    (send_c,) = call(relay_kernel, [plan, u, d, *got], [TRAVEL])
     got.append(trade(4, send_c))
     (result,) = call(
         tail_kernel,
-        [slots, counts, u, d, top, *got],
+        [plan, u, d, top, *got],
         [(4, 5, 16, 256)],
-        [TRAVEL] + [(4, 2, 2) + TILE] * 3,
-        smem=2,
+        [(4, 5, 16, 256)] + [(4, 2, 2) + TILE] * 3 + [pltpu.SemaphoreType.DMA((4,))] * 2,
+        hbm_out=1,
     )
     return result.reshape((1, 1) + result.shape)
 

time: 43.1 us -> 41 us (0.951)
  Pallas kernels: 9.34 us -> 5.66 us
  starting transfers between devices: 23.8 us -> 24.6 us
  waiting for transfers between devices: 8.73 us -> 9.46 us
    pallas_call x5, Pallas kernels: 9.34 us -> 5.66 us  [call(): pl.pallas_call(kernel, in_specs=[VMEM] * len(inputs), out_specs=[VMEM] *...]
    all_to_all x1, waiting for transfers between devices: 8.7 us -> 9.43 us  [on_device(): top = lax.all_to_all(top, ('bx', 'by'), 0, 0, axis_index_groups=groups)]
    ppermute x4, starting transfers between devices: 9.16 us -> 9.79 us  [on_device(): lax.ppermute(block, 'by', [(k, k ^ m) for k in range(columns)])]
  transfers between devices with their start and end apart: 10 -> 10, of which waited for: 1 -> 1; matrix products, arithmetic and copies ran while one was open for 0% -> 0% of each run, Pallas kernels for 10% -> 6%
where the time goes in v4:
time: 41 us
  starting transfers between devices  24.6 us (60%)
  waiting for transfers between devices  9.46 us (23%)
  Pallas kernels  5.66 us (14%)
  local copies, waits for them, and re-layouts  1.1 us (3%)
    ppermute x4, starting transfers between devices, on_device(): lax.ppermute(block, 'by', [(k, k ^ m) for k in range(columns)])  9.79 us
    all_to_all x1, waiting for transfers between devices, on_device(): top = lax.all_to_all(top, ('bx', 'by'), 0, 0, axis_index_groups=groups)  9.43 us
    all_to_all x1, starting transfers between devices, on_device(): top = lax.all_to_all(top, ('bx', 'by'), 0, 0, axis_index_groups=groups)  6.16 us
    pallas_call x5, Pallas kernels, call(): pl.pallas_call(kernel, in_specs=[VMEM] * len(inputs), out_specs=[VMEM] *...  5.66 us
    ppermute x1, starting transfers between devices, on_device(): lax.ppermute(o_bx, 'bx', pair_odd(rows))  3.13 us
    ppermute x1, starting transfers between devices, on_device(): lax.ppermute(slabs[-1], 'by', [(k, k ^ 2) for k in range(columns)])  2.76 us
    ppermute x1, starting transfers between devices, on_device(): lax.ppermute(e_by, 'by', pair_even(columns))  2.36 us
    unnamed x6, local copies, waits for them, and re-layouts  1.1 us
  transfers between devices with their start and end apart: 10, of which 1 were waited for; matrix products, arithmetic and copies ran while one was open for 0% of the time, Pallas kernels for 6%

profile of v4, /device:TPU:2, one launch (start us, length us, event | category | flops | bytes accessed | tf_op | source)
XLA Modules:
  0.0 41.0 jit_solution(17295817825391944037)
XLA Ops:
  0.0 0.0 copy-start
  0.0 1.1 %copy-done = f32[5,16,16,64]{3,2,1,0:T(8,128)S(1)} copy-done((f32[5,16,16,64]{3,2,1,0:T(8,128)S(1)}, f32[5,16,16,64]{3,2,1,0:T(8,128)}, u32[]{:S(2)}) %copy-start) | copy-done | bytes 327704
  1.1 0.0 copy-start.1
  1.1 0.6 %shard_map.37 = (f32[4,5,2,2,8,128]{5,4,3,2,1,0:T(8,128)S(1)}, f32[4,5,2,2,8,128]{5,4,3,2,1,0:T(8,128)S(1)}, f32[10,8,128]{2,1,0:T(8,128)S(1)}, f32[10,8,128]{2,...) custom-call(f32[5,256,64]{2,1,0:T(8,128)S(1)} %bitcast.6), custom_call_target="tpu_custom_call" | custom-call | tf_op jit(solution)/shard_map/pallas_call | solution.py:487
  1.7 0.0 copy-start.2
  1.7 2.4 %collective-permute-start.2 = (f32[11,8,128]{2,1,0:T(8,128)S(1)}, f32[11,8,128]{2,1,0:T(8,128)S(1)}, u32[]{:S(2)}, u32[]{:S(2)}) collective-permute-start(f32[11,8,128]{2,1,0:T(8,128)S(1)} %get-tuple-element.26.se_by), channel_id=1, source_target_pairs={{0,1},{1,0},{2,3},{3,2},{4,5},{5,4},{6,7},{7,6},{8,9},{9,8},{10,11... | collective-permute-start | bytes 135176 | tf_op jit(solution)/shard_map/ppermute | solution.py:512
  4.1 0.4 %collective-permute-start.3 = (f32[11,8,128]{2,1,0:T(8,128)S(1)}, f32[11,8,128]{2,1,0:T(8,128)S(1)}, u32[]{:S(2)}, u32[]{:S(2)}) collective-permute-start(f32[11,8,128]{2,1,0:T(8,128)S(1)} %get-tuple-element.27.so_by), channel_id=1, source_target_pairs={{0,31},{1,2},{2,1},{3,4},{4,3},{5,6},{6,5},{7,8},{8,7},{9,10},{10,... | collective-permute-start | bytes 135176 | tf_op jit(solution)/shard_map/ppermute | solution.py:513
  4.5 0.0 collective-permute-start
  4.5 3.1 %collective-permute-start.1 = (f32[10,8,128]{2,1,0:T(8,128)S(1)}, f32[10,8,128]{2,1,0:T(8,128)S(1)}, u32[]{:S(2)}, u32[]{:S(2)}) collective-permute-start(f32[10,8,128]{2,1,0:T(8,128)S(1)} %get-tuple-element.25.so_bx), channel_id=1, source_target_pairs={{0,224},{32,64},{64,32},{96,128},{128,96},{160,192},{192,160},{224... | collective-permute-start | bytes 122888 | tf_op jit(solution)/shard_map/ppermute | solution.py:511
  7.6 2.8 %collective-permute-start.4 = (f32[8,128]{1,0:T(8,128)S(1)}, f32[8,128]{1,0:T(8,128)S(1)}, u32[]{:S(2)}, u32[]{:S(2)}) collective-permute-start(f32[8,128]{1,0:T(8,128)S(1)} %get-tuple-element.30.top), channel_id=1, source_target_pairs={{0,2},{1,3},{2,0},{3,1},{4,6},{5,7},{6,4},{7,5},{8,10},{9,11},{10,... | collective-permute-start | bytes 12296 | tf_op jit(solution)/shard_map/ppermute | solution.py:514
  10.4 0.0 copy-done.1
  10.4 0.0 copy-done.2
  10.4 2.5 %shard_map.38 = (f32[4,5,2,2,8,128]{5,4,3,2,1,0:T(8,128)S(1)}, s32[16,128]{1,0:T(8,128)S(1)}) custom-call(s32[3,8,32]{2,1,0:T(8,128)S(1)} %bitcast.9, s32[8,4,32]{2,1,0:T(4,128)S(1)} %bitcast.8, f32[4,5,2,2,8,128]{5,4,3,2,1,0:T(8,128)S(1)} %get-tuple-element.20.w), custom_call_target="tpu_custom_call" | custom-call | tf_op jit(solution)/shard_map/pallas_call | solution.py:487
  12.9 0.0 collective-permute-done.4.top2
  12.9 0.0 collective-permute-done.re_bx
  12.9 0.0 collective-permute-done.1.ro_bx
  12.9 0.0 collective-permute-done.2.re_by
  12.9 0.0 collective-permute-done.3.ro_by
  12.9 1.0 %shard_map.39 = (f32[4,5,2,2,8,128]{5,4,3,2,1,0:T(8,128)S(1)}, f32[2,5,2,2,8,128]{5,4,3,2,1,0:T(8,128)S(1)}, f32[2,5,2,2,8,128]{5,4,3,2,1,0:T(8,128)S(1)}, f32[32,8,128]{2,1,0:T(8,128)}) custom-call(s32[16,128]{1,0:T(8,128)S(1)} %get-tuple-element.21.plan, f32[4,5,2,2,8,128]{5,4,3,2,1,0:T(8,128)S(1)} %get-tuple-element.22.u, ...), custom_call_target="tpu_custom_call" | custom-call | tf_op jit(solution)/shard_map/pallas_call | solution.py:487
  13.9 2.7 %collective-permute-start.6 = (f32[2,5,2,2,8,128]{5,4,3,2,1,0:T(8,128)S(1)}, f32[2,5,2,2,8,128]{5,4,3,2,1,0:T(8,128)S(1)}, u32[]{:S(2)}, u32[]{:S(2)}) collective-permute-start(f32[2,5,2,2,8,128]{5,4,3,2,1,0:T(8,128)S(1)} %get-tuple-element.34), channel_id=1, source_target_pairs={{0,2},{1,3},{2,0},{3,1},{4,6},{5,7},{6,4},{7,5},{8,10},{9,11},{10,... | collective-permute-start | bytes 491528 | tf_op jit(solution)/shard_map/ppermute | solution.py:529
  16.6 5.4 %collective-permute-start.7 = (f32[2,5,2,2,8,128]{5,4,3,2,1,0:T(8,128)S(1)}, f32[2,5,2,2,8,128]{5,4,3,2,1,0:T(8,128)S(1)}, u32[]{:S(2)}, u32[]{:S(2)}) collective-permute-start(f32[2,5,2,2,8,128]{5,4,3,2,1,0:T(8,128)S(1)} %get-tuple-element.33), channel_id=1, source_target_pairs={{0,3},{1,2},{2,1},{3,0},{4,7},{5,6},{6,5},{7,4},{8,11},{9,10},{10,... | collective-permute-start | bytes 491528 | tf_op jit(solution)/shard_map/ppermute | solution.py:529
  22.1 0.0 collective-permute-start.5
  22.1 6.2 %all-to-all-start = ((f32[64,4,128]{2,1,0:T(4,128)}), f32[64,4,128]{2,1,0:T(4,128)S(1)}, u32[]{:S(2)}, u32[]{:S(2)}) async-start(f32[64,4,128]{2,1,0:T(4,128)} %bitcast.3), calls=%async_computation | async-start | bytes 262144 | tf_op jit(solution)/shard_map/all_to_all | solution.py:532
  28.2 0.0 collective-permute-done.6.got2
  28.3 0.0 collective-permute-done.7.got3
  28.3 0.0 collective-permute-done.5.got1
  28.3 0.1 shard_map.40
  28.3 1.7 %collective-permute-start.8 = (f32[2,5,2,2,8,128]{5,4,3,2,1,0:T(8,128)S(1)}, f32[2,5,2,2,8,128]{5,4,3,2,1,0:T(8,128)S(1)}, u32[]{:S(2)}, u32[]{:S(2)}) collective-permute-start(f32[2,5,2,2,8,128]{5,4,3,2,1,0:T(8,128)S(1)} %shard_map.40), channel_id=1, source_target_pairs={{0,4},{1,5},{2,6},{3,7},{4,0},{5,1},{6,2},{7,3},{8,12},{9,13},{10,... | collective-permute-start | bytes 491528 | tf_op jit(solution)/shard_map/ppermute | solution.py:529
  30.0 9.4 %all-to-all-done = f32[64,4,128]{2,1,0:T(4,128)S(1)} async-done(((f32[64,4,128]{2,1,0:T(4,128)}), f32[64,4,128]{2,1,0:T(4,128)S(1)}, u32[]{:S(2)}, u32[]{:S(2)}) %all-to-all-start) | async-done | bytes 131104 | tf_op jit(solution)/shard_map/all_to_all | solution.py:532
  39.4 0.0 collective-permute-done.8.got4
  39.4 1.5 %shard_map.41 = f32[4,5,16,256]{3,2,1,0:T(8,128)} custom-call(s32[16,128]{1,0:T(8,128)S(1)} %get-tuple-element.21.plan, f32[4,5,2,2,8,128]{5,4,3,2,1,0:T(8,128)S(1)} %get-tuple-element.22.u, f32[4,5,2,2,8,128]{5,4,3,2,1,0:T(8,128)S(1)} %get-tuple-element.31.d, f32[32,8,128]{2,1,0:T(8,128)S(1)} %bitcast.7, ...), custom_call_target="tpu_custom_call" | custom-call | tf_op jit(solution)/shard_map/pallas_call | solution.py:487
Async XLA Ops:
  0.0 1.1 %copy-start = (f32[5,16,16,64]{3,2,1,0:T(8,128)S(1)}, f32[5,16,16,64]{3,2,1,0:T(8,128)}, u32[]{:S(2)}) copy-start(f32[5,16,16,64]{3,2,1,0:T(8,128)} %param.3) | copy-start | bytes 983044
  1.1 9.3 %copy-start.1 = (s32[8,32,4]{1,2,0:T(4,128)S(1)}, s32[8,32,4]{1,2,0:T(4,128)}, u32[]{:S(2)}) copy-start(s32[8,32,4]{1,2,0:T(4,128)} %param.4) | copy-start | bytes 12292
  1.7 8.7 %copy-start.2 = (s32[8,32,3]{1,0,2:T(8,128)S(1)}, s32[8,32,3]{1,0,2:T(8,128)}, u32[]{:S(2)}) copy-start(s32[8,32,3]{1,0,2:T(8,128)} %param.5) | copy-start | bytes 9220
  1.7 11.2 %collective-permute-start.2 = (f32[11,8,128]{2,1,0:T(8,128)S(1)}, f32[11,8,128]{2,1,0:T(8,128)S(1)}, u32[]{:S(2)}, u32[]{:S(2)}) collective-permute-start(f32[11,8,128]{2,1,0:T(8,128)S(1)} %get-tuple-element.26.se_by), channel_id=1, source_target_pairs={{0,1},{1,0},{2,3},{3,2},{4,5},{5,4},{6,7},{7,6},{8,9},{9,8},{10,11... | collective-permute-start | bytes 135176 | tf_op jit(solution)/shard_map/ppermute | solution.py:512
  4.1 8.8 %collective-permute-start.3 = (f32[11,8,128]{2,1,0:T(8,128)S(1)}, f32[11,8,128]{2,1,0:T(8,128)S(1)}, u32[]{:S(2)}, u32[]{:S(2)}) collective-permute-start(f32[11,8,128]{2,1,0:T(8,128)S(1)} %get-tuple-element.27.so_by), channel_id=1, source_target_pairs={{0,31},{1,2},{2,1},{3,4},{4,3},{5,6},{6,5},{7,8},{8,7},{9,10},{10,... | collective-permute-start | bytes 135176 | tf_op jit(solution)/shard_map/ppermute | solution.py:513
  4.5 8.4 %collective-permute-start = (f32[10,8,128]{2,1,0:T(8,128)S(1)}, f32[10,8,128]{2,1,0:T(8,128)S(1)}, u32[]{:S(2)}, u32[]{:S(2)}) collective-permute-start(f32[10,8,128]{2,1,0:T(8,128)S(1)} %get-tuple-element.24.se_bx), channel_id=1, source_target_pairs={{0,32},{32,0},{64,96},{96,64},{128,160},{160,128},{192,224},{224,1... | collective-permute-start | bytes 122888 | tf_op jit(solution)/shard_map/ppermute | solution.py:510
  4.5 8.4 %collective-permute-start.1 = (f32[10,8,128]{2,1,0:T(8,128)S(1)}, f32[10,8,128]{2,1,0:T(8,128)S(1)}, u32[]{:S(2)}, u32[]{:S(2)}) collective-permute-start(f32[10,8,128]{2,1,0:T(8,128)S(1)} %get-tuple-element.25.so_bx), channel_id=1, source_target_pairs={{0,224},{32,64},{64,32},{96,128},{128,96},{160,192},{192,160},{224... | collective-permute-start | bytes 122888 | tf_op jit(solution)/shard_map/ppermute | solution.py:511
  7.6 5.2 %collective-permute-start.4 = (f32[8,128]{1,0:T(8,128)S(1)}, f32[8,128]{1,0:T(8,128)S(1)}, u32[]{:S(2)}, u32[]{:S(2)}) collective-permute-start(f32[8,128]{1,0:T(8,128)S(1)} %get-tuple-element.30.top), channel_id=1, source_target_pairs={{0,2},{1,3},{2,0},{3,1},{4,6},{5,7},{6,4},{7,5},{8,10},{9,11},{10,... | collective-permute-start | bytes 12296 | tf_op jit(solution)/shard_map/ppermute | solution.py:514
  13.9 14.3 %collective-permute-start.6 = (f32[2,5,2,2,8,128]{5,4,3,2,1,0:T(8,128)S(1)}, f32[2,5,2,2,8,128]{5,4,3,2,1,0:T(8,128)S(1)}, u32[]{:S(2)}, u32[]{:S(2)}) collective-permute-start(f32[2,5,2,2,8,128]{5,4,3,2,1,0:T(8,128)S(1)} %get-tuple-element.34), channel_id=1, source_target_pairs={{0,2},{1,3},{2,0},{3,1},{4,6},{5,7},{6,4},{7,5},{8,10},{9,11},{10,... | collective-permute-start | bytes 491528 | tf_op jit(solution)/shard_map/ppermute | solution.py:529
  16.6 11.6 %collective-permute-start.7 = (f32[2,5,2,2,8,128]{5,4,3,2,1,0:T(8,128)S(1)}, f32[2,5,2,2,8,128]{5,4,3,2,1,0:T(8,128)S(1)}, u32[]{:S(2)}, u32[]{:S(2)}) collective-permute-start(f32[2,5,2,2,8,128]{5,4,3,2,1,0:T(8,128)S(1)} %get-tuple-element.33), channel_id=1, source_target_pairs={{0,3},{1,2},{2,1},{3,0},{4,7},{5,6},{6,5},{7,4},{8,11},{9,10},{10,... | collective-permute-start | bytes 491528 | tf_op jit(solution)/shard_map/ppermute | solution.py:529
  22.1 6.2 %collective-permute-start.5 = (f32[2,5,2,2,8,128]{5,4,3,2,1,0:T(8,128)S(1)}, f32[2,5,2,2,8,128]{5,4,3,2,1,0:T(8,128)S(1)}, u32[]{:S(2)}, u32[]{:S(2)}) collective-permute-start(f32[2,5,2,2,8,128]{5,4,3,2,1,0:T(8,128)S(1)} %get-tuple-element.33), channel_id=1, source_target_pairs={{0,1},{1,0},{2,3},{3,2},{4,5},{5,4},{6,7},{7,6},{8,9},{9,8},{10,11... | collective-permute-start | bytes 491528 | tf_op jit(solution)/shard_map/ppermute | solution.py:529
  22.1 17.4 %all-to-all-start = ((f32[64,4,128]{2,1,0:T(4,128)}), f32[64,4,128]{2,1,0:T(4,128)S(1)}, u32[]{:S(2)}, u32[]{:S(2)}) async-start(f32[64,4,128]{2,1,0:T(4,128)} %bitcast.3), calls=%async_computation | async-start | bytes 262144 | tf_op jit(solution)/shard_map/all_to_all | solution.py:532
  28.3 11.1 %collective-permute-start.8 = (f32[2,5,2,2,8,128]{5,4,3,2,1,0:T(8,128)S(1)}, f32[2,5,2,2,8,128]{5,4,3,2,1,0:T(8,128)S(1)}, u32[]{:S(2)}, u32[]{:S(2)}) collective-permute-start(f32[2,5,2,2,8,128]{5,4,3,2,1,0:T(8,128)S(1)} %shard_map.40), channel_id=1, source_target_pairs={{0,4},{1,5},{2,6},{3,7},{4,0},{5,1},{6,2},{7,3},{8,12},{9,13},{10,... | collective-permute-start | bytes 491528 | tf_op jit(solution)/shard_map/ppermute | solution.py:529

commit v5 on v4

--- a/solution.py
+++ b/solution.py
@@ -1,3 +1,5 @@
+import functools
+
 import jax
 import jax.numpy as jnp
 from jax import lax
@@ -15,7 +17,7 @@
 VMEM = pl.BlockSpec(memory_space=pltpu.VMEM)
 ANY = pl.BlockSpec(memory_space=pl.ANY)
 PARAMS = pltpu.CompilerParams(vmem_limit_bytes=16 * 1024 * 1024)
-PLAN = jax.ShapeDtypeStruct((16, 128), jnp.int32)
+PLAN = jax.ShapeDtypeStruct((24, 128), jnp.int32)
 BIG = 3e38
 SMALL = 1e-37
 
@@ -144,7 +146,7 @@
             in_bx[f * 2 + h] = inner
     for ref in (e_by, o_by):
         ref[10] = top
-    top_out[...] = top
+    top_out[0] = top
 
 
 def make_plan(slots, counts, plan):
@@ -167,27 +169,24 @@
 
     give = [columns(slots[r, pl.ds(i, 1), :]) for r in range(3)]
     loads = [columns(counts[i, pl.ds(k, 1), :]) for k in range(4)]
-    through = across(give[1], 2) == across(give[0], 2)
-    from_one, from_two, from_three = across(give[0], 1), across(give[1], 2), across(give[0], 3)
-
-    def content(slot):
-        second, first = slot == give[1], slot == give[0]
-        mask = jnp.where(second, jnp.where(through, 3.0, 2.0), jnp.where(first, 1.0, 0.0))
-        index = jnp.where(
-            second,
-            jnp.where(through, from_three, from_two),
-            jnp.where(first, from_one, slot),
-        )
-        return mask, index
-
-    relay_mask, relay_index = content(give[2])
-    entries = [give[0], give[1], relay_mask, relay_index]
-    far_mask, far_index = across(relay_mask, 4) + 4.0, across(relay_index, 4)
+    def first_round(slot):
+        moved = slot == give[0]
+        return jnp.where(moved, 1.0, 0.0), jnp.where(moved, across(give[0], 1), slot)
+
+    one, two = first_round(give[1]), first_round(give[2])
+    same = give[2] == give[1]
+    entries = [give[0], *one, jnp.where(same, 2.0, two[0]), two[1]]
+    by_two = [across(one[0], 2) + 2.0, across(one[1], 2)]
+    third = [jnp.where(same, a, b) for a, b in zip(by_two, two)]
+    by_four = [across(third[0], 4) + 4.0, across(third[1], 4)]
     for slot in range(4):
-        is_last = give[2] == float(slot)
-        mask, index = content(jnp.full(TILE, slot, F32))
-        source = jnp.where(is_last, far_mask, mask)
-        index = jnp.where(is_last, far_index, index)
+        here_now = first_round(jnp.full(TILE, slot, F32))
+        is_second, is_last = give[1] == float(slot), give[2] == float(slot)
+        source, index = [
+            jnp.where(is_last, a, jnp.where(is_second, b, c))
+            for a, b, c in zip(by_four, by_two, here_now)
+        ]
+        code = jnp.where(is_last, 3.0, jnp.where(is_second, 2.0, here_now[0]))
         source0 = jnp.broadcast_to(source[0:1], TILE)
         index0 = jnp.broadcast_to(index[0:1], TILE)
         count = jnp.zeros(TILE, F32)
@@ -195,7 +194,7 @@
             hit = (row.astype(F32) == source0) & (index0 == float(k))
             count += jnp.where(hit, loads[k], 0.0)
         count = jnp.sum(count, axis=0, keepdims=True)
-        entries += [jnp.where(is_last, 4.0, mask), index, count]
+        entries += [code, index, count]
     for e, value in enumerate(entries):
         plan[pl.ds(e, 1), :] = value[0:1].astype(jnp.int32)
 
@@ -314,16 +313,16 @@
 
 def edge_kernel(
     plan, u, d_in, se_bx, so_bx, se_by, so_by, in_bx, in_by, top, re_bx, ro_bx, re_by, ro_by, top2,
-    d, send_a, send_b, top_out, spread, sent,
+    d, send, top_out, spread, sent,
 ):
     i, j = lax.axis_index("bx"), lax.axis_index("by")
     even_i, even_j = i % 2 == 0, j % 2 == 0
     row, lane = iota(0), iota(1)
 
-    top = jnp.maximum(jnp.maximum(top[...], top2[...]), jnp.maximum(re_by[10], ro_by[10]))
+    top = jnp.maximum(jnp.maximum(top[0], top2[0]), jnp.maximum(re_by[10], ro_by[10]))
     top = jnp.broadcast_to(jnp.max(top, axis=0, keepdims=True), TILE)
     for k in range(spread.shape[0]):
-        spread[k] = top
+        spread[k] = top[:6]
     copy = pltpu.make_async_copy(spread, top_out, sent)
     copy.start()
 
@@ -385,30 +384,30 @@
                 two = pltpu.roll(high[f], 48 - 16 * s, 1)
                 d[s, f, at, 1] += jnp.where(lane >= 112, two, jnp.where(lane >= 96, one, 0.0))
 
-    for r, ref in enumerate((send_a, send_b)):
-        slot = entry(plan, r)
-        ref[0] = u[slot]
-        ref[1] = d[slot]
+    slot = entry(plan, 0)
+    send[0] = u[slot]
+    send[1] = d[slot]
     copy.wait()
 
 
-def relay_kernel(plan, u, d, got1, got2, got3, send):
-    mask, index = entry(plan, 2), entry(plan, 3)
-
-    @pl.when(mask == 0)
+def relay_kernel(first, plan, u, d, *refs):
+    *got, send = refs
+    code, index = entry(plan, first), entry(plan, first + 1)
+
+    @pl.when(code == 0)
     def _():
         send[0] = u[index]
         send[1] = d[index]
 
-    for m, ref in enumerate((got1, got2, got3), 1):
-
-        @pl.when(mask == m)
+    for m, ref in enumerate(got, 1):
+
+        @pl.when(code == m)
         def _():
             send[...] = ref[...]
 
 
 def tail_kernel(
-    plan, u, d, top, got1, got2, got3, got4, result, out, energy, factor, tick, sent, last
+    plan, u, d, top, got1, got2, got4, result, out, energy, factor, tick, sent, last
 ):
     speed = jnp.max(jnp.max(top[...], axis=0), axis=0, keepdims=True)
     speed = jnp.max(speed, axis=1, keepdims=True)
@@ -416,7 +415,7 @@
     tiles = [(at, h) for at in range(2) for h in range(2)]
 
     def load(slot, _):
-        mask, index, count = [entry(plan, 4 + 3 * slot + k) for k in range(3)]
+        mask, index, count = [entry(plan, 5 + 3 * slot + k) for k in range(3)]
         chill = step / count.astype(F32)
 
         def update(u_of, d_of):
@@ -436,7 +435,7 @@
         def _():
             update(lambda f, at, h: u[index, f, at, h], lambda f, at, h: d[index, f, at, h])
 
-        for m, ref in enumerate((got1, got2, got3, got4), 1):
+        for m, ref in enumerate((got1, got2, got4), 1):
 
             @pl.when(mask == m)
             def _():
@@ -447,7 +446,7 @@
         return 0
 
     lax.fori_loop(0, 4, load, 0)
-    limits = [entry(plan, 6 + 3 * slot) for slot in range(4)]
+    limits = [entry(plan, 7 + 3 * slot) for slot in range(4)]
     most = jnp.maximum(jnp.maximum(limits[0], limits[1]), jnp.maximum(limits[2], limits[3]))
     places = [(slot, at, h) for slot in range(4) for at, h in tiles]
 
@@ -498,12 +497,14 @@
     rows, columns = lax.axis_size("bx"), lax.axis_size("by")
     slots = swap_slot.transpose(2, 0, 1)
     counts = cool_steps.transpose(0, 2, 1)
-    slab = (11,) + TILE
     face = (10,) + TILE
     u, w, *slabs = call(
         prep_kernel,
         [conserved.reshape(5, 256, 64)],
-        [BLOCKS] * 2 + [face] * 2 + [slab] * 2 + [face] * 2 + [TILE],
+        [BLOCKS] * 2
+        + [(10,) + TILE, (12,) + TILE, (11,) + TILE, (14,) + TILE]
+        + [face] * 2
+        + [(13,) + TILE],
     )
     e_bx, o_bx, e_by, o_by = slabs[:4]
     got_slabs = [
@@ -518,21 +519,20 @@
         [i * columns + j for i in range(rows) for j in range(x, columns, 4)] for x in range(4)
     ]
     size = len(groups[0])
-    d, send_a, send_b, top = call(
+    d, send, top = call(
         edge_kernel,
         [plan, u, d, *slabs, *got_slabs],
-        [BLOCKS] + [TRAVEL] * 2 + [(size // 2,) + TILE],
-        [(size // 2,) + TILE, pltpu.SemaphoreType.DMA],
+        [BLOCKS, TRAVEL, (size, 6, 128)],
+        [(size, 6, 128), pltpu.SemaphoreType.DMA],
         hbm_out=1,
     )
-    sends = {1: send_a, 2: send_b, 3: send_a}
     trade = lambda m, block: lax.ppermute(block, "by", [(k, k ^ m) for k in range(columns)])
-    got = [trade(m, block) for m, block in sends.items()]
-    top = top.reshape(size, 4, 128)
+    got = [trade(1, send)]
     top = lax.all_to_all(top, ("bx", "by"), 0, 0, axis_index_groups=groups)
-    top = top.reshape((size // 2,) + TILE)
-    (send_c,) = call(relay_kernel, [plan, u, d, *got], [TRAVEL])
-    got.append(trade(4, send_c))
+    for first, mask in ((1, 2), (3, 4)):
+        kernel = functools.partial(relay_kernel, first)
+        (send,) = call(kernel, [plan, u, d, *got], [TRAVEL])
+        got.append(trade(mask, send))
     (result,) = call(
         tail_kernel,
         [plan, u, d, top, *got],

time: 41 us -> 39.5 us (0.963)
  the two profiles are of different devices: /device:TPU:2 before, /device:TPU:16 now
where the time goes in v5:
time: 39.5 us; the launch traced here: 39.3 us
  starting transfers between devices  21.6 us (55%)
  waiting for transfers between devices  10.8 us (27%)
  Pallas kernels  5.73 us (15%)
  local copies, waits for them, and re-layouts  1.1 us (3%)
    ppermute x1, starting transfers between devices, on_device(): lax.ppermute(o_by, 'by', pair_odd(columns))  8.14 us
    all_to_all x1, starting transfers between devices, on_device(): top = lax.all_to_all(top, ('bx', 'by'), 0, 0, axis_index_groups=groups)  7.59 us
    ppermute x3, waiting for transfers between devices, on_device(): lax.ppermute(block, 'by', [(k, k ^ m) for k in range(columns)])  6.17 us
    pallas_call x6, Pallas kernels, call(): pl.pallas_call(kernel, in_specs=[VMEM] * len(inputs), out_specs=[VMEM] *...  5.73 us
    ppermute x3, starting transfers between devices, on_device(): lax.ppermute(block, 'by', [(k, k ^ m) for k in range(columns)])  4.49 us
    all_to_all x1, waiting for transfers between devices, on_device(): top = lax.all_to_all(top, ('bx', 'by'), 0, 0, axis_index_groups=groups)  2.86 us
    ppermute x1, waiting for transfers between devices, on_device(): lax.ppermute(slabs[-1], 'by', [(k, k ^ 2) for k in range(columns)])  1.44 us
    ppermute x1, starting transfers between devices, on_device(): lax.ppermute(e_bx, 'bx', pair_even(rows))  1.39 us
  transfers between devices with their start and end apart: 9, of which 5 were waited for; matrix products, arithmetic and copies ran while one was open for 0% of the time, Pallas kernels for 7%

profile of v5, /device:TPU:16, one launch (start us, length us, event | category | flops | bytes accessed | tf_op | source)
XLA Modules:
  0.0 39.3 jit_solution(12895286340387856221)
XLA Ops:
  0.0 0.0 copy-start
  0.0 1.1 %copy-done = f32[5,16,16,64]{3,2,1,0:T(8,128)S(1)} copy-done((f32[5,16,16,64]{3,2,1,0:T(8,128)S(1)}, f32[5,16,16,64]{3,2,1,0:T(8,128)}, u32[]{:S(2)}) %copy-start) | copy-done | bytes 327704
  1.1 0.0 copy-start.1
  1.1 0.6 %shard_map.37 = (f32[4,5,2,2,8,128]{5,4,3,2,1,0:T(8,128)S(1)}, f32[4,5,2,2,8,128]{5,4,3,2,1,0:T(8,128)S(1)}, f32[10,8,128]{2,1,0:T(8,128)S(1)}, f32[12,8,128]{2,...) custom-call(f32[5,256,64]{2,1,0:T(8,128)S(1)} %bitcast.4), custom_call_target="tpu_custom_call" | custom-call | tf_op jit(solution)/shard_map/pallas_call | solution.py:486
  1.7 0.0 copy-start.2
  1.7 8.1 %collective-permute-start.3 = (f32[14,8,128]{2,1,0:T(8,128)S(1)}, f32[14,8,128]{2,1,0:T(8,128)S(1)}, u32[]{:S(2)}, u32[]{:S(2)}) collective-permute-start(f32[14,8,128]{2,1,0:T(8,128)S(1)} %get-tuple-element.26.so_by), channel_id=1, source_target_pairs={{0,31},{1,2},{2,1},{3,4},{4,3},{5,6},{6,5},{7,8},{8,7},{9,10},{10,... | collective-permute-start | bytes 172040 | tf_op jit(solution)/shard_map/ppermute | solution.py:514
  9.9 0.0 collective-permute-start.4
  9.9 0.0 collective-permute-start.1
  9.9 0.0 collective-permute-start.2
  9.9 1.4 %collective-permute-start = (f32[10,8,128]{2,1,0:T(8,128)S(1)}, f32[10,8,128]{2,1,0:T(8,128)S(1)}, u32[]{:S(2)}, u32[]{:S(2)}) collective-permute-start(f32[10,8,128]{2,1,0:T(8,128)S(1)} %get-tuple-element.23.se_bx), channel_id=1, source_target_pairs={{0,32},{32,0},{64,96},{96,64},{128,160},{160,128},{192,224},{224,1... | collective-permute-start | bytes 122888 | tf_op jit(solution)/shard_map/ppermute | solution.py:511
  11.3 0.0 copy-done.1
  11.3 0.0 copy-done.2
  11.3 2.5 %shard_map.38 = (f32[4,5,2,2,8,128]{5,4,3,2,1,0:T(8,128)S(1)}, s32[24,128]{1,0:T(8,128)S(1)}) custom-call(s32[3,8,32]{2,1,0:T(8,128)S(1)} %bitcast.6, s32[8,4,32]{2,1,0:T(4,128)S(1)} %bitcast.5, f32[4,5,2,2,8,128]{5,4,3,2,1,0:T(8,128)S(1)} %get-tuple-element.19.w), custom_call_target="tpu_custom_call" | custom-call | tf_op jit(solution)/shard_map/pallas_call | solution.py:486
  13.7 0.0 collective-permute-done.re_bx
  13.7 0.3 collective-permute-done.2.re_by
  14.1 0.0 collective-permute-done.1.ro_bx
  14.1 1.4 %collective-permute-done.4.top2 = f32[13,8,128]{2,1,0:T(8,128)S(1)} collective-permute-done((f32[13,8,128]{2,1,0:T(8,128)S(1)}, f32[13,8,128]{2,1,0:T(8,128)S(1)}, u32[]{:S(2)}, u32[]{:S(2)}) %collective-permute-start.4) | collective-permute-done | bytes 53280 | tf_op jit(solution)/shard_map/ppermute | solution.py:515
  15.5 0.0 collective-permute-done.3.ro_by
  15.5 1.1 %shard_map.39 = (f32[4,5,2,2,8,128]{5,4,3,2,1,0:T(8,128)S(1)}, f32[2,5,2,2,8,128]{5,4,3,2,1,0:T(8,128)S(1)}, f32[64,6,128]{2,1,0:T(8,128)}) custom-call(s32[24,128]{1,0:T(8,128)S(1)} %get-tuple-element.20.plan, f32[4,5,2,2,8,128]{5,4,3,2,1,0:T(8,128)S(1)} %get-tuple-element.21.u, f32[4,5,2,2,8,128]{5,4,3,2,1,0:T(8,128)S(1)} %get-tuple-element.22.d_in, ...), custom_call_target="tpu_custom_call" | custom-call | tf_op jit(solution)/shard_map/pallas_call | solution.py:486
  16.6 0.1 collective-permute-start.5
  16.7 7.6 %all-to-all-start = ((f32[64,6,128]{2,1,0:T(8,128)}), f32[64,6,128]{2,1,0:T(8,128)S(1)}, u32[]{:S(2)}, u32[]{:S(2)}) async-start(f32[64,6,128]{2,1,0:T(8,128)} %get-tuple-element.31), calls=%async_computation | async-start | bytes 524288 | tf_op jit(solution)/shard_map/all_to_all | solution.py:531
  24.3 0.0 collective-permute-done.5.refs_0_.got1
  24.3 0.1 shard_map.40
  24.4 2.8 %collective-permute-start.6 = (f32[2,5,2,2,8,128]{5,4,3,2,1,0:T(8,128)S(1)}, f32[2,5,2,2,8,128]{5,4,3,2,1,0:T(8,128)S(1)}, u32[]{:S(2)}, u32[]{:S(2)}) collective-permute-start(f32[2,5,2,2,8,128]{5,4,3,2,1,0:T(8,128)S(1)} %shard_map.40), channel_id=1, source_target_pairs={{0,2},{1,3},{2,0},{3,1},{4,6},{5,7},{6,4},{7,5},{8,10},{9,11},{10,... | collective-permute-start | bytes 491528 | tf_op jit(solution)/shard_map/ppermute | solution.py:529
  27.2 5.0 %collective-permute-done.6.refs_1_.got2 = f32[2,5,2,2,8,128]{5,4,3,2,1,0:T(8,128)S(1)} collective-permute-done((f32[2,5,2,2,8,128]{5,4,3,2,1,0:T(8,128)S(1)}, f32[2,5,2,2,8,128]{5,4,3,2,1,0:T(8,128)S(1)}, u32[]{:S(2)}, u32[]{:S(2)}) %collective-permute-start.6) | collective-permute-done | bytes 163872 | tf_op jit(solution)/shard_map/ppermute | solution.py:529
  32.2 0.1 shard_map.41
  32.3 1.6 %collective-permute-start.7 = (f32[2,5,2,2,8,128]{5,4,3,2,1,0:T(8,128)S(1)}, f32[2,5,2,2,8,128]{5,4,3,2,1,0:T(8,128)S(1)}, u32[]{:S(2)}, u32[]{:S(2)}) collective-permute-start(f32[2,5,2,2,8,128]{5,4,3,2,1,0:T(8,128)S(1)} %shard_map.41), channel_id=1, source_target_pairs={{0,4},{1,5},{2,6},{3,7},{4,0},{5,1},{6,2},{7,3},{8,12},{9,13},{10,... | collective-permute-start | bytes 491528 | tf_op jit(solution)/shard_map/ppermute | solution.py:529
  33.8 2.9 %all-to-all-done.top = f32[64,6,128]{2,1,0:T(8,128)S(1)} async-done(((f32[64,6,128]{2,1,0:T(8,128)}), f32[64,6,128]{2,1,0:T(8,128)S(1)}, u32[]{:S(2)}, u32[]{:S(2)}) %all-to-all-start) | async-done | bytes 196640 | tf_op jit(solution)/shard_map/all_to_all | solution.py:531
  36.7 1.1 %collective-permute-done.7.got4 = f32[2,5,2,2,8,128]{5,4,3,2,1,0:T(8,128)S(1)} collective-permute-done((f32[2,5,2,2,8,128]{5,4,3,2,1,0:T(8,128)S(1)}, f32[2,5,2,2,8,128]{5,4,3,2,1,0:T(8,128)S(1)}, u32[]{:S(2)}, u32[]{:S(2)}) %collective-permute-start.7) | collective-permute-done | bytes 163872 | tf_op jit(solution)/shard_map/ppermute | solution.py:529
  37.8 1.5 %shard_map.42 = f32[4,5,16,256]{3,2,1,0:T(8,128)} custom-call(s32[24,128]{1,0:T(8,128)S(1)} %get-tuple-element.20.plan, f32[4,5,2,2,8,128]{5,4,3,2,1,0:T(8,128)S(1)} %get-tuple-element.21.u, f32[4,5,2,2,8,128]{5,4,3,2,1,0:T(8,128)S(1)} %get-tuple-element.30.d, f32[64,6,128]{2,1,0:T(8,128)S(1)} %all-to-all-done.top, ...), custom_call_target="tpu_custom_call" | custom-call | tf_op jit(solution)/shard_map/pallas_call | solution.py:486
Async XLA Ops:
  0.0 1.1 %copy-start = (f32[5,16,16,64]{3,2,1,0:T(8,128)S(1)}, f32[5,16,16,64]{3,2,1,0:T(8,128)}, u32[]{:S(2)}) copy-start(f32[5,16,16,64]{3,2,1,0:T(8,128)} %param.3) | copy-start | bytes 983044
  1.1 10.2 %copy-start.1 = (s32[8,32,4]{1,2,0:T(4,128)S(1)}, s32[8,32,4]{1,2,0:T(4,128)}, u32[]{:S(2)}) copy-start(s32[8,32,4]{1,2,0:T(4,128)} %param.4) | copy-start | bytes 12292
  1.7 9.6 %copy-start.2 = (s32[8,32,3]{1,0,2:T(8,128)S(1)}, s32[8,32,3]{1,0,2:T(8,128)}, u32[]{:S(2)}) copy-start(s32[8,32,3]{1,0,2:T(8,128)} %param.5) | copy-start | bytes 9220
  1.7 13.8 %collective-permute-start.3 = (f32[14,8,128]{2,1,0:T(8,128)S(1)}, f32[14,8,128]{2,1,0:T(8,128)S(1)}, u32[]{:S(2)}, u32[]{:S(2)}) collective-permute-start(f32[14,8,128]{2,1,0:T(8,128)S(1)} %get-tuple-element.26.so_by), channel_id=1, source_target_pairs={{0,31},{1,2},{2,1},{3,4},{4,3},{5,6},{6,5},{7,8},{8,7},{9,10},{10,... | collective-permute-start | bytes 172040 | tf_op jit(solution)/shard_map/ppermute | solution.py:514
  9.9 5.6 %collective-permute-start.4 = (f32[13,8,128]{2,1,0:T(8,128)S(1)}, f32[13,8,128]{2,1,0:T(8,128)S(1)}, u32[]{:S(2)}, u32[]{:S(2)}) collective-permute-start(f32[13,8,128]{2,1,0:T(8,128)S(1)} %get-tuple-element.29.top), channel_id=1, source_target_pairs={{0,2},{1,3},{2,0},{3,1},{4,6},{5,7},{6,4},{7,5},{8,10},{9,11},{10,... | collective-permute-start | bytes 159752 | tf_op jit(solution)/shard_map/ppermute | solution.py:515
  9.9 4.2 %collective-permute-start.1 = (f32[12,8,128]{2,1,0:T(8,128)S(1)}, f32[12,8,128]{2,1,0:T(8,128)S(1)}, u32[]{:S(2)}, u32[]{:S(2)}) collective-permute-start(f32[12,8,128]{2,1,0:T(8,128)S(1)} %get-tuple-element.24.so_bx), channel_id=1, source_target_pairs={{0,224},{32,64},{64,32},{96,128},{128,96},{160,192},{192,160},{224... | collective-permute-start | bytes 147464 | tf_op jit(solution)/shard_map/ppermute | solution.py:512
  9.9 4.2 %collective-permute-start.2 = (f32[11,8,128]{2,1,0:T(8,128)S(1)}, f32[11,8,128]{2,1,0:T(8,128)S(1)}, u32[]{:S(2)}, u32[]{:S(2)}) collective-permute-start(f32[11,8,128]{2,1,0:T(8,128)S(1)} %get-tuple-element.25.se_by), channel_id=1, source_target_pairs={{0,1},{1,0},{2,3},{3,2},{4,5},{5,4},{6,7},{7,6},{8,9},{9,8},{10,11... | collective-permute-start | bytes 135176 | tf_op jit(solution)/shard_map/ppermute | solution.py:513
  9.9 3.9 %collective-permute-start = (f32[10,8,128]{2,1,0:T(8,128)S(1)}, f32[10,8,128]{2,1,0:T(8,128)S(1)}, u32[]{:S(2)}, u32[]{:S(2)}) collective-permute-start(f32[10,8,128]{2,1,0:T(8,128)S(1)} %get-tuple-element.23.se_bx), channel_id=1, source_target_pairs={{0,32},{32,0},{64,96},{96,64},{128,160},{160,128},{192,224},{224,1... | collective-permute-start | bytes 122888 | tf_op jit(solution)/shard_map/ppermute | solution.py:511
  16.6 7.7 %collective-permute-start.5 = (f32[2,5,2,2,8,128]{5,4,3,2,1,0:T(8,128)S(1)}, f32[2,5,2,2,8,128]{5,4,3,2,1,0:T(8,128)S(1)}, u32[]{:S(2)}, u32[]{:S(2)}) collective-permute-start(f32[2,5,2,2,8,128]{5,4,3,2,1,0:T(8,128)S(1)} %get-tuple-element.32), channel_id=1, source_target_pairs={{0,1},{1,0},{2,3},{3,2},{4,5},{5,4},{6,7},{7,6},{8,9},{9,8},{10,11... | collective-permute-start | bytes 491528 | tf_op jit(solution)/shard_map/ppermute | solution.py:529
  16.7 20.0 %all-to-all-start = ((f32[64,6,128]{2,1,0:T(8,128)}), f32[64,6,128]{2,1,0:T(8,128)S(1)}, u32[]{:S(2)}, u32[]{:S(2)}) async-start(f32[64,6,128]{2,1,0:T(8,128)} %get-tuple-element.31), calls=%async_computation | async-start | bytes 524288 | tf_op jit(solution)/shard_map/all_to_all | solution.py:531
  24.4 7.9 %collective-permute-start.6 = (f32[2,5,2,2,8,128]{5,4,3,2,1,0:T(8,128)S(1)}, f32[2,5,2,2,8,128]{5,4,3,2,1,0:T(8,128)S(1)}, u32[]{:S(2)}, u32[]{:S(2)}) collective-permute-start(f32[2,5,2,2,8,128]{5,4,3,2,1,0:T(8,128)S(1)} %shard_map.40), channel_id=1, source_target_pairs={{0,2},{1,3},{2,0},{3,1},{4,6},{5,7},{6,4},{7,5},{8,10},{9,11},{10,... | collective-permute-start | bytes 491528 | tf_op jit(solution)/shard_map/ppermute | solution.py:529
  32.3 5.5 %collective-permute-start.7 = (f32[2,5,2,2,8,128]{5,4,3,2,1,0:T(8,128)S(1)}, f32[2,5,2,2,8,128]{5,4,3,2,1,0:T(8,128)S(1)}, u32[]{:S(2)}, u32[]{:S(2)}) collective-permute-start(f32[2,5,2,2,8,128]{5,4,3,2,1,0:T(8,128)S(1)} %shard_map.41), channel_id=1, source_target_pairs={{0,4},{1,5},{2,6},{3,7},{4,0},{5,1},{6,2},{7,3},{8,12},{9,13},{10,... | collective-permute-start | bytes 491528 | tf_op jit(solution)/shard_map/ppermute | solution.py:529

commit v6 on v5

--- a/solution.py
+++ b/solution.py
@@ -195,6 +195,7 @@
             count += jnp.where(hit, loads[k], 0.0)
         count = jnp.sum(count, axis=0, keepdims=True)
         entries += [code, index, count]
+    entries.append(give[2])
     for e, value in enumerate(entries):
         plan[pl.ds(e, 1), :] = value[0:1].astype(jnp.int32)
 
@@ -322,7 +323,7 @@
     top = jnp.maximum(jnp.maximum(top[0], top2[0]), jnp.maximum(re_by[10], ro_by[10]))
     top = jnp.broadcast_to(jnp.max(top, axis=0, keepdims=True), TILE)
     for k in range(spread.shape[0]):
-        spread[k] = top[:6]
+        spread[k] = top
     copy = pltpu.make_async_copy(spread, top_out, sent)
     copy.start()
 
@@ -406,49 +407,30 @@
             send[...] = ref[...]
 
 
-def tail_kernel(
-    plan, u, d, top, got1, got2, got4, result, out, energy, factor, tick, sent, last
-):
-    speed = jnp.max(jnp.max(top[...], axis=0), axis=0, keepdims=True)
-    speed = jnp.max(speed, axis=1, keepdims=True)
-    step = COURANT_FACTOR / jnp.broadcast_to(speed, TILE)
-    tiles = [(at, h) for at in range(2) for h in range(2)]
-
-    def load(slot, _):
-        mask, index, count = [entry(plan, 5 + 3 * slot + k) for k in range(3)]
-        chill = step / count.astype(F32)
-
-        def update(u_of, d_of):
-            for at, h in tiles:
-                new = [u_of(f, at, h) - step * d_of(f, at, h) for f in range(5)]
-                inverse = invert(new[0])
-                squares = new[1] * new[1] + new[2] * new[2] + new[3] * new[3]
-                kinetic = 0.5 * squares * inverse
-                energy[slot, at, h] = new[4] - kinetic
-                factor[slot, at, h] = (HEAT_RATIO - 1.0) * inverse
-                tick[slot, at, h] = chill * new[0] * EMISSION_RATE
-                new[4] = kinetic
-                for f in range(5):
-                    out[slot, f, pl.ds(8 * at, 8), pl.ds(128 * h, 128)] = new[f]
-
-        @pl.when(mask == 0)
-        def _():
-            update(lambda f, at, h: u[index, f, at, h], lambda f, at, h: d[index, f, at, h])
-
-        for m, ref in enumerate((got1, got2, got4), 1):
-
-            @pl.when(mask == m)
-            def _():
-                update(lambda f, at, h: ref[0, f, at, h], lambda f, at, h: ref[1, f, at, h])
-
-        place = (slot, pl.ds(0, 4))
-        pltpu.make_async_copy(out.at[place], result.at[place], sent.at[slot]).start()
-        return 0
-
-    lax.fori_loop(0, 4, load, 0)
-    limits = [entry(plan, 7 + 3 * slot) for slot in range(4)]
-    most = jnp.maximum(jnp.maximum(limits[0], limits[1]), jnp.maximum(limits[2], limits[3]))
-    places = [(slot, at, h) for slot in range(4) for at, h in tiles]
+def block_tiles():
+    return [(at, h) for at in range(2) for h in range(2)]
+
+
+def update(out, energy, factor, tick, slot, step, count, u_of, d_of):
+    chill = step / count.astype(F32)
+    for at, h in block_tiles():
+        new = [u_of(f, at, h) - step * d_of(f, at, h) for f in range(5)]
+        inverse = invert(new[0])
+        squares = new[1] * new[1] + new[2] * new[2] + new[3] * new[3]
+        kinetic = 0.5 * squares * inverse
+        energy[slot, at, h] = new[4] - kinetic
+        factor[slot, at, h] = (HEAT_RATIO - 1.0) * inverse
+        tick[slot, at, h] = chill * new[0] * EMISSION_RATE
+        new[4] = kinetic
+        for f in range(5):
+            out[slot, f, pl.ds(8 * at, 8), pl.ds(128 * h, 128)] = new[f]
+
+
+def cool(out, energy, factor, tick, limits):
+    places = [(slot, at, h) for slot in range(len(limits)) for at, h in block_tiles()]
+    most = limits[0]
+    for limit in limits[1:]:
+        most = jnp.maximum(most, limit)
 
     def advance(k, state):
         after = []
@@ -463,15 +445,69 @@
     for left, (slot, at, h) in zip(state, places):
         place = (slot, 4, pl.ds(8 * at, 8), pl.ds(128 * h, 128))
         out[place] = out[place] + left
+
+
+def near_kernel(
+    plan, u, d, top, got1, got2, step_out, result, out, energy, factor, tick, sent, last
+):
+    speed = jnp.max(jnp.max(top[...], axis=0), axis=0, keepdims=True)
+    speed = jnp.max(speed, axis=1, keepdims=True)
+    step = COURANT_FACTOR / jnp.broadcast_to(speed, TILE)
+    step_out[...] = step
+    skipped = entry(plan, 17)
+    target = lambda k: k + jnp.where(k >= skipped, 1, 0)
+
+    def load(k, _):
+        code, index, count = [entry(plan, 5 + 3 * target(k) + e) for e in range(3)]
+        store = lambda *parts: update(out, energy, factor, tick, k, step, count, *parts)
+
+        @pl.when(code == 0)
+        def _():
+            store(lambda f, at, h: u[index, f, at, h], lambda f, at, h: d[index, f, at, h])
+
+        for m, ref in enumerate((got1, got2), 1):
+
+            @pl.when(code == m)
+            def _():
+                store(lambda f, at, h: ref[0, f, at, h], lambda f, at, h: ref[1, f, at, h])
+
+        rows = pl.ds(0, 4)
+        pltpu.make_async_copy(
+            out.at[k, rows], result.at[target(k), rows], sent.at[k]
+        ).start()
+        return 0
+
+    lax.fori_loop(0, 3, load, 0)
+    cool(out, energy, factor, tick, [entry(plan, 7 + 3 * target(k)) for k in range(3)])
     copies = []
-    for slot in range(4):
-        place = (slot, pl.ds(4, 1))
-        copies.append(pltpu.make_async_copy(out.at[place], result.at[place], last.at[slot]))
+    for k in range(3):
+        row = pl.ds(4, 1)
+        copies.append(
+            pltpu.make_async_copy(out.at[k, row], result.at[target(k), row], last.at[k])
+        )
         copies[-1].start()
-    for slot in range(4):
-        place = (slot, pl.ds(0, 4))
-        pltpu.make_async_copy(out.at[place], result.at[place], sent.at[slot]).wait()
-        copies[slot].wait()
+    for k in range(3):
+        rows = pl.ds(0, 4)
+        pltpu.make_async_copy(out.at[k, rows], result.at[target(k), rows], sent.at[k]).wait()
+        copies[k].wait()
+
+
+def far_kernel(plan, step, got, given, result, out, energy, factor, tick, sent, last):
+    slot = entry(plan, 17)
+    count = entry(plan, 7 + 3 * slot)
+    u_of, d_of = [lambda f, at, h, k=k: got[k, f, at, h] for k in range(2)]
+    update(out, energy, factor, tick, 0, step[...], count, u_of, d_of)
+    first = pltpu.make_async_copy(
+        out.at[0, pl.ds(0, 4)], result.at[slot, pl.ds(0, 4)], sent
+    )
+    first.start()
+    cool(out, energy, factor, tick, [count])
+    second = pltpu.make_async_copy(
+        out.at[0, pl.ds(4, 1)], result.at[slot, pl.ds(4, 1)], last
+    )
+    second.start()
+    first.wait()
+    second.wait()
 
 
 def pair_even(count):
@@ -482,14 +518,15 @@
     return [(k, (k + 1) % count if k % 2 else (k - 1) % count) for k in range(count)]
 
 
-def call(kernel, inputs, outputs, scratch=(), hbm_out=0, plan=0):
+def call(kernel, inputs, outputs, scratch=(), hbm_in=0, hbm_out=0, plan=0, aliases=None):
     return pl.pallas_call(
         kernel,
-        in_specs=[VMEM] * len(inputs),
+        in_specs=[VMEM] * (len(inputs) - hbm_in) + [ANY] * hbm_in,
         out_specs=[VMEM] * (len(outputs) - hbm_out) + [ANY] * hbm_out + [VMEM] * plan,
         out_shape=[shape(*dims) for dims in outputs] + [PLAN] * plan,
         scratch_shapes=[pltpu.VMEM(x, F32) if isinstance(x, tuple) else x for x in scratch],
         compiler_params=PARAMS,
+        input_output_aliases=aliases or {},
     )(*inputs)
 
 
@@ -519,26 +556,40 @@
         [i * columns + j for i in range(rows) for j in range(x, columns, 4)] for x in range(4)
     ]
     size = len(groups[0])
+    chunks = (size * 6 // 8,) + TILE
     d, send, top = call(
         edge_kernel,
         [plan, u, d, *slabs, *got_slabs],
-        [BLOCKS, TRAVEL, (size, 6, 128)],
-        [(size, 6, 128), pltpu.SemaphoreType.DMA],
+        [BLOCKS, TRAVEL, chunks],
+        [chunks, pltpu.SemaphoreType.DMA],
         hbm_out=1,
     )
     trade = lambda m, block: lax.ppermute(block, "by", [(k, k ^ m) for k in range(columns)])
     got = [trade(1, send)]
+    top = top.reshape(size, 6, 1, 128)
     top = lax.all_to_all(top, ("bx", "by"), 0, 0, axis_index_groups=groups)
+    top = top.reshape(chunks)
     for first, mask in ((1, 2), (3, 4)):
         kernel = functools.partial(relay_kernel, first)
         (send,) = call(kernel, [plan, u, d, *got], [TRAVEL])
         got.append(trade(mask, send))
+    block = (5, 16, 256)
+    state = (2, 2) + TILE
+    step, result = call(
+        near_kernel,
+        [plan, u, d, top, *got[:2]],
+        [TILE, (4,) + block],
+        [(3,) + block] + [(3,) + state] * 3 + [pltpu.SemaphoreType.DMA((3,))] * 2,
+        hbm_out=1,
+    )
     (result,) = call(
-        tail_kernel,
-        [plan, u, d, top, *got],
-        [(4, 5, 16, 256)],
-        [(4, 5, 16, 256)] + [(4, 2, 2) + TILE] * 3 + [pltpu.SemaphoreType.DMA((4,))] * 2,
+        far_kernel,
+        [plan, step, got[2], result],
+        [(4,) + block],
+        [(1,) + block] + [(1,) + state] * 3 + [pltpu.SemaphoreType.DMA] * 2,
+        hbm_in=1,
         hbm_out=1,
+        aliases={3: 0},
     )
     return result.reshape((1, 1) + result.shape)
 

time: 39.5 us -> 38.9 us (0.985)
  the two profiles are of different devices: /device:TPU:16 before, /device:TPU:2 now
where the time goes in v6:
time: 38.9 us; the launch traced here: 38.1 us
  starting transfers between devices  22.3 us (57%)
  waiting for transfers between devices  8.53 us (22%)
  Pallas kernels  6.11 us (16%)
  local copies, waits for them, and re-layouts  1.1 us (3%)
    all_to_all x1, starting transfers between devices, on_device(): top = lax.all_to_all(top, ('bx', 'by'), 0, 0, axis_index_groups=groups)  6.27 us
    pallas_call x7, Pallas kernels, call(): pl.pallas_call(kernel, in_specs=[VMEM] * (len(inputs) - hbm_in) + [ANY] *...  6.11 us
    ppermute x3, waiting for transfers between devices, on_device(): lax.ppermute(block, 'by', [(k, k ^ m) for k in range(columns)])  5.97 us
    ppermute x3, starting transfers between devices, on_device(): lax.ppermute(block, 'by', [(k, k ^ m) for k in range(columns)])  5.15 us
    ppermute x1, starting transfers between devices, on_device(): lax.ppermute(e_by, 'by', pair_even(columns))  4.91 us
    all_to_all x1, waiting for transfers between devices, on_device(): top = lax.all_to_all(top, ('bx', 'by'), 0, 0, axis_index_groups=groups)  2.55 us
    ppermute x1, starting transfers between devices, on_device(): lax.ppermute(slabs[-1], 'by', [(k, k ^ 2) for k in range(columns)])  2.47 us
    ppermute x1, starting transfers between devices, on_device(): lax.ppermute(o_bx, 'bx', pair_odd(rows))  1.89 us
  transfers between devices with their start and end apart: 9, of which 2 were waited for; matrix products, arithmetic and copies ran while one was open for 0% of the time, Pallas kernels for 10%

profile of v6, /device:TPU:2, one launch (start us, length us, event | category | flops | bytes accessed | tf_op | source)
XLA Modules:
  0.0 38.1 jit_solution(17014738623989197110)
XLA Ops:
  0.0 0.0 copy-start
  0.0 1.1 %copy-done = f32[5,16,16,64]{3,2,1,0:T(8,128)S(1)} copy-done((f32[5,16,16,64]{3,2,1,0:T(8,128)S(1)}, f32[5,16,16,64]{3,2,1,0:T(8,128)}, u32[]{:S(2)}) %copy-start) | copy-done | bytes 327704
  1.1 0.0 copy-start.1
  1.1 0.6 %shard_map.37 = (f32[4,5,2,2,8,128]{5,4,3,2,1,0:T(8,128)S(1)}, f32[4,5,2,2,8,128]{5,4,3,2,1,0:T(8,128)S(1)}, f32[10,8,128]{2,1,0:T(8,128)S(1)}, f32[12,8,128]{2,...) custom-call(f32[5,256,64]{2,1,0:T(8,128)S(1)} %bitcast.7), custom_call_target="tpu_custom_call" | custom-call | tf_op jit(solution)/shard_map/pallas_call | solution.py:522
  1.7 0.0 copy-start.2
  1.7 1.6 %collective-permute-start.3 = (f32[14,8,128]{2,1,0:T(8,128)S(1)}, f32[14,8,128]{2,1,0:T(8,128)S(1)}, u32[]{:S(2)}, u32[]{:S(2)}) collective-permute-start(f32[14,8,128]{2,1,0:T(8,128)S(1)} %get-tuple-element.28.so_by), channel_id=1, source_target_pairs={{0,31},{1,2},{2,1},{3,4},{4,3},{5,6},{6,5},{7,8},{8,7},{9,10},{10,... | collective-permute-start | bytes 172040 | tf_op jit(solution)/shard_map/ppermute | solution.py:551
  3.3 2.5 %collective-permute-start.4 = (f32[13,8,128]{2,1,0:T(8,128)S(1)}, f32[13,8,128]{2,1,0:T(8,128)S(1)}, u32[]{:S(2)}, u32[]{:S(2)}) collective-permute-start(f32[13,8,128]{2,1,0:T(8,128)S(1)} %get-tuple-element.31.top), channel_id=1, source_target_pairs={{0,2},{1,3},{2,0},{3,1},{4,6},{5,7},{6,4},{7,5},{8,10},{9,11},{10,... | collective-permute-start | bytes 159752 | tf_op jit(solution)/shard_map/ppermute | solution.py:552
  5.8 1.9 %collective-permute-start.1 = (f32[12,8,128]{2,1,0:T(8,128)S(1)}, f32[12,8,128]{2,1,0:T(8,128)S(1)}, u32[]{:S(2)}, u32[]{:S(2)}) collective-permute-start(f32[12,8,128]{2,1,0:T(8,128)S(1)} %get-tuple-element.26.so_bx), channel_id=1, source_target_pairs={{0,224},{32,64},{64,32},{96,128},{128,96},{160,192},{192,160},{224... | collective-permute-start | bytes 147464 | tf_op jit(solution)/shard_map/ppermute | solution.py:549
  7.7 4.9 %collective-permute-start.2 = (f32[11,8,128]{2,1,0:T(8,128)S(1)}, f32[11,8,128]{2,1,0:T(8,128)S(1)}, u32[]{:S(2)}, u32[]{:S(2)}) collective-permute-start(f32[11,8,128]{2,1,0:T(8,128)S(1)} %get-tuple-element.27.se_by), channel_id=1, source_target_pairs={{0,1},{1,0},{2,3},{3,2},{4,5},{5,4},{6,7},{7,6},{8,9},{9,8},{10,11... | collective-permute-start | bytes 135176 | tf_op jit(solution)/shard_map/ppermute | solution.py:550
  12.6 0.0 collective-permute-start
  12.6 0.0 copy-done.1
  12.6 0.0 copy-done.2
  12.6 2.5 %shard_map.38 = (f32[4,5,2,2,8,128]{5,4,3,2,1,0:T(8,128)S(1)}, s32[24,128]{1,0:T(8,128)S(1)}) custom-call(s32[3,8,32]{2,1,0:T(8,128)S(1)} %bitcast.9, s32[8,4,32]{2,1,0:T(4,128)S(1)} %bitcast.8, f32[4,5,2,2,8,128]{5,4,3,2,1,0:T(8,128)S(1)} %get-tuple-element.21.w), custom_call_target="tpu_custom_call" | custom-call | tf_op jit(solution)/shard_map/pallas_call | solution.py:522
  15.1 0.0 collective-permute-done.re_bx
  15.1 0.0 collective-permute-done.2.re_by
  15.1 0.0 collective-permute-done.1.ro_bx
  15.1 0.0 collective-permute-done.4.top2
  15.1 0.0 collective-permute-done.3.ro_by
  15.1 1.1 %shard_map.39 = (f32[4,5,2,2,8,128]{5,4,3,2,1,0:T(8,128)S(1)}, f32[2,5,2,2,8,128]{5,4,3,2,1,0:T(8,128)S(1)}, f32[48,8,128]{2,1,0:T(8,128)}) custom-call(s32[24,128]{1,0:T(8,128)S(1)} %get-tuple-element.22.plan, f32[4,5,2,2,8,128]{5,4,3,2,1,0:T(8,128)S(1)} %get-tuple-element.23.u, f32[4,5,2,2,8,128]{5,4,3,2,1,0:T(8,128)S(1)} %get-tuple-element.24.d_in, ...), custom_call_target="tpu_custom_call" | custom-call | tf_op jit(solution)/shard_map/pallas_call | solution.py:522
  16.2 1.6 %collective-permute-start.5 = (f32[2,5,2,2,8,128]{5,4,3,2,1,0:T(8,128)S(1)}, f32[2,5,2,2,8,128]{5,4,3,2,1,0:T(8,128)S(1)}, u32[]{:S(2)}, u32[]{:S(2)}) collective-permute-start(f32[2,5,2,2,8,128]{5,4,3,2,1,0:T(8,128)S(1)} %get-tuple-element.34), channel_id=1, source_target_pairs={{0,1},{1,0},{2,3},{3,2},{4,5},{5,4},{6,7},{7,6},{8,9},{9,8},{10,11... | collective-permute-start | bytes 491528 | tf_op jit(solution)/shard_map/ppermute | solution.py:567
  17.8 6.3 %all-to-all-start = ((f32[64,6,1,128]{3,2,1,0:T(1,128)}), f32[64,6,1,128]{3,2,1,0:T(1,128)S(1)}, u32[]{:S(2)}, u32[]{:S(2)}) async-start(f32[64,6,1,128]{3,2,1,0:T(1,128)} %bitcast.3), calls=%async_computation | async-start | bytes 393216 | tf_op jit(solution)/shard_map/all_to_all | solution.py:570
  24.1 0.0 collective-permute-done.5.refs_0_.got1
  24.1 0.1 shard_map.40
  24.1 1.8 %collective-permute-start.6 = (f32[2,5,2,2,8,128]{5,4,3,2,1,0:T(8,128)S(1)}, f32[2,5,2,2,8,128]{5,4,3,2,1,0:T(8,128)S(1)}, u32[]{:S(2)}, u32[]{:S(2)}) collective-permute-start(f32[2,5,2,2,8,128]{5,4,3,2,1,0:T(8,128)S(1)} %shard_map.40), channel_id=1, source_target_pairs={{0,2},{1,3},{2,0},{3,1},{4,6},{5,7},{6,4},{7,5},{8,10},{9,11},{10,... | collective-permute-start | bytes 491528 | tf_op jit(solution)/shard_map/ppermute | solution.py:567
  25.9 6.0 %collective-permute-done.6.got2.refs_1_ = f32[2,5,2,2,8,128]{5,4,3,2,1,0:T(8,128)S(1)} collective-permute-done((f32[2,5,2,2,8,128]{5,4,3,2,1,0:T(8,128)S(1)}, f32[2,5,2,2,8,128]{5,4,3,2,1,0:T(8,128)S(1)}, u32[]{:S(2)}, u32[]{:S(2)}) %collective-permute-start.6) | collective-permute-done | bytes 163872 | tf_op jit(solution)/shard_map/ppermute | solution.py:567
  31.9 0.1 shard_map.42
  32.0 1.7 %collective-permute-start.7 = (f32[2,5,2,2,8,128]{5,4,3,2,1,0:T(8,128)S(1)}, f32[2,5,2,2,8,128]{5,4,3,2,1,0:T(8,128)S(1)}, u32[]{:S(2)}, u32[]{:S(2)}) collective-permute-start(f32[2,5,2,2,8,128]{5,4,3,2,1,0:T(8,128)S(1)} %shard_map.42), channel_id=1, source_target_pairs={{0,4},{1,5},{2,6},{3,7},{4,0},{5,1},{6,2},{7,3},{8,12},{9,13},{10,... | collective-permute-start | bytes 491528 | tf_op jit(solution)/shard_map/ppermute | solution.py:567
  33.7 2.5 %all-to-all-done = f32[64,6,1,128]{3,2,1,0:T(1,128)S(1)} async-done(((f32[64,6,1,128]{3,2,1,0:T(1,128)}), f32[64,6,1,128]{3,2,1,0:T(1,128)S(1)}, u32[]{:S(2)}, u32[]{:S(2)}) %all-to-all-start) | async-done | bytes 196640 | tf_op jit(solution)/shard_map/all_to_all | solution.py:570
  36.3 1.1 %shard_map.41 = (f32[8,128]{1,0:T(8,128)S(1)}, f32[4,5,16,256]{3,2,1,0:T(8,128)}) custom-call(s32[24,128]{1,0:T(8,128)S(1)} %get-tuple-element.22.plan, f32[4,5,2,2,8,128]{5,4,3,2,1,0:T(8,128)S(1)} %get-tuple-element.23.u, f32[4,5,2,2,8,128]{5,4,3,2,1,0:T(8,128)S(1)} %get-tuple-element.32.d, f32[48,8,128]{2,1,0:T(8,128)S(1)} %bitcast.6, ...), custom_call_target="tpu_custom_call" | custom-call | tf_op jit(solution)/shard_map/pallas_call | solution.py:522
  37.4 0.0 collective-permute-done.7.got
  37.4 0.7 %shard_map.43 = f32[4,5,16,256]{3,2,1,0:T(8,128)} custom-call(s32[24,128]{1,0:T(8,128)S(1)} %get-tuple-element.22.plan, f32[8,128]{1,0:T(8,128)S(1)} %get-tuple-element.35.step, f32[2,5,2,2,8,128]{5,4,3,2,1,0:T(8,128)S(1)} %collective-permute-done.7.got, f32[4,5,16,256]{3,2,1,0:T(8,128)} %get-tuple-element.36.given), custom_call_target="tpu_custom_call", output_to_operand_aliasing={{}: (3, {})} | custom-call | tf_op jit(solution)/shard_map/pallas_call | solution.py:522
Async XLA Ops:
  0.0 1.1 %copy-start = (f32[5,16,16,64]{3,2,1,0:T(8,128)S(1)}, f32[5,16,16,64]{3,2,1,0:T(8,128)}, u32[]{:S(2)}) copy-start(f32[5,16,16,64]{3,2,1,0:T(8,128)} %param.3) | copy-start | bytes 983044
  1.1 11.5 %copy-start.1 = (s32[8,32,4]{1,2,0:T(4,128)S(1)}, s32[8,32,4]{1,2,0:T(4,128)}, u32[]{:S(2)}) copy-start(s32[8,32,4]{1,2,0:T(4,128)} %param.4) | copy-start | bytes 12292
  1.7 10.9 %copy-start.2 = (s32[8,32,3]{1,0,2:T(8,128)S(1)}, s32[8,32,3]{1,0,2:T(8,128)}, u32[]{:S(2)}) copy-start(s32[8,32,3]{1,0,2:T(8,128)} %param.5) | copy-start | bytes 9220
  1.7 13.4 %collective-permute-start.3 = (f32[14,8,128]{2,1,0:T(8,128)S(1)}, f32[14,8,128]{2,1,0:T(8,128)S(1)}, u32[]{:S(2)}, u32[]{:S(2)}) collective-permute-start(f32[14,8,128]{2,1,0:T(8,128)S(1)} %get-tuple-element.28.so_by), channel_id=1, source_target_pairs={{0,31},{1,2},{2,1},{3,4},{4,3},{5,6},{6,5},{7,8},{8,7},{9,10},{10,... | collective-permute-start | bytes 172040 | tf_op jit(solution)/shard_map/ppermute | solution.py:551
  3.3 11.8 %collective-permute-start.4 = (f32[13,8,128]{2,1,0:T(8,128)S(1)}, f32[13,8,128]{2,1,0:T(8,128)S(1)}, u32[]{:S(2)}, u32[]{:S(2)}) collective-permute-start(f32[13,8,128]{2,1,0:T(8,128)S(1)} %get-tuple-element.31.top), channel_id=1, source_target_pairs={{0,2},{1,3},{2,0},{3,1},{4,6},{5,7},{6,4},{7,5},{8,10},{9,11},{10,... | collective-permute-start | bytes 159752 | tf_op jit(solution)/shard_map/ppermute | solution.py:552
  5.8 9.3 %collective-permute-start.1 = (f32[12,8,128]{2,1,0:T(8,128)S(1)}, f32[12,8,128]{2,1,0:T(8,128)S(1)}, u32[]{:S(2)}, u32[]{:S(2)}) collective-permute-start(f32[12,8,128]{2,1,0:T(8,128)S(1)} %get-tuple-element.26.so_bx), channel_id=1, source_target_pairs={{0,224},{32,64},{64,32},{96,128},{128,96},{160,192},{192,160},{224... | collective-permute-start | bytes 147464 | tf_op jit(solution)/shard_map/ppermute | solution.py:549
  7.7 7.4 %collective-permute-start.2 = (f32[11,8,128]{2,1,0:T(8,128)S(1)}, f32[11,8,128]{2,1,0:T(8,128)S(1)}, u32[]{:S(2)}, u32[]{:S(2)}) collective-permute-start(f32[11,8,128]{2,1,0:T(8,128)S(1)} %get-tuple-element.27.se_by), channel_id=1, source_target_pairs={{0,1},{1,0},{2,3},{3,2},{4,5},{5,4},{6,7},{7,6},{8,9},{9,8},{10,11... | collective-permute-start | bytes 135176 | tf_op jit(solution)/shard_map/ppermute | solution.py:550
  12.6 2.5 %collective-permute-start = (f32[10,8,128]{2,1,0:T(8,128)S(1)}, f32[10,8,128]{2,1,0:T(8,128)S(1)}, u32[]{:S(2)}, u32[]{:S(2)}) collective-permute-start(f32[10,8,128]{2,1,0:T(8,128)S(1)} %get-tuple-element.25.se_bx), channel_id=1, source_target_pairs={{0,32},{32,0},{64,96},{96,64},{128,160},{160,128},{192,224},{224,1... | collective-permute-start | bytes 122888 | tf_op jit(solution)/shard_map/ppermute | solution.py:548
  16.2 7.9 %collective-permute-start.5 = (f32[2,5,2,2,8,128]{5,4,3,2,1,0:T(8,128)S(1)}, f32[2,5,2,2,8,128]{5,4,3,2,1,0:T(8,128)S(1)}, u32[]{:S(2)}, u32[]{:S(2)}) collective-permute-start(f32[2,5,2,2,8,128]{5,4,3,2,1,0:T(8,128)S(1)} %get-tuple-element.34), channel_id=1, source_target_pairs={{0,1},{1,0},{2,3},{3,2},{4,5},{5,4},{6,7},{7,6},{8,9},{9,8},{10,11... | collective-permute-start | bytes 491528 | tf_op jit(solution)/shard_map/ppermute | solution.py:567
  17.8 18.5 %all-to-all-start = ((f32[64,6,1,128]{3,2,1,0:T(1,128)}), f32[64,6,1,128]{3,2,1,0:T(1,128)S(1)}, u32[]{:S(2)}, u32[]{:S(2)}) async-start(f32[64,6,1,128]{3,2,1,0:T(1,128)} %bitcast.3), calls=%async_computation | async-start | bytes 393216 | tf_op jit(solution)/shard_map/all_to_all | solution.py:570
  24.1 7.8 %collective-permute-start.6 = (f32[2,5,2,2,8,128]{5,4,3,2,1,0:T(8,128)S(1)}, f32[2,5,2,2,8,128]{5,4,3,2,1,0:T(8,128)S(1)}, u32[]{:S(2)}, u32[]{:S(2)}) collective-permute-start(f32[2,5,2,2,8,128]{5,4,3,2,1,0:T(8,128)S(1)} %shard_map.40), channel_id=1, source_target_pairs={{0,2},{1,3},{2,0},{3,1},{4,6},{5,7},{6,4},{7,5},{8,10},{9,11},{10,... | collective-permute-start | bytes 491528 | tf_op jit(solution)/shard_map/ppermute | solution.py:567
  32.0 5.4 %collective-permute-start.7 = (f32[2,5,2,2,8,128]{5,4,3,2,1,0:T(8,128)S(1)}, f32[2,5,2,2,8,128]{5,4,3,2,1,0:T(8,128)S(1)}, u32[]{:S(2)}, u32[]{:S(2)}) collective-permute-start(f32[2,5,2,2,8,128]{5,4,3,2,1,0:T(8,128)S(1)} %shard_map.42), channel_id=1, source_target_pairs={{0,4},{1,5},{2,6},{3,7},{4,0},{5,1},{6,2},{7,3},{8,12},{9,13},{10,... | collective-permute-start | bytes 491528 | tf_op jit(solution)/shard_map/ppermute | solution.py:567

commit v7 on v6

--- a/solution.py
+++ b/solution.py
@@ -14,6 +14,7 @@
 TILE = (8, 128)
 BLOCKS = (4, 5, 2, 2) + TILE
 TRAVEL = (2, 5, 2, 2) + TILE
+HALF = (5, 2, 2) + TILE
 VMEM = pl.BlockSpec(memory_space=pltpu.VMEM)
 ANY = pl.BlockSpec(memory_space=pl.ANY)
 PARAMS = pltpu.CompilerParams(vmem_limit_bytes=16 * 1024 * 1024)
@@ -309,7 +310,8 @@
         return 0
 
     for body in (along_first, along_second, third_states, third_fluxes, third_change):
-        lax.fori_loop(0, 8, body, 0, unroll=4)
+        unroll = 8 if body in (third_states, third_change) else 4
+        lax.fori_loop(0, 8, body, 0, unroll=unroll)
 
 
 def edge_kernel(
@@ -391,20 +393,34 @@
     copy.wait()
 
 
-def relay_kernel(first, plan, u, d, *refs):
-    *got, send = refs
-    code, index = entry(plan, first), entry(plan, first + 1)
+def relay_kernel(plan, u, d, got1, send_u, send_d):
+    code, index = entry(plan, 1), entry(plan, 2)
 
     @pl.when(code == 0)
     def _():
-        send[0] = u[index]
-        send[1] = d[index]
-
-    for m, ref in enumerate(got, 1):
-
-        @pl.when(code == m)
-        def _():
-            send[...] = ref[...]
+        send_u[...] = u[index]
+        send_d[...] = d[index]
+
+    @pl.when(code == 1)
+    def _():
+        send_u[...] = got1[0]
+        send_d[...] = got1[1]
+
+
+def pass_kernel(part, plan, own, got1, got2, send):
+    code, index = entry(plan, 3), entry(plan, 4)
+
+    @pl.when(code == 0)
+    def _():
+        send[...] = own[index]
+
+    @pl.when(code == 1)
+    def _():
+        send[...] = got1[part]
+
+    @pl.when(code == 2)
+    def _():
+        send[...] = got2[...]
 
 
 def block_tiles():
@@ -448,7 +464,7 @@
 
 
 def near_kernel(
-    plan, u, d, top, got1, got2, step_out, result, out, energy, factor, tick, sent, last
+    plan, u, d, top, got1, got_u, got_d, step_out, result, out, energy, factor, tick, sent, last
 ):
     speed = jnp.max(jnp.max(top[...], axis=0), axis=0, keepdims=True)
     speed = jnp.max(speed, axis=1, keepdims=True)
@@ -465,11 +481,13 @@
         def _():
             store(lambda f, at, h: u[index, f, at, h], lambda f, at, h: d[index, f, at, h])
 
-        for m, ref in enumerate((got1, got2), 1):
-
-            @pl.when(code == m)
-            def _():
-                store(lambda f, at, h: ref[0, f, at, h], lambda f, at, h: ref[1, f, at, h])
+        @pl.when(code == 1)
+        def _():
+            store(lambda f, at, h: got1[0, f, at, h], lambda f, at, h: got1[1, f, at, h])
+
+        @pl.when(code == 2)
+        def _():
+            store(lambda f, at, h: got_u[f, at, h], lambda f, at, h: got_d[f, at, h])
 
         rows = pl.ds(0, 4)
         pltpu.make_async_copy(
@@ -492,10 +510,10 @@
         copies[k].wait()
 
 
-def far_kernel(plan, step, got, given, result, out, energy, factor, tick, sent, last):
+def far_kernel(plan, step, got_u, got_d, given, result, out, energy, factor, tick, sent, last):
     slot = entry(plan, 17)
     count = entry(plan, 7 + 3 * slot)
-    u_of, d_of = [lambda f, at, h, k=k: got[k, f, at, h] for k in range(2)]
+    u_of, d_of = [lambda f, at, h, ref=ref: ref[f, at, h] for ref in (got_u, got_d)]
     update(out, energy, factor, tick, 0, step[...], count, u_of, d_of)
     first = pltpu.make_async_copy(
         out.at[0, pl.ds(0, 4)], result.at[slot, pl.ds(0, 4)], sent
@@ -556,7 +574,7 @@
         [i * columns + j for i in range(rows) for j in range(x, columns, 4)] for x in range(4)
     ]
     size = len(groups[0])
-    chunks = (size * 6 // 8,) + TILE
+    chunks = (size * 3 // 8,) + TILE
     d, send, top = call(
         edge_kernel,
         [plan, u, d, *slabs, *got_slabs],
@@ -565,31 +583,34 @@
         hbm_out=1,
     )
     trade = lambda m, block: lax.ppermute(block, "by", [(k, k ^ m) for k in range(columns)])
-    got = [trade(1, send)]
-    top = top.reshape(size, 6, 1, 128)
+    got1 = trade(1, send)
+    top = top.reshape(size, 3, 1, 128)
     top = lax.all_to_all(top, ("bx", "by"), 0, 0, axis_index_groups=groups)
     top = top.reshape(chunks)
-    for first, mask in ((1, 2), (3, 4)):
-        kernel = functools.partial(relay_kernel, first)
-        (send,) = call(kernel, [plan, u, d, *got], [TRAVEL])
-        got.append(trade(mask, send))
+    sends = call(relay_kernel, [plan, u, d, got1], [HALF] * 2)
+    got2 = [trade(2, send) for send in sends]
+    got4 = []
+    for part, own in enumerate((u, d)):
+        kernel = functools.partial(pass_kernel, part)
+        (send,) = call(kernel, [plan, own, got1, got2[part]], [HALF])
+        got4.append(trade(4, send))
     block = (5, 16, 256)
     state = (2, 2) + TILE
     step, result = call(
         near_kernel,
-        [plan, u, d, top, *got[:2]],
+        [plan, u, d, top, got1, *got2],
         [TILE, (4,) + block],
         [(3,) + block] + [(3,) + state] * 3 + [pltpu.SemaphoreType.DMA((3,))] * 2,
         hbm_out=1,
     )
     (result,) = call(
         far_kernel,
-        [plan, step, got[2], result],
+        [plan, step, *got4, result],
         [(4,) + block],
         [(1,) + block] + [(1,) + state] * 3 + [pltpu.SemaphoreType.DMA] * 2,
         hbm_in=1,
         hbm_out=1,
-        aliases={3: 0},
+        aliases={4: 0},
     )
     return result.reshape((1, 1) + result.shape)
 

time: 38.9 us -> 38.5 us (0.990)
  waiting for transfers between devices: 8.53 us -> 5.26 us
  starting transfers between devices: 22.3 us -> 25.4 us
    ppermute x3 -> x5, starting transfers between devices: 5.15 us -> 8.27 us  [on_device(): lax.ppermute(block, 'by', [(k, k ^ m) for k in range(columns)])]
    all_to_all x1, waiting for transfers between devices: 2.55 us -> 0.88 us  [on_device(): top = lax.all_to_all(top, ('bx', 'by'), 0, 0, axis_index_groups=groups)]
    ppermute x3 -> x5, waiting for transfers between devices: 5.97 us -> 4.37 us  [on_device(): lax.ppermute(block, 'by', [(k, k ^ m) for k in range(columns)])]
    pallas_call x7 -> x8, Pallas kernels: 6.11 us -> 5.95 us  [call(): pl.pallas_call(kernel, in_specs=[VMEM] * (len(inputs) - hbm_in) + [ANY] *...]
  transfers between devices with their start and end apart: 9 -> 11, of which waited for: 2 -> 4; matrix products, arithmetic and copies ran while one was open for 0% -> 0% of each run, Pallas kernels for 10% -> 9%
where the time goes in v7:
time: 38.5 us; the launch traced here: 37.8 us
  starting transfers between devices  25.4 us (66%)
  Pallas kernels  5.95 us (15%)
  waiting for transfers between devices  5.26 us (14%)
  local copies, waits for them, and re-layouts  1.1 us (3%)
    ppermute x5, starting transfers between devices, on_device(): lax.ppermute(block, 'by', [(k, k ^ m) for k in range(columns)])  8.27 us
    all_to_all x1, starting transfers between devices, on_device(): top = lax.all_to_all(top, ('bx', 'by'), 0, 0, axis_index_groups=groups)  6.27 us
    pallas_call x8, Pallas kernels, call(): pl.pallas_call(kernel, in_specs=[VMEM] * (len(inputs) - hbm_in) + [ANY] *...  5.95 us
    ppermute x1, starting transfers between devices, on_device(): lax.ppermute(e_by, 'by', pair_even(columns))  4.91 us
    ppermute x5, waiting for transfers between devices, on_device(): lax.ppermute(block, 'by', [(k, k ^ m) for k in range(columns)])  4.37 us
    ppermute x1, starting transfers between devices, on_device(): lax.ppermute(slabs[-1], 'by', [(k, k ^ 2) for k in range(columns)])  2.47 us
    ppermute x1, starting transfers between devices, on_device(): lax.ppermute(o_bx, 'bx', pair_odd(rows))  1.89 us
    ppermute x1, starting transfers between devices, on_device(): lax.ppermute(o_by, 'by', pair_odd(columns))  1.58 us
  transfers between devices with their start and end apart: 11, of which 4 were waited for; matrix products, arithmetic and copies ran while one was open for 0% of the time, Pallas kernels for 9%

profile of v7, /device:TPU:2, one launch (start us, length us, event | category | flops | bytes accessed | tf_op | source)
XLA Modules:
  0.0 37.8 jit_solution(15494186230402572175)
XLA Ops:
  0.0 0.0 copy-start
  0.0 1.1 %copy-done = f32[5,16,16,64]{3,2,1,0:T(8,128)S(1)} copy-done((f32[5,16,16,64]{3,2,1,0:T(8,128)S(1)}, f32[5,16,16,64]{3,2,1,0:T(8,128)}, u32[]{:S(2)}) %copy-start) | copy-done | bytes 327704
  1.1 0.0 copy-start.1
  1.1 0.6 %shard_map.37 = (f32[4,5,2,2,8,128]{5,4,3,2,1,0:T(8,128)S(1)}, f32[4,5,2,2,8,128]{5,4,3,2,1,0:T(8,128)S(1)}, f32[10,8,128]{2,1,0:T(8,128)S(1)}, f32[12,8,128]{2,...) custom-call(f32[5,256,64]{2,1,0:T(8,128)S(1)} %bitcast.6), custom_call_target="tpu_custom_call" | custom-call | tf_op jit(solution)/shard_map/pallas_call | solution.py:540
  1.7 0.0 copy-start.2
  1.7 1.6 %collective-permute-start.3 = (f32[14,8,128]{2,1,0:T(8,128)S(1)}, f32[14,8,128]{2,1,0:T(8,128)S(1)}, u32[]{:S(2)}, u32[]{:S(2)}) collective-permute-start(f32[14,8,128]{2,1,0:T(8,128)S(1)} %get-tuple-element.30.so_by), channel_id=1, source_target_pairs={{0,31},{1,2},{2,1},{3,4},{4,3},{5,6},{6,5},{7,8},{8,7},{9,10},{10,... | collective-permute-start | bytes 172040 | tf_op jit(solution)/shard_map/ppermute | solution.py:569
  3.3 2.5 %collective-permute-start.4 = (f32[13,8,128]{2,1,0:T(8,128)S(1)}, f32[13,8,128]{2,1,0:T(8,128)S(1)}, u32[]{:S(2)}, u32[]{:S(2)}) collective-permute-start(f32[13,8,128]{2,1,0:T(8,128)S(1)} %get-tuple-element.33.top), channel_id=1, source_target_pairs={{0,2},{1,3},{2,0},{3,1},{4,6},{5,7},{6,4},{7,5},{8,10},{9,11},{10,... | collective-permute-start | bytes 159752 | tf_op jit(solution)/shard_map/ppermute | solution.py:570
  5.8 1.9 %collective-permute-start.1 = (f32[12,8,128]{2,1,0:T(8,128)S(1)}, f32[12,8,128]{2,1,0:T(8,128)S(1)}, u32[]{:S(2)}, u32[]{:S(2)}) collective-permute-start(f32[12,8,128]{2,1,0:T(8,128)S(1)} %get-tuple-element.28.so_bx), channel_id=1, source_target_pairs={{0,224},{32,64},{64,32},{96,128},{128,96},{160,192},{192,160},{224... | collective-permute-start | bytes 147464 | tf_op jit(solution)/shard_map/ppermute | solution.py:567
  7.7 4.9 %collective-permute-start.2 = (f32[11,8,128]{2,1,0:T(8,128)S(1)}, f32[11,8,128]{2,1,0:T(8,128)S(1)}, u32[]{:S(2)}, u32[]{:S(2)}) collective-permute-start(f32[11,8,128]{2,1,0:T(8,128)S(1)} %get-tuple-element.29.se_by), channel_id=1, source_target_pairs={{0,1},{1,0},{2,3},{3,2},{4,5},{5,4},{6,7},{7,6},{8,9},{9,8},{10,11... | collective-permute-start | bytes 135176 | tf_op jit(solution)/shard_map/ppermute | solution.py:568
  12.6 0.0 collective-permute-start
  12.6 0.0 copy-done.1
  12.6 0.0 copy-done.2
  12.6 2.3 %shard_map.38 = (f32[4,5,2,2,8,128]{5,4,3,2,1,0:T(8,128)S(1)}, s32[24,128]{1,0:T(8,128)S(1)}) custom-call(s32[3,8,32]{2,1,0:T(8,128)S(1)} %bitcast.9, s32[8,4,32]{2,1,0:T(4,128)S(1)} %bitcast.8, f32[4,5,2,2,8,128]{5,4,3,2,1,0:T(8,128)S(1)} %get-tuple-element.23.w), custom_call_target="tpu_custom_call" | custom-call | tf_op jit(solution)/shard_map/pallas_call | solution.py:540
  14.9 0.0 collective-permute-done.re_bx
  14.9 0.0 collective-permute-done.2.re_by
  14.9 0.0 collective-permute-done.1.ro_bx
  14.9 0.0 collective-permute-done.4.top2
  14.9 0.0 collective-permute-done.3.ro_by
  14.9 1.0 %shard_map.39 = (f32[4,5,2,2,8,128]{5,4,3,2,1,0:T(8,128)S(1)}, f32[2,5,2,2,8,128]{5,4,3,2,1,0:T(8,128)S(1)}, f32[24,8,128]{2,1,0:T(8,128)}) custom-call(s32[24,128]{1,0:T(8,128)S(1)} %get-tuple-element.24.plan, f32[4,5,2,2,8,128]{5,4,3,2,1,0:T(8,128)S(1)} %get-tuple-element.25.u.own, f32[4,5,2,2,8,128]{5,4,3,2,1,0:T(8,128)S(1)} %get-tuple-element.26.d_in, ...), custom_call_target="tpu_custom_call" | custom-call | tf_op jit(solution)/shard_map/pallas_call | solution.py:540
  16.0 1.8 %collective-permute-start.5 = (f32[2,5,2,2,8,128]{5,4,3,2,1,0:T(8,128)S(1)}, f32[2,5,2,2,8,128]{5,4,3,2,1,0:T(8,128)S(1)}, u32[]{:S(2)}, u32[]{:S(2)}) collective-permute-start(f32[2,5,2,2,8,128]{5,4,3,2,1,0:T(8,128)S(1)} %get-tuple-element.36), channel_id=1, source_target_pairs={{0,1},{1,0},{2,3},{3,2},{4,5},{5,4},{6,7},{7,6},{8,9},{9,8},{10,11... | collective-permute-start | bytes 491528 | tf_op jit(solution)/shard_map/ppermute | solution.py:585
  17.8 6.3 %all-to-all-start = ((f32[64,3,1,128]{3,2,1,0:T(1,128)}), f32[64,3,1,128]{3,2,1,0:T(1,128)S(1)}, u32[]{:S(2)}, u32[]{:S(2)}) async-start(f32[64,3,1,128]{3,2,1,0:T(1,128)} %bitcast.3), calls=%async_computation | async-start | bytes 196608 | tf_op jit(solution)/shard_map/all_to_all | solution.py:588
  24.0 0.0 collective-permute-done.5.got1
  24.0 0.1 shard_map.40
  24.1 1.6 %collective-permute-start.6 = (f32[5,2,2,8,128]{4,3,2,1,0:T(8,128)S(1)}, f32[5,2,2,8,128]{4,3,2,1,0:T(8,128)S(1)}, u32[]{:S(2)}, u32[]{:S(2)}) collective-permute-start(f32[5,2,2,8,128]{4,3,2,1,0:T(8,128)S(1)} %get-tuple-element.37), channel_id=1, source_target_pairs={{0,2},{1,3},{2,0},{3,1},{4,6},{5,7},{6,4},{7,5},{8,10},{9,11},{10,... | collective-permute-start | bytes 245768 | tf_op jit(solution)/shard_map/ppermute | solution.py:585
  25.7 2.0 %collective-permute-start.7 = (f32[5,2,2,8,128]{4,3,2,1,0:T(8,128)S(1)}, f32[5,2,2,8,128]{4,3,2,1,0:T(8,128)S(1)}, u32[]{:S(2)}, u32[]{:S(2)}) collective-permute-start(f32[5,2,2,8,128]{4,3,2,1,0:T(8,128)S(1)} %get-tuple-element.38), channel_id=1, source_target_pairs={{0,2},{1,3},{2,0},{3,1},{4,6},{5,7},{6,4},{7,5},{8,10},{9,11},{10,... | collective-permute-start | bytes 245768 | tf_op jit(solution)/shard_map/ppermute | solution.py:585
  27.7 3.0 %collective-permute-done.6.got_u.got2 = f32[5,2,2,8,128]{4,3,2,1,0:T(8,128)S(1)} collective-permute-done((f32[5,2,2,8,128]{4,3,2,1,0:T(8,128)S(1)}, f32[5,2,2,8,128]{4,3,2,1,0:T(8,128)S(1)}, u32[]{:S(2)}, u32[]{:S(2)}) %collective-permute-start.6) | collective-permute-done | bytes 81952 | tf_op jit(solution)/shard_map/ppermute | solution.py:585
  30.7 0.1 shard_map.42
  30.7 1.8 %collective-permute-start.8 = (f32[5,2,2,8,128]{4,3,2,1,0:T(8,128)S(1)}, f32[5,2,2,8,128]{4,3,2,1,0:T(8,128)S(1)}, u32[]{:S(2)}, u32[]{:S(2)}) collective-permute-start(f32[5,2,2,8,128]{4,3,2,1,0:T(8,128)S(1)} %shard_map.42), channel_id=1, source_target_pairs={{0,4},{1,5},{2,6},{3,7},{4,0},{5,1},{6,2},{7,3},{8,12},{9,13},{10,... | collective-permute-start | bytes 245768 | tf_op jit(solution)/shard_map/ppermute | solution.py:585
  32.5 0.0 collective-permute-done.7.got_d.got2
  32.5 0.1 shard_map.43
  32.6 1.1 %collective-permute-start.9 = (f32[5,2,2,8,128]{4,3,2,1,0:T(8,128)S(1)}, f32[5,2,2,8,128]{4,3,2,1,0:T(8,128)S(1)}, u32[]{:S(2)}, u32[]{:S(2)}) collective-permute-start(f32[5,2,2,8,128]{4,3,2,1,0:T(8,128)S(1)} %shard_map.43), channel_id=1, source_target_pairs={{0,4},{1,5},{2,6},{3,7},{4,0},{5,1},{6,2},{7,3},{8,12},{9,13},{10,... | collective-permute-start | bytes 245768 | tf_op jit(solution)/shard_map/ppermute | solution.py:585
  33.7 0.9 %all-to-all-done = f32[64,3,1,128]{3,2,1,0:T(1,128)S(1)} async-done(((f32[64,3,1,128]{3,2,1,0:T(1,128)}), f32[64,3,1,128]{3,2,1,0:T(1,128)S(1)}, u32[]{:S(2)}, u32[]{:S(2)}) %all-to-all-start) | async-done | bytes 98336 | tf_op jit(solution)/shard_map/all_to_all | solution.py:588
  34.6 1.1 %shard_map.41 = (f32[8,128]{1,0:T(8,128)S(1)}, f32[4,5,16,256]{3,2,1,0:T(8,128)}) custom-call(s32[24,128]{1,0:T(8,128)S(1)} %get-tuple-element.24.plan, f32[4,5,2,2,8,128]{5,4,3,2,1,0:T(8,128)S(1)} %get-tuple-element.25.u.own, f32[4,5,2,2,8,128]{5,4,3,2,1,0:T(8,128)S(1)} %get-tuple-element.34.d.own, f32[24,8,128]{2,1,0:T(8,128)S(1)} %bitcast.7, ...), custom_call_target="tpu_custom_call" | custom-call | tf_op jit(solution)/shard_map/pallas_call | solution.py:540
  35.7 0.2 collective-permute-done.8.got_u
  35.8 1.3 %collective-permute-done.9.got_d = f32[5,2,2,8,128]{4,3,2,1,0:T(8,128)S(1)} collective-permute-done((f32[5,2,2,8,128]{4,3,2,1,0:T(8,128)S(1)}, f32[5,2,2,8,128]{4,3,2,1,0:T(8,128)S(1)}, u32[]{:S(2)}, u32[]{:S(2)}) %collective-permute-start.9) | collective-permute-done | bytes 81952 | tf_op jit(solution)/shard_map/ppermute | solution.py:585
  37.1 0.7 %shard_map.44 = f32[4,5,16,256]{3,2,1,0:T(8,128)} custom-call(s32[24,128]{1,0:T(8,128)S(1)} %get-tuple-element.24.plan, f32[8,128]{1,0:T(8,128)S(1)} %get-tuple-element.39.step, f32[5,2,2,8,128]{4,3,2,1,0:T(8,128)S(1)} %collective-permute-done.8.got_u, f32[5,2,2,8,128]{4,3,2,1,0:T(8,128)S(1)} %collective-permute-done.9.got_d, ...), custom_call_target="tpu_custom_call", output_to_operand_aliasing={{}: (4, {})} | custom-call | tf_op jit(solution)/shard_map/pallas_call | solution.py:540
Async XLA Ops:
  0.0 1.1 %copy-start = (f32[5,16,16,64]{3,2,1,0:T(8,128)S(1)}, f32[5,16,16,64]{3,2,1,0:T(8,128)}, u32[]{:S(2)}) copy-start(f32[5,16,16,64]{3,2,1,0:T(8,128)} %param.3) | copy-start | bytes 983044
  1.1 11.5 %copy-start.1 = (s32[8,32,4]{1,2,0:T(4,128)S(1)}, s32[8,32,4]{1,2,0:T(4,128)}, u32[]{:S(2)}) copy-start(s32[8,32,4]{1,2,0:T(4,128)} %param.4) | copy-start | bytes 12292
  1.7 10.9 %copy-start.2 = (s32[8,32,3]{1,0,2:T(8,128)S(1)}, s32[8,32,3]{1,0,2:T(8,128)}, u32[]{:S(2)}) copy-start(s32[8,32,3]{1,0,2:T(8,128)} %param.5) | copy-start | bytes 9220
  1.7 13.2 %collective-permute-start.3 = (f32[14,8,128]{2,1,0:T(8,128)S(1)}, f32[14,8,128]{2,1,0:T(8,128)S(1)}, u32[]{:S(2)}, u32[]{:S(2)}) collective-permute-start(f32[14,8,128]{2,1,0:T(8,128)S(1)} %get-tuple-element.30.so_by), channel_id=1, source_target_pairs={{0,31},{1,2},{2,1},{3,4},{4,3},{5,6},{6,5},{7,8},{8,7},{9,10},{10,... | collective-permute-start | bytes 172040 | tf_op jit(solution)/shard_map/ppermute | solution.py:569
  3.3 11.6 %collective-permute-start.4 = (f32[13,8,128]{2,1,0:T(8,128)S(1)}, f32[13,8,128]{2,1,0:T(8,128)S(1)}, u32[]{:S(2)}, u32[]{:S(2)}) collective-permute-start(f32[13,8,128]{2,1,0:T(8,128)S(1)} %get-tuple-element.33.top), channel_id=1, source_target_pairs={{0,2},{1,3},{2,0},{3,1},{4,6},{5,7},{6,4},{7,5},{8,10},{9,11},{10,... | collective-permute-start | bytes 159752 | tf_op jit(solution)/shard_map/ppermute | solution.py:570
  5.8 9.1 %collective-permute-start.1 = (f32[12,8,128]{2,1,0:T(8,128)S(1)}, f32[12,8,128]{2,1,0:T(8,128)S(1)}, u32[]{:S(2)}, u32[]{:S(2)}) collective-permute-start(f32[12,8,128]{2,1,0:T(8,128)S(1)} %get-tuple-element.28.so_bx), channel_id=1, source_target_pairs={{0,224},{32,64},{64,32},{96,128},{128,96},{160,192},{192,160},{224... | collective-permute-start | bytes 147464 | tf_op jit(solution)/shard_map/ppermute | solution.py:567
  7.7 7.2 %collective-permute-start.2 = (f32[11,8,128]{2,1,0:T(8,128)S(1)}, f32[11,8,128]{2,1,0:T(8,128)S(1)}, u32[]{:S(2)}, u32[]{:S(2)}) collective-permute-start(f32[11,8,128]{2,1,0:T(8,128)S(1)} %get-tuple-element.29.se_by), channel_id=1, source_target_pairs={{0,1},{1,0},{2,3},{3,2},{4,5},{5,4},{6,7},{7,6},{8,9},{9,8},{10,11... | collective-permute-start | bytes 135176 | tf_op jit(solution)/shard_map/ppermute | solution.py:568
  12.6 2.3 %collective-permute-start = (f32[10,8,128]{2,1,0:T(8,128)S(1)}, f32[10,8,128]{2,1,0:T(8,128)S(1)}, u32[]{:S(2)}, u32[]{:S(2)}) collective-permute-start(f32[10,8,128]{2,1,0:T(8,128)S(1)} %get-tuple-element.27.se_bx), channel_id=1, source_target_pairs={{0,32},{32,0},{64,96},{96,64},{128,160},{160,128},{192,224},{224,1... | collective-permute-start | bytes 122888 | tf_op jit(solution)/shard_map/ppermute | solution.py:566
  16.0 8.1 %collective-permute-start.5 = (f32[2,5,2,2,8,128]{5,4,3,2,1,0:T(8,128)S(1)}, f32[2,5,2,2,8,128]{5,4,3,2,1,0:T(8,128)S(1)}, u32[]{:S(2)}, u32[]{:S(2)}) collective-permute-start(f32[2,5,2,2,8,128]{5,4,3,2,1,0:T(8,128)S(1)} %get-tuple-element.36), channel_id=1, source_target_pairs={{0,1},{1,0},{2,3},{3,2},{4,5},{5,4},{6,7},{7,6},{8,9},{9,8},{10,11... | collective-permute-start | bytes 491528 | tf_op jit(solution)/shard_map/ppermute | solution.py:585
  17.8 16.8 %all-to-all-start = ((f32[64,3,1,128]{3,2,1,0:T(1,128)}), f32[64,3,1,128]{3,2,1,0:T(1,128)S(1)}, u32[]{:S(2)}, u32[]{:S(2)}) async-start(f32[64,3,1,128]{3,2,1,0:T(1,128)} %bitcast.3), calls=%async_computation | async-start | bytes 196608 | tf_op jit(solution)/shard_map/all_to_all | solution.py:588
  24.1 6.6 %collective-permute-start.6 = (f32[5,2,2,8,128]{4,3,2,1,0:T(8,128)S(1)}, f32[5,2,2,8,128]{4,3,2,1,0:T(8,128)S(1)}, u32[]{:S(2)}, u32[]{:S(2)}) collective-permute-start(f32[5,2,2,8,128]{4,3,2,1,0:T(8,128)S(1)} %get-tuple-element.37), channel_id=1, source_target_pairs={{0,2},{1,3},{2,0},{3,1},{4,6},{5,7},{6,4},{7,5},{8,10},{9,11},{10,... | collective-permute-start | bytes 245768 | tf_op jit(solution)/shard_map/ppermute | solution.py:585
  25.7 6.8 %collective-permute-start.7 = (f32[5,2,2,8,128]{4,3,2,1,0:T(8,128)S(1)}, f32[5,2,2,8,128]{4,3,2,1,0:T(8,128)S(1)}, u32[]{:S(2)}, u32[]{:S(2)}) collective-permute-start(f32[5,2,2,8,128]{4,3,2,1,0:T(8,128)S(1)} %get-tuple-element.38), channel_id=1, source_target_pairs={{0,2},{1,3},{2,0},{3,1},{4,6},{5,7},{6,4},{7,5},{8,10},{9,11},{10,... | collective-permute-start | bytes 245768 | tf_op jit(solution)/shard_map/ppermute | solution.py:585
  30.7 5.1 %collective-permute-start.8 = (f32[5,2,2,8,128]{4,3,2,1,0:T(8,128)S(1)}, f32[5,2,2,8,128]{4,3,2,1,0:T(8,128)S(1)}, u32[]{:S(2)}, u32[]{:S(2)}) collective-permute-start(f32[5,2,2,8,128]{4,3,2,1,0:T(8,128)S(1)} %shard_map.42), channel_id=1, source_target_pairs={{0,4},{1,5},{2,6},{3,7},{4,0},{5,1},{6,2},{7,3},{8,12},{9,13},{10,... | collective-permute-start | bytes 245768 | tf_op jit(solution)/shard_map/ppermute | solution.py:585
  32.6 4.5 %collective-permute-start.9 = (f32[5,2,2,8,128]{4,3,2,1,0:T(8,128)S(1)}, f32[5,2,2,8,128]{4,3,2,1,0:T(8,128)S(1)}, u32[]{:S(2)}, u32[]{:S(2)}) collective-permute-start(f32[5,2,2,8,128]{4,3,2,1,0:T(8,128)S(1)} %shard_map.43), channel_id=1, source_target_pairs={{0,4},{1,5},{2,6},{3,7},{4,0},{5,1},{6,2},{7,3},{8,12},{9,13},{10,... | collective-permute-start | bytes 245768 | tf_op jit(solution)/shard_map/ppermute | solution.py:585

commit v8 on v7

--- a/solution.py
+++ b/solution.py
@@ -36,7 +36,8 @@
 
 
 def root(x):
-    return x * lax.rsqrt(jnp.maximum(x, SMALL))
+    x = jnp.maximum(x, SMALL)
+    return x * lax.rsqrt(x)
 
 
 def half_minmod(a, b):
@@ -557,9 +558,9 @@
         prep_kernel,
         [conserved.reshape(5, 256, 64)],
         [BLOCKS] * 2
-        + [(10,) + TILE, (12,) + TILE, (11,) + TILE, (14,) + TILE]
+        + [(10,) + TILE, (13,) + TILE, (11,) + TILE, (14,) + TILE]
         + [face] * 2
-        + [(13,) + TILE],
+        + [(12,) + TILE],
     )
     e_bx, o_bx, e_by, o_by = slabs[:4]
     got_slabs = [

time: 38.5 us -> 38.3 us (level)
    all_to_all x1, starting transfers between devices: 6.27 us -> 4.84 us  [on_device(): top = lax.all_to_all(top, ('bx', 'by'), 0, 0, axis_index_groups=groups)]
    ppermute x5, starting transfers between devices: 8.27 us -> 9.61 us  [on_device(): lax.ppermute(block, 'by', [(k, k ^ m) for k in range(columns)])]
  transfers between devices with their start and end apart: 11 -> 11, of which waited for: 4 -> 5; matrix products, arithmetic and copies ran while one was open for 0% -> 0% of each run, Pallas kernels for 9% -> 9%
where the time goes in v8:
time: 38.3 us; the launch traced here: 37.9 us
  starting transfers between devices  25.3 us (66%)
  Pallas kernels  5.93 us (15%)
  waiting for transfers between devices  5.48 us (14%)
  local copies, waits for them, and re-layouts  1.1 us (3%)
    ppermute x5, starting transfers between devices, on_device(): lax.ppermute(block, 'by', [(k, k ^ m) for k in range(columns)])  9.61 us
    pallas_call x8, Pallas kernels, call(): pl.pallas_call(kernel, in_specs=[VMEM] * (len(inputs) - hbm_in) + [ANY] *...  5.93 us
    all_to_all x1, starting transfers between devices, on_device(): top = lax.all_to_all(top, ('bx', 'by'), 0, 0, axis_index_groups=groups)  4.84 us
    ppermute x1, starting transfers between devices, on_device(): lax.ppermute(e_by, 'by', pair_even(columns))  4.63 us
    ppermute x5, waiting for transfers between devices, on_device(): lax.ppermute(block, 'by', [(k, k ^ m) for k in range(columns)])  4.37 us
    ppermute x1, starting transfers between devices, on_device(): lax.ppermute(slabs[-1], 'by', [(k, k ^ 2) for k in range(columns)])  2.47 us
    ppermute x1, starting transfers between devices, on_device(): lax.ppermute(o_bx, 'bx', pair_odd(rows))  2.17 us
    ppermute x1, starting transfers between devices, on_device(): lax.ppermute(o_by, 'by', pair_odd(columns))  1.58 us
  transfers between devices with their start and end apart: 11, of which 5 were waited for; matrix products, arithmetic and copies ran while one was open for 0% of the time, Pallas kernels for 9%

profile of v8, /device:TPU:2, one launch (start us, length us, event | category | flops | bytes accessed | tf_op | source)
XLA Modules:
  0.0 37.9 jit_solution(7848445983967277894)
XLA Ops:
  0.0 0.0 copy-start
  0.0 1.1 %copy-done = f32[5,16,16,64]{3,2,1,0:T(8,128)S(1)} copy-done((f32[5,16,16,64]{3,2,1,0:T(8,128)S(1)}, f32[5,16,16,64]{3,2,1,0:T(8,128)}, u32[]{:S(2)}) %copy-start) | copy-done | bytes 327704
  1.1 0.0 copy-start.1
  1.1 0.6 %shard_map.37 = (f32[4,5,2,2,8,128]{5,4,3,2,1,0:T(8,128)S(1)}, f32[4,5,2,2,8,128]{5,4,3,2,1,0:T(8,128)S(1)}, f32[10,8,128]{2,1,0:T(8,128)S(1)}, f32[13,8,128]{2,...) custom-call(f32[5,256,64]{2,1,0:T(8,128)S(1)} %bitcast.6), custom_call_target="tpu_custom_call" | custom-call | tf_op jit(solution)/shard_map/pallas_call | solution.py:541
  1.7 0.0 copy-start.2
  1.7 1.6 %collective-permute-start.3 = (f32[14,8,128]{2,1,0:T(8,128)S(1)}, f32[14,8,128]{2,1,0:T(8,128)S(1)}, u32[]{:S(2)}, u32[]{:S(2)}) collective-permute-start(f32[14,8,128]{2,1,0:T(8,128)S(1)} %get-tuple-element.30.so_by), channel_id=1, source_target_pairs={{0,31},{1,2},{2,1},{3,4},{4,3},{5,6},{6,5},{7,8},{8,7},{9,10},{10,... | collective-permute-start | bytes 172040 | tf_op jit(solution)/shard_map/ppermute | solution.py:570
  3.3 2.2 %collective-permute-start.1 = (f32[13,8,128]{2,1,0:T(8,128)S(1)}, f32[13,8,128]{2,1,0:T(8,128)S(1)}, u32[]{:S(2)}, u32[]{:S(2)}) collective-permute-start(f32[13,8,128]{2,1,0:T(8,128)S(1)} %get-tuple-element.28.so_bx), channel_id=1, source_target_pairs={{0,224},{32,64},{64,32},{96,128},{128,96},{160,192},{192,160},{224... | collective-permute-start | bytes 159752 | tf_op jit(solution)/shard_map/ppermute | solution.py:568
  5.5 2.5 %collective-permute-start.4 = (f32[12,8,128]{2,1,0:T(8,128)S(1)}, f32[12,8,128]{2,1,0:T(8,128)S(1)}, u32[]{:S(2)}, u32[]{:S(2)}) collective-permute-start(f32[12,8,128]{2,1,0:T(8,128)S(1)} %get-tuple-element.33.top), channel_id=1, source_target_pairs={{0,2},{1,3},{2,0},{3,1},{4,6},{5,7},{6,4},{7,5},{8,10},{9,11},{10,... | collective-permute-start | bytes 147464 | tf_op jit(solution)/shard_map/ppermute | solution.py:571
  8.0 4.6 %collective-permute-start.2 = (f32[11,8,128]{2,1,0:T(8,128)S(1)}, f32[11,8,128]{2,1,0:T(8,128)S(1)}, u32[]{:S(2)}, u32[]{:S(2)}) collective-permute-start(f32[11,8,128]{2,1,0:T(8,128)S(1)} %get-tuple-element.29.se_by), channel_id=1, source_target_pairs={{0,1},{1,0},{2,3},{3,2},{4,5},{5,4},{6,7},{7,6},{8,9},{9,8},{10,11... | collective-permute-start | bytes 135176 | tf_op jit(solution)/shard_map/ppermute | solution.py:569
  12.6 0.0 collective-permute-start
  12.6 0.0 copy-done.1
  12.6 0.0 copy-done.2
  12.6 2.3 %shard_map.38 = (f32[4,5,2,2,8,128]{5,4,3,2,1,0:T(8,128)S(1)}, s32[24,128]{1,0:T(8,128)S(1)}) custom-call(s32[3,8,32]{2,1,0:T(8,128)S(1)} %bitcast.9, s32[8,4,32]{2,1,0:T(4,128)S(1)} %bitcast.8, f32[4,5,2,2,8,128]{5,4,3,2,1,0:T(8,128)S(1)} %get-tuple-element.23.w), custom_call_target="tpu_custom_call" | custom-call | tf_op jit(solution)/shard_map/pallas_call | solution.py:541
  14.9 0.0 collective-permute-done.re_bx
  14.9 0.2 collective-permute-done.2.re_by
  15.1 0.0 collective-permute-done.4.top2
  15.1 0.0 collective-permute-done.1.ro_bx
  15.1 0.0 collective-permute-done.3.ro_by
  15.1 1.0 %shard_map.39 = (f32[4,5,2,2,8,128]{5,4,3,2,1,0:T(8,128)S(1)}, f32[2,5,2,2,8,128]{5,4,3,2,1,0:T(8,128)S(1)}, f32[24,8,128]{2,1,0:T(8,128)}) custom-call(s32[24,128]{1,0:T(8,128)S(1)} %get-tuple-element.24.plan, f32[4,5,2,2,8,128]{5,4,3,2,1,0:T(8,128)S(1)} %get-tuple-element.25.u.own, f32[4,5,2,2,8,128]{5,4,3,2,1,0:T(8,128)S(1)} %get-tuple-element.26.d_in, ...), custom_call_target="tpu_custom_call" | custom-call | tf_op jit(solution)/shard_map/pallas_call | solution.py:541
  16.2 3.1 %collective-permute-start.5 = (f32[2,5,2,2,8,128]{5,4,3,2,1,0:T(8,128)S(1)}, f32[2,5,2,2,8,128]{5,4,3,2,1,0:T(8,128)S(1)}, u32[]{:S(2)}, u32[]{:S(2)}) collective-permute-start(f32[2,5,2,2,8,128]{5,4,3,2,1,0:T(8,128)S(1)} %get-tuple-element.36), channel_id=1, source_target_pairs={{0,1},{1,0},{2,3},{3,2},{4,5},{5,4},{6,7},{7,6},{8,9},{9,8},{10,11... | collective-permute-start | bytes 491528 | tf_op jit(solution)/shard_map/ppermute | solution.py:586
  19.3 4.8 %all-to-all-start = ((f32[64,3,1,128]{3,2,1,0:T(1,128)}), f32[64,3,1,128]{3,2,1,0:T(1,128)S(1)}, u32[]{:S(2)}, u32[]{:S(2)}) async-start(f32[64,3,1,128]{3,2,1,0:T(1,128)} %bitcast.3), calls=%async_computation | async-start | bytes 196608 | tf_op jit(solution)/shard_map/all_to_all | solution.py:589
  24.1 0.0 collective-permute-done.5.got1
  24.1 0.1 shard_map.40
  24.2 1.6 %collective-permute-start.6 = (f32[5,2,2,8,128]{4,3,2,1,0:T(8,128)S(1)}, f32[5,2,2,8,128]{4,3,2,1,0:T(8,128)S(1)}, u32[]{:S(2)}, u32[]{:S(2)}) collective-permute-start(f32[5,2,2,8,128]{4,3,2,1,0:T(8,128)S(1)} %get-tuple-element.37), channel_id=1, source_target_pairs={{0,2},{1,3},{2,0},{3,1},{4,6},{5,7},{6,4},{7,5},{8,10},{9,11},{10,... | collective-permute-start | bytes 245768 | tf_op jit(solution)/shard_map/ppermute | solution.py:586
  25.8 2.0 %collective-permute-start.7 = (f32[5,2,2,8,128]{4,3,2,1,0:T(8,128)S(1)}, f32[5,2,2,8,128]{4,3,2,1,0:T(8,128)S(1)}, u32[]{:S(2)}, u32[]{:S(2)}) collective-permute-start(f32[5,2,2,8,128]{4,3,2,1,0:T(8,128)S(1)} %get-tuple-element.38), channel_id=1, source_target_pairs={{0,2},{1,3},{2,0},{3,1},{4,6},{5,7},{6,4},{7,5},{8,10},{9,11},{10,... | collective-permute-start | bytes 245768 | tf_op jit(solution)/shard_map/ppermute | solution.py:586
  27.8 3.0 %collective-permute-done.6.got_u.got2 = f32[5,2,2,8,128]{4,3,2,1,0:T(8,128)S(1)} collective-permute-done((f32[5,2,2,8,128]{4,3,2,1,0:T(8,128)S(1)}, f32[5,2,2,8,128]{4,3,2,1,0:T(8,128)S(1)}, u32[]{:S(2)}, u32[]{:S(2)}) %collective-permute-start.6) | collective-permute-done | bytes 81952 | tf_op jit(solution)/shard_map/ppermute | solution.py:586
  30.8 0.1 shard_map.42
  30.8 1.8 %collective-permute-start.8 = (f32[5,2,2,8,128]{4,3,2,1,0:T(8,128)S(1)}, f32[5,2,2,8,128]{4,3,2,1,0:T(8,128)S(1)}, u32[]{:S(2)}, u32[]{:S(2)}) collective-permute-start(f32[5,2,2,8,128]{4,3,2,1,0:T(8,128)S(1)} %shard_map.42), channel_id=1, source_target_pairs={{0,4},{1,5},{2,6},{3,7},{4,0},{5,1},{6,2},{7,3},{8,12},{9,13},{10,... | collective-permute-start | bytes 245768 | tf_op jit(solution)/shard_map/ppermute | solution.py:586
  32.6 0.0 collective-permute-done.7.got_d.got2
  32.6 0.1 shard_map.43
  32.7 1.1 %collective-permute-start.9 = (f32[5,2,2,8,128]{4,3,2,1,0:T(8,128)S(1)}, f32[5,2,2,8,128]{4,3,2,1,0:T(8,128)S(1)}, u32[]{:S(2)}, u32[]{:S(2)}) collective-permute-start(f32[5,2,2,8,128]{4,3,2,1,0:T(8,128)S(1)} %shard_map.43), channel_id=1, source_target_pairs={{0,4},{1,5},{2,6},{3,7},{4,0},{5,1},{6,2},{7,3},{8,12},{9,13},{10,... | collective-permute-start | bytes 245768 | tf_op jit(solution)/shard_map/ppermute | solution.py:586
  33.8 0.9 %all-to-all-done = f32[64,3,1,128]{3,2,1,0:T(1,128)S(1)} async-done(((f32[64,3,1,128]{3,2,1,0:T(1,128)}), f32[64,3,1,128]{3,2,1,0:T(1,128)S(1)}, u32[]{:S(2)}, u32[]{:S(2)}) %all-to-all-start) | async-done | bytes 98336 | tf_op jit(solution)/shard_map/all_to_all | solution.py:589
  34.6 1.1 %shard_map.41 = (f32[8,128]{1,0:T(8,128)S(1)}, f32[4,5,16,256]{3,2,1,0:T(8,128)}) custom-call(s32[24,128]{1,0:T(8,128)S(1)} %get-tuple-element.24.plan, f32[4,5,2,2,8,128]{5,4,3,2,1,0:T(8,128)S(1)} %get-tuple-element.25.u.own, f32[4,5,2,2,8,128]{5,4,3,2,1,0:T(8,128)S(1)} %get-tuple-element.34.d.own, f32[24,8,128]{2,1,0:T(8,128)S(1)} %bitcast.7, ...), custom_call_target="tpu_custom_call" | custom-call | tf_op jit(solution)/shard_map/pallas_call | solution.py:541
  35.8 0.2 collective-permute-done.8.got_u
  35.9 1.3 %collective-permute-done.9.got_d = f32[5,2,2,8,128]{4,3,2,1,0:T(8,128)S(1)} collective-permute-done((f32[5,2,2,8,128]{4,3,2,1,0:T(8,128)S(1)}, f32[5,2,2,8,128]{4,3,2,1,0:T(8,128)S(1)}, u32[]{:S(2)}, u32[]{:S(2)}) %collective-permute-start.9) | collective-permute-done | bytes 81952 | tf_op jit(solution)/shard_map/ppermute | solution.py:586
  37.2 0.7 %shard_map.44 = f32[4,5,16,256]{3,2,1,0:T(8,128)} custom-call(s32[24,128]{1,0:T(8,128)S(1)} %get-tuple-element.24.plan, f32[8,128]{1,0:T(8,128)S(1)} %get-tuple-element.39.step, f32[5,2,2,8,128]{4,3,2,1,0:T(8,128)S(1)} %collective-permute-done.8.got_u, f32[5,2,2,8,128]{4,3,2,1,0:T(8,128)S(1)} %collective-permute-done.9.got_d, ...), custom_call_target="tpu_custom_call", output_to_operand_aliasing={{}: (4, {})} | custom-call | tf_op jit(solution)/shard_map/pallas_call | solution.py:541
Async XLA Ops:
  0.0 1.1 %copy-start = (f32[5,16,16,64]{3,2,1,0:T(8,128)S(1)}, f32[5,16,16,64]{3,2,1,0:T(8,128)}, u32[]{:S(2)}) copy-start(f32[5,16,16,64]{3,2,1,0:T(8,128)} %param.3) | copy-start | bytes 983044
  1.1 11.5 %copy-start.1 = (s32[8,32,4]{1,2,0:T(4,128)S(1)}, s32[8,32,4]{1,2,0:T(4,128)}, u32[]{:S(2)}) copy-start(s32[8,32,4]{1,2,0:T(4,128)} %param.4) | copy-start | bytes 12292
  1.7 10.9 %copy-start.2 = (s32[8,32,3]{1,0,2:T(8,128)S(1)}, s32[8,32,3]{1,0,2:T(8,128)}, u32[]{:S(2)}) copy-start(s32[8,32,3]{1,0,2:T(8,128)} %param.5) | copy-start | bytes 9220
  1.7 13.4 %collective-permute-start.3 = (f32[14,8,128]{2,1,0:T(8,128)S(1)}, f32[14,8,128]{2,1,0:T(8,128)S(1)}, u32[]{:S(2)}, u32[]{:S(2)}) collective-permute-start(f32[14,8,128]{2,1,0:T(8,128)S(1)} %get-tuple-element.30.so_by), channel_id=1, source_target_pairs={{0,31},{1,2},{2,1},{3,4},{4,3},{5,6},{6,5},{7,8},{8,7},{9,10},{10,... | collective-permute-start | bytes 172040 | tf_op jit(solution)/shard_map/ppermute | solution.py:570
  3.3 11.8 %collective-permute-start.1 = (f32[13,8,128]{2,1,0:T(8,128)S(1)}, f32[13,8,128]{2,1,0:T(8,128)S(1)}, u32[]{:S(2)}, u32[]{:S(2)}) collective-permute-start(f32[13,8,128]{2,1,0:T(8,128)S(1)} %get-tuple-element.28.so_bx), channel_id=1, source_target_pairs={{0,224},{32,64},{64,32},{96,128},{128,96},{160,192},{192,160},{224... | collective-permute-start | bytes 159752 | tf_op jit(solution)/shard_map/ppermute | solution.py:568
  5.5 9.6 %collective-permute-start.4 = (f32[12,8,128]{2,1,0:T(8,128)S(1)}, f32[12,8,128]{2,1,0:T(8,128)S(1)}, u32[]{:S(2)}, u32[]{:S(2)}) collective-permute-start(f32[12,8,128]{2,1,0:T(8,128)S(1)} %get-tuple-element.33.top), channel_id=1, source_target_pairs={{0,2},{1,3},{2,0},{3,1},{4,6},{5,7},{6,4},{7,5},{8,10},{9,11},{10,... | collective-permute-start | bytes 147464 | tf_op jit(solution)/shard_map/ppermute | solution.py:571
  8.0 7.2 %collective-permute-start.2 = (f32[11,8,128]{2,1,0:T(8,128)S(1)}, f32[11,8,128]{2,1,0:T(8,128)S(1)}, u32[]{:S(2)}, u32[]{:S(2)}) collective-permute-start(f32[11,8,128]{2,1,0:T(8,128)S(1)} %get-tuple-element.29.se_by), channel_id=1, source_target_pairs={{0,1},{1,0},{2,3},{3,2},{4,5},{5,4},{6,7},{7,6},{8,9},{9,8},{10,11... | collective-permute-start | bytes 135176 | tf_op jit(solution)/shard_map/ppermute | solution.py:569
  12.6 2.3 %collective-permute-start = (f32[10,8,128]{2,1,0:T(8,128)S(1)}, f32[10,8,128]{2,1,0:T(8,128)S(1)}, u32[]{:S(2)}, u32[]{:S(2)}) collective-permute-start(f32[10,8,128]{2,1,0:T(8,128)S(1)} %get-tuple-element.27.se_bx), channel_id=1, source_target_pairs={{0,32},{32,0},{64,96},{96,64},{128,160},{160,128},{192,224},{224,1... | collective-permute-start | bytes 122888 | tf_op jit(solution)/shard_map/ppermute | solution.py:567
  16.2 8.0 %collective-permute-start.5 = (f32[2,5,2,2,8,128]{5,4,3,2,1,0:T(8,128)S(1)}, f32[2,5,2,2,8,128]{5,4,3,2,1,0:T(8,128)S(1)}, u32[]{:S(2)}, u32[]{:S(2)}) collective-permute-start(f32[2,5,2,2,8,128]{5,4,3,2,1,0:T(8,128)S(1)} %get-tuple-element.36), channel_id=1, source_target_pairs={{0,1},{1,0},{2,3},{3,2},{4,5},{5,4},{6,7},{7,6},{8,9},{9,8},{10,11... | collective-permute-start | bytes 491528 | tf_op jit(solution)/shard_map/ppermute | solution.py:586
  19.3 15.4 %all-to-all-start = ((f32[64,3,1,128]{3,2,1,0:T(1,128)}), f32[64,3,1,128]{3,2,1,0:T(1,128)S(1)}, u32[]{:S(2)}, u32[]{:S(2)}) async-start(f32[64,3,1,128]{3,2,1,0:T(1,128)} %bitcast.3), calls=%async_computation | async-start | bytes 196608 | tf_op jit(solution)/shard_map/all_to_all | solution.py:589
  24.2 6.6 %collective-permute-start.6 = (f32[5,2,2,8,128]{4,3,2,1,0:T(8,128)S(1)}, f32[5,2,2,8,128]{4,3,2,1,0:T(8,128)S(1)}, u32[]{:S(2)}, u32[]{:S(2)}) collective-permute-start(f32[5,2,2,8,128]{4,3,2,1,0:T(8,128)S(1)} %get-tuple-element.37), channel_id=1, source_target_pairs={{0,2},{1,3},{2,0},{3,1},{4,6},{5,7},{6,4},{7,5},{8,10},{9,11},{10,... | collective-permute-start | bytes 245768 | tf_op jit(solution)/shard_map/ppermute | solution.py:586
  25.8 6.8 %collective-permute-start.7 = (f32[5,2,2,8,128]{4,3,2,1,0:T(8,128)S(1)}, f32[5,2,2,8,128]{4,3,2,1,0:T(8,128)S(1)}, u32[]{:S(2)}, u32[]{:S(2)}) collective-permute-start(f32[5,2,2,8,128]{4,3,2,1,0:T(8,128)S(1)} %get-tuple-element.38), channel_id=1, source_target_pairs={{0,2},{1,3},{2,0},{3,1},{4,6},{5,7},{6,4},{7,5},{8,10},{9,11},{10,... | collective-permute-start | bytes 245768 | tf_op jit(solution)/shard_map/ppermute | solution.py:586
  30.8 5.1 %collective-permute-start.8 = (f32[5,2,2,8,128]{4,3,2,1,0:T(8,128)S(1)}, f32[5,2,2,8,128]{4,3,2,1,0:T(8,128)S(1)}, u32[]{:S(2)}, u32[]{:S(2)}) collective-permute-start(f32[5,2,2,8,128]{4,3,2,1,0:T(8,128)S(1)} %shard_map.42), channel_id=1, source_target_pairs={{0,4},{1,5},{2,6},{3,7},{4,0},{5,1},{6,2},{7,3},{8,12},{9,13},{10,... | collective-permute-start | bytes 245768 | tf_op jit(solution)/shard_map/ppermute | solution.py:586
  32.7 4.5 %collective-permute-start.9 = (f32[5,2,2,8,128]{4,3,2,1,0:T(8,128)S(1)}, f32[5,2,2,8,128]{4,3,2,1,0:T(8,128)S(1)}, u32[]{:S(2)}, u32[]{:S(2)}) collective-permute-start(f32[5,2,2,8,128]{4,3,2,1,0:T(8,128)S(1)} %shard_map.43), channel_id=1, source_target_pairs={{0,4},{1,5},{2,6},{3,7},{4,0},{5,1},{6,2},{7,3},{8,12},{9,13},{10,... | collective-permute-start | bytes 245768 | tf_op jit(solution)/shard_map/ppermute | solution.py:586

commit v9 on v8

--- a/solution.py
+++ b/solution.py
@@ -17,7 +17,6 @@
 HALF = (5, 2, 2) + TILE
 VMEM = pl.BlockSpec(memory_space=pltpu.VMEM)
 ANY = pl.BlockSpec(memory_space=pl.ANY)
-PARAMS = pltpu.CompilerParams(vmem_limit_bytes=16 * 1024 * 1024)
 PLAN = jax.ShapeDtypeStruct((24, 128), jnp.int32)
 BIG = 3e38
 SMALL = 1e-37
@@ -80,8 +79,16 @@
 
 
 def prep_kernel(
-    cons, u_out, w_out, e_bx, o_bx, e_by, o_by, in_bx, in_by, top_out
+    source, u_out, w_out, e_bx, o_bx, e_by, o_by, in_bx, in_by, top_out, cons, arrived
 ):
+    copies = []
+    for at in range(2):
+        for f in range(5):
+            place = (f, pl.ds(at * 128, 128))
+            copies.append(
+                pltpu.make_async_copy(source.at[place], cons.at[place], arrived.at[at, f])
+            )
+            copies[-1].start()
     even_i = lax.axis_index("bx") % 2 == 0
     even_j = lax.axis_index("by") % 2 == 0
     lane = iota(1)
@@ -90,6 +97,8 @@
     row = iota(0)
     top = jnp.zeros(TILE, F32)
     for at in range(2):
+        for copy in copies[at * 5 : at * 5 + 5]:
+            copy.wait()
         low, high, inner = [], [], []
         for h in range(2):
             tiles = []
@@ -537,14 +546,14 @@
     return [(k, (k + 1) % count if k % 2 else (k - 1) % count) for k in range(count)]
 
 
-def call(kernel, inputs, outputs, scratch=(), hbm_in=0, hbm_out=0, plan=0, aliases=None):
+def call(kernel, inputs, outputs, scratch=(), hbm_in=0, hbm_out=0, plan=0, aliases=None, room=16):
     return pl.pallas_call(
         kernel,
         in_specs=[VMEM] * (len(inputs) - hbm_in) + [ANY] * hbm_in,
         out_specs=[VMEM] * (len(outputs) - hbm_out) + [ANY] * hbm_out + [VMEM] * plan,
         out_shape=[shape(*dims) for dims in outputs] + [PLAN] * plan,
         scratch_shapes=[pltpu.VMEM(x, F32) if isinstance(x, tuple) else x for x in scratch],
-        compiler_params=PARAMS,
+        compiler_params=pltpu.CompilerParams(vmem_limit_bytes=room * 2**20),
         input_output_aliases=aliases or {},
     )(*inputs)
 
@@ -561,6 +570,9 @@
         + [(10,) + TILE, (13,) + TILE, (11,) + TILE, (14,) + TILE]
         + [face] * 2
         + [(12,) + TILE],
+        [(5, 256, 64), pltpu.SemaphoreType.DMA((2, 5))],
+        hbm_in=1,
+        room=53,
     )
     e_bx, o_bx, e_by, o_by = slabs[:4]
     got_slabs = [

time: 38.3 us -> 38.2 us (level)
  local copies, waits for them, and re-layouts: 1.1 us -> 0.01 us
  Pallas kernels: 5.93 us -> 6.96 us
    unnamed x6 -> x4, local copies, waits for them, and re-layouts: 1.1 us -> 0.01 us
    pallas_call x8, Pallas kernels: 5.93 us -> 6.96 us  [call(): pl.pallas_call(kernel, in_specs=[VMEM] * (len(inputs) - hbm_in) + [ANY] *...]
where the time goes in v9:
time: 38.2 us; the launch traced here: 37.9 us
  starting transfers between devices  25.3 us (66%)
  Pallas kernels  6.96 us (18%)
  waiting for transfers between devices  5.51 us (14%)
    ppermute x5, starting transfers between devices, on_device(): lax.ppermute(block, 'by', [(k, k ^ m) for k in range(columns)])  9.61 us
    pallas_call x8, Pallas kernels, call(): pl.pallas_call(kernel, in_specs=[VMEM] * (len(inputs) - hbm_in) + [ANY] *...  6.96 us
    all_to_all x1, starting transfers between devices, on_device(): top = lax.all_to_all(top, ('bx', 'by'), 0, 0, axis_index_groups=groups)  4.84 us
    ppermute x1, starting transfers between devices, on_device(): lax.ppermute(e_by, 'by', pair_even(columns))  4.63 us
    ppermute x5, waiting for transfers between devices, on_device(): lax.ppermute(block, 'by', [(k, k ^ m) for k in range(columns)])  4.4 us
    ppermute x1, starting transfers between devices, on_device(): lax.ppermute(slabs[-1], 'by', [(k, k ^ 2) for k in range(columns)])  2.47 us
    ppermute x1, starting transfers between devices, on_device(): lax.ppermute(o_bx, 'bx', pair_odd(rows))  2.17 us
    ppermute x1, starting transfers between devices, on_device(): lax.ppermute(o_by, 'by', pair_odd(columns))  1.58 us
  transfers between devices with their start and end apart: 11, of which 5 were waited for; matrix products, arithmetic and copies ran while one was open for 0% of the time, Pallas kernels for 9%

profile of v9, /device:TPU:2, one launch (start us, length us, event | category | flops | bytes accessed | tf_op | source)
XLA Modules:
  0.0 37.9 jit_solution(1338749207452238843)
XLA Ops:
  0.0 0.0 copy-start
  0.0 1.6 %shard_map.37 = (f32[4,5,2,2,8,128]{5,4,3,2,1,0:T(8,128)S(1)}, f32[4,5,2,2,8,128]{5,4,3,2,1,0:T(8,128)S(1)}, f32[10,8,128]{2,1,0:T(8,128)S(1)}, f32[13,8,128]{2,...) custom-call(f32[5,256,64]{2,1,0:T(8,128)} %bitcast.9), custom_call_target="tpu_custom_call" | custom-call | tf_op jit(solution)/shard_map/pallas_call | solution.py:550
  1.6 0.0 copy-start.1
  1.7 1.6 %collective-permute-start.3 = (f32[14,8,128]{2,1,0:T(8,128)S(1)}, f32[14,8,128]{2,1,0:T(8,128)S(1)}, u32[]{:S(2)}, u32[]{:S(2)}) collective-permute-start(f32[14,8,128]{2,1,0:T(8,128)S(1)} %get-tuple-element.30.so_by), channel_id=1, source_target_pairs={{0,31},{1,2},{2,1},{3,4},{4,3},{5,6},{6,5},{7,8},{8,7},{9,10},{10,... | collective-permute-start | bytes 172040 | tf_op jit(solution)/shard_map/ppermute | solution.py:582
  3.2 2.2 %collective-permute-start.1 = (f32[13,8,128]{2,1,0:T(8,128)S(1)}, f32[13,8,128]{2,1,0:T(8,128)S(1)}, u32[]{:S(2)}, u32[]{:S(2)}) collective-permute-start(f32[13,8,128]{2,1,0:T(8,128)S(1)} %get-tuple-element.28.so_bx), channel_id=1, source_target_pairs={{0,224},{32,64},{64,32},{96,128},{128,96},{160,192},{192,160},{224... | collective-permute-start | bytes 159752 | tf_op jit(solution)/shard_map/ppermute | solution.py:580
  5.4 2.5 %collective-permute-start.4 = (f32[12,8,128]{2,1,0:T(8,128)S(1)}, f32[12,8,128]{2,1,0:T(8,128)S(1)}, u32[]{:S(2)}, u32[]{:S(2)}) collective-permute-start(f32[12,8,128]{2,1,0:T(8,128)S(1)} %get-tuple-element.33.top), channel_id=1, source_target_pairs={{0,2},{1,3},{2,0},{3,1},{4,6},{5,7},{6,4},{7,5},{8,10},{9,11},{10,... | collective-permute-start | bytes 147464 | tf_op jit(solution)/shard_map/ppermute | solution.py:583
  7.9 4.6 %collective-permute-start.2 = (f32[11,8,128]{2,1,0:T(8,128)S(1)}, f32[11,8,128]{2,1,0:T(8,128)S(1)}, u32[]{:S(2)}, u32[]{:S(2)}) collective-permute-start(f32[11,8,128]{2,1,0:T(8,128)S(1)} %get-tuple-element.29.se_by), channel_id=1, source_target_pairs={{0,1},{1,0},{2,3},{3,2},{4,5},{5,4},{6,7},{7,6},{8,9},{9,8},{10,11... | collective-permute-start | bytes 135176 | tf_op jit(solution)/shard_map/ppermute | solution.py:581
  12.5 0.0 collective-permute-start
  12.5 0.0 copy-done
  12.5 0.0 copy-done.1
  12.5 2.3 %shard_map.38 = (f32[4,5,2,2,8,128]{5,4,3,2,1,0:T(8,128)S(1)}, s32[24,128]{1,0:T(8,128)S(1)}) custom-call(s32[3,8,32]{2,1,0:T(8,128)S(1)} %bitcast.8, s32[8,4,32]{2,1,0:T(4,128)S(1)} %bitcast.7, f32[4,5,2,2,8,128]{5,4,3,2,1,0:T(8,128)S(1)} %get-tuple-element.23.w), custom_call_target="tpu_custom_call" | custom-call | tf_op jit(solution)/shard_map/pallas_call | solution.py:550
  14.8 0.0 collective-permute-done.re_bx
  14.8 0.2 collective-permute-done.2.re_by
  15.0 0.0 collective-permute-done.4.top2
  15.1 0.0 collective-permute-done.1.ro_bx
  15.1 0.0 collective-permute-done.3.ro_by
  15.1 1.0 %shard_map.39 = (f32[4,5,2,2,8,128]{5,4,3,2,1,0:T(8,128)S(1)}, f32[2,5,2,2,8,128]{5,4,3,2,1,0:T(8,128)S(1)}, f32[24,8,128]{2,1,0:T(8,128)}) custom-call(s32[24,128]{1,0:T(8,128)S(1)} %get-tuple-element.24.plan, f32[4,5,2,2,8,128]{5,4,3,2,1,0:T(8,128)S(1)} %get-tuple-element.25.u.own, f32[4,5,2,2,8,128]{5,4,3,2,1,0:T(8,128)S(1)} %get-tuple-element.26.d_in, ...), custom_call_target="tpu_custom_call" | custom-call | tf_op jit(solution)/shard_map/pallas_call | solution.py:550
  16.1 3.1 %collective-permute-start.5 = (f32[2,5,2,2,8,128]{5,4,3,2,1,0:T(8,128)S(1)}, f32[2,5,2,2,8,128]{5,4,3,2,1,0:T(8,128)S(1)}, u32[]{:S(2)}, u32[]{:S(2)}) collective-permute-start(f32[2,5,2,2,8,128]{5,4,3,2,1,0:T(8,128)S(1)} %get-tuple-element.36), channel_id=1, source_target_pairs={{0,1},{1,0},{2,3},{3,2},{4,5},{5,4},{6,7},{7,6},{8,9},{9,8},{10,11... | collective-permute-start | bytes 491528 | tf_op jit(solution)/shard_map/ppermute | solution.py:598
  19.2 4.8 %all-to-all-start = ((f32[64,3,1,128]{3,2,1,0:T(1,128)}), f32[64,3,1,128]{3,2,1,0:T(1,128)S(1)}, u32[]{:S(2)}, u32[]{:S(2)}) async-start(f32[64,3,1,128]{3,2,1,0:T(1,128)} %bitcast.3), calls=%async_computation | async-start | bytes 196608 | tf_op jit(solution)/shard_map/all_to_all | solution.py:601
  24.0 0.0 collective-permute-done.5.got1
  24.0 0.1 shard_map.40
  24.1 1.6 %collective-permute-start.6 = (f32[5,2,2,8,128]{4,3,2,1,0:T(8,128)S(1)}, f32[5,2,2,8,128]{4,3,2,1,0:T(8,128)S(1)}, u32[]{:S(2)}, u32[]{:S(2)}) collective-permute-start(f32[5,2,2,8,128]{4,3,2,1,0:T(8,128)S(1)} %get-tuple-element.37), channel_id=1, source_target_pairs={{0,2},{1,3},{2,0},{3,1},{4,6},{5,7},{6,4},{7,5},{8,10},{9,11},{10,... | collective-permute-start | bytes 245768 | tf_op jit(solution)/shard_map/ppermute | solution.py:598
  25.7 2.0 %collective-permute-start.7 = (f32[5,2,2,8,128]{4,3,2,1,0:T(8,128)S(1)}, f32[5,2,2,8,128]{4,3,2,1,0:T(8,128)S(1)}, u32[]{:S(2)}, u32[]{:S(2)}) collective-permute-start(f32[5,2,2,8,128]{4,3,2,1,0:T(8,128)S(1)} %get-tuple-element.38), channel_id=1, source_target_pairs={{0,2},{1,3},{2,0},{3,1},{4,6},{5,7},{6,4},{7,5},{8,10},{9,11},{10,... | collective-permute-start | bytes 245768 | tf_op jit(solution)/shard_map/ppermute | solution.py:598
  27.7 3.0 %collective-permute-done.6.got_u.got2 = f32[5,2,2,8,128]{4,3,2,1,0:T(8,128)S(1)} collective-permute-done((f32[5,2,2,8,128]{4,3,2,1,0:T(8,128)S(1)}, f32[5,2,2,8,128]{4,3,2,1,0:T(8,128)S(1)}, u32[]{:S(2)}, u32[]{:S(2)}) %collective-permute-start.6) | collective-permute-done | bytes 81952 | tf_op jit(solution)/shard_map/ppermute | solution.py:598
  30.7 0.1 shard_map.42
  30.7 1.8 %collective-permute-start.8 = (f32[5,2,2,8,128]{4,3,2,1,0:T(8,128)S(1)}, f32[5,2,2,8,128]{4,3,2,1,0:T(8,128)S(1)}, u32[]{:S(2)}, u32[]{:S(2)}) collective-permute-start(f32[5,2,2,8,128]{4,3,2,1,0:T(8,128)S(1)} %shard_map.42), channel_id=1, source_target_pairs={{0,4},{1,5},{2,6},{3,7},{4,0},{5,1},{6,2},{7,3},{8,12},{9,13},{10,... | collective-permute-start | bytes 245768 | tf_op jit(solution)/shard_map/ppermute | solution.py:598
  32.5 0.0 collective-permute-done.7.got_d.got2
  32.5 0.1 shard_map.43
  32.6 1.1 %collective-permute-start.9 = (f32[5,2,2,8,128]{4,3,2,1,0:T(8,128)S(1)}, f32[5,2,2,8,128]{4,3,2,1,0:T(8,128)S(1)}, u32[]{:S(2)}, u32[]{:S(2)}) collective-permute-start(f32[5,2,2,8,128]{4,3,2,1,0:T(8,128)S(1)} %shard_map.43), channel_id=1, source_target_pairs={{0,4},{1,5},{2,6},{3,7},{4,0},{5,1},{6,2},{7,3},{8,12},{9,13},{10,... | collective-permute-start | bytes 245768 | tf_op jit(solution)/shard_map/ppermute | solution.py:598
  33.7 0.9 %all-to-all-done = f32[64,3,1,128]{3,2,1,0:T(1,128)S(1)} async-done(((f32[64,3,1,128]{3,2,1,0:T(1,128)}), f32[64,3,1,128]{3,2,1,0:T(1,128)S(1)}, u32[]{:S(2)}, u32[]{:S(2)}) %all-to-all-start) | async-done | bytes 98336 | tf_op jit(solution)/shard_map/all_to_all | solution.py:601
  34.6 1.1 %shard_map.41 = (f32[8,128]{1,0:T(8,128)S(1)}, f32[4,5,16,256]{3,2,1,0:T(8,128)}) custom-call(s32[24,128]{1,0:T(8,128)S(1)} %get-tuple-element.24.plan, f32[4,5,2,2,8,128]{5,4,3,2,1,0:T(8,128)S(1)} %get-tuple-element.25.u.own, f32[4,5,2,2,8,128]{5,4,3,2,1,0:T(8,128)S(1)} %get-tuple-element.34.d.own, f32[24,8,128]{2,1,0:T(8,128)S(1)} %bitcast.6, ...), custom_call_target="tpu_custom_call" | custom-call | tf_op jit(solution)/shard_map/pallas_call | solution.py:550
  35.7 0.2 collective-permute-done.8.got_u
  35.8 1.3 %collective-permute-done.9.got_d = f32[5,2,2,8,128]{4,3,2,1,0:T(8,128)S(1)} collective-permute-done((f32[5,2,2,8,128]{4,3,2,1,0:T(8,128)S(1)}, f32[5,2,2,8,128]{4,3,2,1,0:T(8,128)S(1)}, u32[]{:S(2)}, u32[]{:S(2)}) %collective-permute-start.9) | collective-permute-done | bytes 81952 | tf_op jit(solution)/shard_map/ppermute | solution.py:598
  37.1 0.8 %shard_map.44 = f32[4,5,16,256]{3,2,1,0:T(8,128)} custom-call(s32[24,128]{1,0:T(8,128)S(1)} %get-tuple-element.24.plan, f32[8,128]{1,0:T(8,128)S(1)} %get-tuple-element.39.step, f32[5,2,2,8,128]{4,3,2,1,0:T(8,128)S(1)} %collective-permute-done.8.got_u, f32[5,2,2,8,128]{4,3,2,1,0:T(8,128)S(1)} %collective-permute-done.9.got_d, ...), custom_call_target="tpu_custom_call", output_to_operand_aliasing={{}: (4, {})} | custom-call | tf_op jit(solution)/shard_map/pallas_call | solution.py:550
Async XLA Ops:
  0.0 12.5 %copy-start = (s32[8,32,4]{1,2,0:T(4,128)S(1)}, s32[8,32,4]{1,2,0:T(4,128)}, u32[]{:S(2)}) copy-start(s32[8,32,4]{1,2,0:T(4,128)} %param.4) | copy-start | bytes 12292
  1.6 10.9 %copy-start.1 = (s32[8,32,3]{1,0,2:T(8,128)S(1)}, s32[8,32,3]{1,0,2:T(8,128)}, u32[]{:S(2)}) copy-start(s32[8,32,3]{1,0,2:T(8,128)} %param.5) | copy-start | bytes 9220
  1.7 13.4 %collective-permute-start.3 = (f32[14,8,128]{2,1,0:T(8,128)S(1)}, f32[14,8,128]{2,1,0:T(8,128)S(1)}, u32[]{:S(2)}, u32[]{:S(2)}) collective-permute-start(f32[14,8,128]{2,1,0:T(8,128)S(1)} %get-tuple-element.30.so_by), channel_id=1, source_target_pairs={{0,31},{1,2},{2,1},{3,4},{4,3},{5,6},{6,5},{7,8},{8,7},{9,10},{10,... | collective-permute-start | bytes 172040 | tf_op jit(solution)/shard_map/ppermute | solution.py:582
  3.2 11.8 %collective-permute-start.1 = (f32[13,8,128]{2,1,0:T(8,128)S(1)}, f32[13,8,128]{2,1,0:T(8,128)S(1)}, u32[]{:S(2)}, u32[]{:S(2)}) collective-permute-start(f32[13,8,128]{2,1,0:T(8,128)S(1)} %get-tuple-element.28.so_bx), channel_id=1, source_target_pairs={{0,224},{32,64},{64,32},{96,128},{128,96},{160,192},{192,160},{224... | collective-permute-start | bytes 159752 | tf_op jit(solution)/shard_map/ppermute | solution.py:580
  5.4 9.6 %collective-permute-start.4 = (f32[12,8,128]{2,1,0:T(8,128)S(1)}, f32[12,8,128]{2,1,0:T(8,128)S(1)}, u32[]{:S(2)}, u32[]{:S(2)}) collective-permute-start(f32[12,8,128]{2,1,0:T(8,128)S(1)} %get-tuple-element.33.top), channel_id=1, source_target_pairs={{0,2},{1,3},{2,0},{3,1},{4,6},{5,7},{6,4},{7,5},{8,10},{9,11},{10,... | collective-permute-start | bytes 147464 | tf_op jit(solution)/shard_map/ppermute | solution.py:583
  7.9 7.2 %collective-permute-start.2 = (f32[11,8,128]{2,1,0:T(8,128)S(1)}, f32[11,8,128]{2,1,0:T(8,128)S(1)}, u32[]{:S(2)}, u32[]{:S(2)}) collective-permute-start(f32[11,8,128]{2,1,0:T(8,128)S(1)} %get-tuple-element.29.se_by), channel_id=1, source_target_pairs={{0,1},{1,0},{2,3},{3,2},{4,5},{5,4},{6,7},{7,6},{8,9},{9,8},{10,11... | collective-permute-start | bytes 135176 | tf_op jit(solution)/shard_map/ppermute | solution.py:581
  12.5 2.3 %collective-permute-start = (f32[10,8,128]{2,1,0:T(8,128)S(1)}, f32[10,8,128]{2,1,0:T(8,128)S(1)}, u32[]{:S(2)}, u32[]{:S(2)}) collective-permute-start(f32[10,8,128]{2,1,0:T(8,128)S(1)} %get-tuple-element.27.se_bx), channel_id=1, source_target_pairs={{0,32},{32,0},{64,96},{96,64},{128,160},{160,128},{192,224},{224,1... | collective-permute-start | bytes 122888 | tf_op jit(solution)/shard_map/ppermute | solution.py:579
  16.1 8.0 %collective-permute-start.5 = (f32[2,5,2,2,8,128]{5,4,3,2,1,0:T(8,128)S(1)}, f32[2,5,2,2,8,128]{5,4,3,2,1,0:T(8,128)S(1)}, u32[]{:S(2)}, u32[]{:S(2)}) collective-permute-start(f32[2,5,2,2,8,128]{5,4,3,2,1,0:T(8,128)S(1)} %get-tuple-element.36), channel_id=1, source_target_pairs={{0,1},{1,0},{2,3},{3,2},{4,5},{5,4},{6,7},{7,6},{8,9},{9,8},{10,11... | collective-permute-start | bytes 491528 | tf_op jit(solution)/shard_map/ppermute | solution.py:598
  19.2 15.4 %all-to-all-start = ((f32[64,3,1,128]{3,2,1,0:T(1,128)}), f32[64,3,1,128]{3,2,1,0:T(1,128)S(1)}, u32[]{:S(2)}, u32[]{:S(2)}) async-start(f32[64,3,1,128]{3,2,1,0:T(1,128)} %bitcast.3), calls=%async_computation | async-start | bytes 196608 | tf_op jit(solution)/shard_map/all_to_all | solution.py:601
  24.1 6.6 %collective-permute-start.6 = (f32[5,2,2,8,128]{4,3,2,1,0:T(8,128)S(1)}, f32[5,2,2,8,128]{4,3,2,1,0:T(8,128)S(1)}, u32[]{:S(2)}, u32[]{:S(2)}) collective-permute-start(f32[5,2,2,8,128]{4,3,2,1,0:T(8,128)S(1)} %get-tuple-element.37), channel_id=1, source_target_pairs={{0,2},{1,3},{2,0},{3,1},{4,6},{5,7},{6,4},{7,5},{8,10},{9,11},{10,... | collective-permute-start | bytes 245768 | tf_op jit(solution)/shard_map/ppermute | solution.py:598
  25.7 6.8 %collective-permute-start.7 = (f32[5,2,2,8,128]{4,3,2,1,0:T(8,128)S(1)}, f32[5,2,2,8,128]{4,3,2,1,0:T(8,128)S(1)}, u32[]{:S(2)}, u32[]{:S(2)}) collective-permute-start(f32[5,2,2,8,128]{4,3,2,1,0:T(8,128)S(1)} %get-tuple-element.38), channel_id=1, source_target_pairs={{0,2},{1,3},{2,0},{3,1},{4,6},{5,7},{6,4},{7,5},{8,10},{9,11},{10,... | collective-permute-start | bytes 245768 | tf_op jit(solution)/shard_map/ppermute | solution.py:598
  30.7 5.1 %collective-permute-start.8 = (f32[5,2,2,8,128]{4,3,2,1,0:T(8,128)S(1)}, f32[5,2,2,8,128]{4,3,2,1,0:T(8,128)S(1)}, u32[]{:S(2)}, u32[]{:S(2)}) collective-permute-start(f32[5,2,2,8,128]{4,3,2,1,0:T(8,128)S(1)} %shard_map.42), channel_id=1, source_target_pairs={{0,4},{1,5},{2,6},{3,7},{4,0},{5,1},{6,2},{7,3},{8,12},{9,13},{10,... | collective-permute-start | bytes 245768 | tf_op jit(solution)/shard_map/ppermute | solution.py:598
  32.6 4.5 %collective-permute-start.9 = (f32[5,2,2,8,128]{4,3,2,1,0:T(8,128)S(1)}, f32[5,2,2,8,128]{4,3,2,1,0:T(8,128)S(1)}, u32[]{:S(2)}, u32[]{:S(2)}) collective-permute-start(f32[5,2,2,8,128]{4,3,2,1,0:T(8,128)S(1)} %shard_map.43), channel_id=1, source_target_pairs={{0,4},{1,5},{2,6},{3,7},{4,0},{5,1},{6,2},{7,3},{8,12},{9,13},{10,... | collective-permute-start | bytes 245768 | tf_op jit(solution)/shard_map/ppermute | solution.py:598

commit v10 on v9

--- a/solution.py
+++ b/solution.py
@@ -320,7 +320,7 @@
         return 0
 
     for body in (along_first, along_second, third_states, third_fluxes, third_change):
-        unroll = 8 if body in (third_states, third_change) else 4
+        unroll = 4 if body in (along_first, along_second) else 8
         lax.fori_loop(0, 8, body, 0, unroll=unroll)
 
 

time: 38.2 us -> 38.3 us (level)
  no operation moved by 1% of the time
where the time goes in v10:
time: 38.3 us; the launch traced here: 38 us
  starting transfers between devices  25.3 us (66%)
  Pallas kernels  6.89 us (18%)
  waiting for transfers between devices  5.71 us (15%)
    ppermute x5, starting transfers between devices, on_device(): lax.ppermute(block, 'by', [(k, k ^ m) for k in range(columns)])  9.61 us
    pallas_call x8, Pallas kernels, call(): pl.pallas_call(kernel, in_specs=[VMEM] * (len(inputs) - hbm_in) + [ANY] *...  6.89 us
    all_to_all x1, starting transfers between devices, on_device(): top = lax.all_to_all(top, ('bx', 'by'), 0, 0, axis_index_groups=groups)  4.84 us
    ppermute x1, starting transfers between devices, on_device(): lax.ppermute(e_by, 'by', pair_even(columns))  4.63 us
    ppermute x5, waiting for transfers between devices, on_device(): lax.ppermute(block, 'by', [(k, k ^ m) for k in range(columns)])  4.37 us
    ppermute x1, starting transfers between devices, on_device(): lax.ppermute(slabs[-1], 'by', [(k, k ^ 2) for k in range(columns)])  2.47 us
    ppermute x1, starting transfers between devices, on_device(): lax.ppermute(o_bx, 'bx', pair_odd(rows))  2.17 us
    ppermute x1, starting transfers between devices, on_device(): lax.ppermute(o_by, 'by', pair_odd(columns))  1.58 us
  transfers between devices with their start and end apart: 11, of which 5 were waited for; matrix products, arithmetic and copies ran while one was open for 0% of the time, Pallas kernels for 9%

profile of v10, /device:TPU:2, one launch (start us, length us, event | category | flops | bytes accessed | tf_op | source)
XLA Modules:
  0.0 38.0 jit_solution(5004639099433408658)
XLA Ops:
  0.0 0.0 copy-start
  0.0 1.6 %shard_map.37 = (f32[4,5,2,2,8,128]{5,4,3,2,1,0:T(8,128)S(1)}, f32[4,5,2,2,8,128]{5,4,3,2,1,0:T(8,128)S(1)}, f32[10,8,128]{2,1,0:T(8,128)S(1)}, f32[13,8,128]{2,...) custom-call(f32[5,256,64]{2,1,0:T(8,128)} %bitcast.9), custom_call_target="tpu_custom_call" | custom-call | tf_op jit(solution)/shard_map/pallas_call | solution.py:550
  1.6 0.0 copy-start.1
  1.7 1.6 %collective-permute-start.3 = (f32[14,8,128]{2,1,0:T(8,128)S(1)}, f32[14,8,128]{2,1,0:T(8,128)S(1)}, u32[]{:S(2)}, u32[]{:S(2)}) collective-permute-start(f32[14,8,128]{2,1,0:T(8,128)S(1)} %get-tuple-element.30.so_by), channel_id=1, source_target_pairs={{0,31},{1,2},{2,1},{3,4},{4,3},{5,6},{6,5},{7,8},{8,7},{9,10},{10,... | collective-permute-start | bytes 172040 | tf_op jit(solution)/shard_map/ppermute | solution.py:582
  3.2 2.2 %collective-permute-start.1 = (f32[13,8,128]{2,1,0:T(8,128)S(1)}, f32[13,8,128]{2,1,0:T(8,128)S(1)}, u32[]{:S(2)}, u32[]{:S(2)}) collective-permute-start(f32[13,8,128]{2,1,0:T(8,128)S(1)} %get-tuple-element.28.so_bx), channel_id=1, source_target_pairs={{0,224},{32,64},{64,32},{96,128},{128,96},{160,192},{192,160},{224... | collective-permute-start | bytes 159752 | tf_op jit(solution)/shard_map/ppermute | solution.py:580
  5.4 2.5 %collective-permute-start.4 = (f32[12,8,128]{2,1,0:T(8,128)S(1)}, f32[12,8,128]{2,1,0:T(8,128)S(1)}, u32[]{:S(2)}, u32[]{:S(2)}) collective-permute-start(f32[12,8,128]{2,1,0:T(8,128)S(1)} %get-tuple-element.33.top), channel_id=1, source_target_pairs={{0,2},{1,3},{2,0},{3,1},{4,6},{5,7},{6,4},{7,5},{8,10},{9,11},{10,... | collective-permute-start | bytes 147464 | tf_op jit(solution)/shard_map/ppermute | solution.py:583
  7.9 4.6 %collective-permute-start.2 = (f32[11,8,128]{2,1,0:T(8,128)S(1)}, f32[11,8,128]{2,1,0:T(8,128)S(1)}, u32[]{:S(2)}, u32[]{:S(2)}) collective-permute-start(f32[11,8,128]{2,1,0:T(8,128)S(1)} %get-tuple-element.29.se_by), channel_id=1, source_target_pairs={{0,1},{1,0},{2,3},{3,2},{4,5},{5,4},{6,7},{7,6},{8,9},{9,8},{10,11... | collective-permute-start | bytes 135176 | tf_op jit(solution)/shard_map/ppermute | solution.py:581
  12.5 0.0 collective-permute-start
  12.5 0.0 copy-done
  12.5 0.0 copy-done.1
  12.5 2.1 %shard_map.38 = (f32[4,5,2,2,8,128]{5,4,3,2,1,0:T(8,128)S(1)}, s32[24,128]{1,0:T(8,128)S(1)}) custom-call(s32[3,8,32]{2,1,0:T(8,128)S(1)} %bitcast.8, s32[8,4,32]{2,1,0:T(4,128)S(1)} %bitcast.7, f32[4,5,2,2,8,128]{5,4,3,2,1,0:T(8,128)S(1)} %get-tuple-element.23.w), custom_call_target="tpu_custom_call" | custom-call | tf_op jit(solution)/shard_map/pallas_call | solution.py:550
  14.6 0.0 collective-permute-done.re_bx
  14.6 0.4 %collective-permute-done.2.re_by = f32[11,8,128]{2,1,0:T(8,128)S(1)} collective-permute-done((f32[11,8,128]{2,1,0:T(8,128)S(1)}, f32[11,8,128]{2,1,0:T(8,128)S(1)}, u32[]{:S(2)}, u32[]{:S(2)}) %collective-permute-start.2) | collective-permute-done | bytes 45088 | tf_op jit(solution)/shard_map/ppermute | solution.py:581
  15.0 0.0 collective-permute-done.4.top2
  15.1 0.0 collective-permute-done.1.ro_bx
  15.1 0.0 collective-permute-done.3.ro_by
  15.1 1.0 %shard_map.39 = (f32[4,5,2,2,8,128]{5,4,3,2,1,0:T(8,128)S(1)}, f32[2,5,2,2,8,128]{5,4,3,2,1,0:T(8,128)S(1)}, f32[24,8,128]{2,1,0:T(8,128)}) custom-call(s32[24,128]{1,0:T(8,128)S(1)} %get-tuple-element.24.plan, f32[4,5,2,2,8,128]{5,4,3,2,1,0:T(8,128)S(1)} %get-tuple-element.25.u.own, f32[4,5,2,2,8,128]{5,4,3,2,1,0:T(8,128)S(1)} %get-tuple-element.26.d_in, ...), custom_call_target="tpu_custom_call" | custom-call | tf_op jit(solution)/shard_map/pallas_call | solution.py:550
  16.1 3.1 %collective-permute-start.5 = (f32[2,5,2,2,8,128]{5,4,3,2,1,0:T(8,128)S(1)}, f32[2,5,2,2,8,128]{5,4,3,2,1,0:T(8,128)S(1)}, u32[]{:S(2)}, u32[]{:S(2)}) collective-permute-start(f32[2,5,2,2,8,128]{5,4,3,2,1,0:T(8,128)S(1)} %get-tuple-element.36), channel_id=1, source_target_pairs={{0,1},{1,0},{2,3},{3,2},{4,5},{5,4},{6,7},{7,6},{8,9},{9,8},{10,11... | collective-permute-start | bytes 491528 | tf_op jit(solution)/shard_map/ppermute | solution.py:598
  19.2 4.8 %all-to-all-start = ((f32[64,3,1,128]{3,2,1,0:T(1,128)}), f32[64,3,1,128]{3,2,1,0:T(1,128)S(1)}, u32[]{:S(2)}, u32[]{:S(2)}) async-start(f32[64,3,1,128]{3,2,1,0:T(1,128)} %bitcast.3), calls=%async_computation | async-start | bytes 196608 | tf_op jit(solution)/shard_map/all_to_all | solution.py:601
  24.0 0.0 collective-permute-done.5.got1
  24.0 0.1 shard_map.40
  24.1 1.6 %collective-permute-start.6 = (f32[5,2,2,8,128]{4,3,2,1,0:T(8,128)S(1)}, f32[5,2,2,8,128]{4,3,2,1,0:T(8,128)S(1)}, u32[]{:S(2)}, u32[]{:S(2)}) collective-permute-start(f32[5,2,2,8,128]{4,3,2,1,0:T(8,128)S(1)} %get-tuple-element.37), channel_id=1, source_target_pairs={{0,2},{1,3},{2,0},{3,1},{4,6},{5,7},{6,4},{7,5},{8,10},{9,11},{10,... | collective-permute-start | bytes 245768 | tf_op jit(solution)/shard_map/ppermute | solution.py:598
  25.7 2.0 %collective-permute-start.7 = (f32[5,2,2,8,128]{4,3,2,1,0:T(8,128)S(1)}, f32[5,2,2,8,128]{4,3,2,1,0:T(8,128)S(1)}, u32[]{:S(2)}, u32[]{:S(2)}) collective-permute-start(f32[5,2,2,8,128]{4,3,2,1,0:T(8,128)S(1)} %get-tuple-element.38), channel_id=1, source_target_pairs={{0,2},{1,3},{2,0},{3,1},{4,6},{5,7},{6,4},{7,5},{8,10},{9,11},{10,... | collective-permute-start | bytes 245768 | tf_op jit(solution)/shard_map/ppermute | solution.py:598
  27.7 3.0 %collective-permute-done.6.got_u.got2 = f32[5,2,2,8,128]{4,3,2,1,0:T(8,128)S(1)} collective-permute-done((f32[5,2,2,8,128]{4,3,2,1,0:T(8,128)S(1)}, f32[5,2,2,8,128]{4,3,2,1,0:T(8,128)S(1)}, u32[]{:S(2)}, u32[]{:S(2)}) %collective-permute-start.6) | collective-permute-done | bytes 81952 | tf_op jit(solution)/shard_map/ppermute | solution.py:598
  30.7 0.1 shard_map.42
  30.7 1.8 %collective-permute-start.8 = (f32[5,2,2,8,128]{4,3,2,1,0:T(8,128)S(1)}, f32[5,2,2,8,128]{4,3,2,1,0:T(8,128)S(1)}, u32[]{:S(2)}, u32[]{:S(2)}) collective-permute-start(f32[5,2,2,8,128]{4,3,2,1,0:T(8,128)S(1)} %shard_map.42), channel_id=1, source_target_pairs={{0,4},{1,5},{2,6},{3,7},{4,0},{5,1},{6,2},{7,3},{8,12},{9,13},{10,... | collective-permute-start | bytes 245768 | tf_op jit(solution)/shard_map/ppermute | solution.py:598
  32.5 0.0 collective-permute-done.7.got_d.got2
  32.5 0.1 shard_map.43
  32.6 1.1 %collective-permute-start.9 = (f32[5,2,2,8,128]{4,3,2,1,0:T(8,128)S(1)}, f32[5,2,2,8,128]{4,3,2,1,0:T(8,128)S(1)}, u32[]{:S(2)}, u32[]{:S(2)}) collective-permute-start(f32[5,2,2,8,128]{4,3,2,1,0:T(8,128)S(1)} %shard_map.43), channel_id=1, source_target_pairs={{0,4},{1,5},{2,6},{3,7},{4,0},{5,1},{6,2},{7,3},{8,12},{9,13},{10,... | collective-permute-start | bytes 245768 | tf_op jit(solution)/shard_map/ppermute | solution.py:598
  33.7 0.9 %all-to-all-done = f32[64,3,1,128]{3,2,1,0:T(1,128)S(1)} async-done(((f32[64,3,1,128]{3,2,1,0:T(1,128)}), f32[64,3,1,128]{3,2,1,0:T(1,128)S(1)}, u32[]{:S(2)}, u32[]{:S(2)}) %all-to-all-start) | async-done | bytes 98336 | tf_op jit(solution)/shard_map/all_to_all | solution.py:601
  34.6 1.1 %shard_map.41 = (f32[8,128]{1,0:T(8,128)S(1)}, f32[4,5,16,256]{3,2,1,0:T(8,128)}) custom-call(s32[24,128]{1,0:T(8,128)S(1)} %get-tuple-element.24.plan, f32[4,5,2,2,8,128]{5,4,3,2,1,0:T(8,128)S(1)} %get-tuple-element.25.u.own, f32[4,5,2,2,8,128]{5,4,3,2,1,0:T(8,128)S(1)} %get-tuple-element.34.d.own, f32[24,8,128]{2,1,0:T(8,128)S(1)} %bitcast.6, ...), custom_call_target="tpu_custom_call" | custom-call | tf_op jit(solution)/shard_map/pallas_call | solution.py:550
  35.7 0.1 collective-permute-done.8.got_u
  35.8 1.3 %collective-permute-done.9.got_d = f32[5,2,2,8,128]{4,3,2,1,0:T(8,128)S(1)} collective-permute-done((f32[5,2,2,8,128]{4,3,2,1,0:T(8,128)S(1)}, f32[5,2,2,8,128]{4,3,2,1,0:T(8,128)S(1)}, u32[]{:S(2)}, u32[]{:S(2)}) %collective-permute-start.9) | collective-permute-done | bytes 81952 | tf_op jit(solution)/shard_map/ppermute | solution.py:598
  37.1 0.9 %shard_map.44 = f32[4,5,16,256]{3,2,1,0:T(8,128)} custom-call(s32[24,128]{1,0:T(8,128)S(1)} %get-tuple-element.24.plan, f32[8,128]{1,0:T(8,128)S(1)} %get-tuple-element.39.step, f32[5,2,2,8,128]{4,3,2,1,0:T(8,128)S(1)} %collective-permute-done.8.got_u, f32[5,2,2,8,128]{4,3,2,1,0:T(8,128)S(1)} %collective-permute-done.9.got_d, ...), custom_call_target="tpu_custom_call", output_to_operand_aliasing={{}: (4, {})} | custom-call | tf_op jit(solution)/shard_map/pallas_call | solution.py:550
Async XLA Ops:
  0.0 12.5 %copy-start = (s32[8,32,4]{1,2,0:T(4,128)S(1)}, s32[8,32,4]{1,2,0:T(4,128)}, u32[]{:S(2)}) copy-start(s32[8,32,4]{1,2,0:T(4,128)} %param.4) | copy-start | bytes 12292
  1.6 10.9 %copy-start.1 = (s32[8,32,3]{1,0,2:T(8,128)S(1)}, s32[8,32,3]{1,0,2:T(8,128)}, u32[]{:S(2)}) copy-start(s32[8,32,3]{1,0,2:T(8,128)} %param.5) | copy-start | bytes 9220
  1.7 13.4 %collective-permute-start.3 = (f32[14,8,128]{2,1,0:T(8,128)S(1)}, f32[14,8,128]{2,1,0:T(8,128)S(1)}, u32[]{:S(2)}, u32[]{:S(2)}) collective-permute-start(f32[14,8,128]{2,1,0:T(8,128)S(1)} %get-tuple-element.30.so_by), channel_id=1, source_target_pairs={{0,31},{1,2},{2,1},{3,4},{4,3},{5,6},{6,5},{7,8},{8,7},{9,10},{10,... | collective-permute-start | bytes 172040 | tf_op jit(solution)/shard_map/ppermute | solution.py:582
  3.2 11.8 %collective-permute-start.1 = (f32[13,8,128]{2,1,0:T(8,128)S(1)}, f32[13,8,128]{2,1,0:T(8,128)S(1)}, u32[]{:S(2)}, u32[]{:S(2)}) collective-permute-start(f32[13,8,128]{2,1,0:T(8,128)S(1)} %get-tuple-element.28.so_bx), channel_id=1, source_target_pairs={{0,224},{32,64},{64,32},{96,128},{128,96},{160,192},{192,160},{224... | collective-permute-start | bytes 159752 | tf_op jit(solution)/shard_map/ppermute | solution.py:580
  5.4 9.6 %collective-permute-start.4 = (f32[12,8,128]{2,1,0:T(8,128)S(1)}, f32[12,8,128]{2,1,0:T(8,128)S(1)}, u32[]{:S(2)}, u32[]{:S(2)}) collective-permute-start(f32[12,8,128]{2,1,0:T(8,128)S(1)} %get-tuple-element.33.top), channel_id=1, source_target_pairs={{0,2},{1,3},{2,0},{3,1},{4,6},{5,7},{6,4},{7,5},{8,10},{9,11},{10,... | collective-permute-start | bytes 147464 | tf_op jit(solution)/shard_map/ppermute | solution.py:583
  7.9 7.2 %collective-permute-start.2 = (f32[11,8,128]{2,1,0:T(8,128)S(1)}, f32[11,8,128]{2,1,0:T(8,128)S(1)}, u32[]{:S(2)}, u32[]{:S(2)}) collective-permute-start(f32[11,8,128]{2,1,0:T(8,128)S(1)} %get-tuple-element.29.se_by), channel_id=1, source_target_pairs={{0,1},{1,0},{2,3},{3,2},{4,5},{5,4},{6,7},{7,6},{8,9},{9,8},{10,11... | collective-permute-start | bytes 135176 | tf_op jit(solution)/shard_map/ppermute | solution.py:581
  12.5 2.1 %collective-permute-start = (f32[10,8,128]{2,1,0:T(8,128)S(1)}, f32[10,8,128]{2,1,0:T(8,128)S(1)}, u32[]{:S(2)}, u32[]{:S(2)}) collective-permute-start(f32[10,8,128]{2,1,0:T(8,128)S(1)} %get-tuple-element.27.se_bx), channel_id=1, source_target_pairs={{0,32},{32,0},{64,96},{96,64},{128,160},{160,128},{192,224},{224,1... | collective-permute-start | bytes 122888 | tf_op jit(solution)/shard_map/ppermute | solution.py:579
  16.1 8.0 %collective-permute-start.5 = (f32[2,5,2,2,8,128]{5,4,3,2,1,0:T(8,128)S(1)}, f32[2,5,2,2,8,128]{5,4,3,2,1,0:T(8,128)S(1)}, u32[]{:S(2)}, u32[]{:S(2)}) collective-permute-start(f32[2,5,2,2,8,128]{5,4,3,2,1,0:T(8,128)S(1)} %get-tuple-element.36), channel_id=1, source_target_pairs={{0,1},{1,0},{2,3},{3,2},{4,5},{5,4},{6,7},{7,6},{8,9},{9,8},{10,11... | collective-permute-start | bytes 491528 | tf_op jit(solution)/shard_map/ppermute | solution.py:598
  19.2 15.4 %all-to-all-start = ((f32[64,3,1,128]{3,2,1,0:T(1,128)}), f32[64,3,1,128]{3,2,1,0:T(1,128)S(1)}, u32[]{:S(2)}, u32[]{:S(2)}) async-start(f32[64,3,1,128]{3,2,1,0:T(1,128)} %bitcast.3), calls=%async_computation | async-start | bytes 196608 | tf_op jit(solution)/shard_map/all_to_all | solution.py:601
  24.1 6.6 %collective-permute-start.6 = (f32[5,2,2,8,128]{4,3,2,1,0:T(8,128)S(1)}, f32[5,2,2,8,128]{4,3,2,1,0:T(8,128)S(1)}, u32[]{:S(2)}, u32[]{:S(2)}) collective-permute-start(f32[5,2,2,8,128]{4,3,2,1,0:T(8,128)S(1)} %get-tuple-element.37), channel_id=1, source_target_pairs={{0,2},{1,3},{2,0},{3,1},{4,6},{5,7},{6,4},{7,5},{8,10},{9,11},{10,... | collective-permute-start | bytes 245768 | tf_op jit(solution)/shard_map/ppermute | solution.py:598
  25.7 6.8 %collective-permute-start.7 = (f32[5,2,2,8,128]{4,3,2,1,0:T(8,128)S(1)}, f32[5,2,2,8,128]{4,3,2,1,0:T(8,128)S(1)}, u32[]{:S(2)}, u32[]{:S(2)}) collective-permute-start(f32[5,2,2,8,128]{4,3,2,1,0:T(8,128)S(1)} %get-tuple-element.38), channel_id=1, source_target_pairs={{0,2},{1,3},{2,0},{3,1},{4,6},{5,7},{6,4},{7,5},{8,10},{9,11},{10,... | collective-permute-start | bytes 245768 | tf_op jit(solution)/shard_map/ppermute | solution.py:598
  30.7 5.1 %collective-permute-start.8 = (f32[5,2,2,8,128]{4,3,2,1,0:T(8,128)S(1)}, f32[5,2,2,8,128]{4,3,2,1,0:T(8,128)S(1)}, u32[]{:S(2)}, u32[]{:S(2)}) collective-permute-start(f32[5,2,2,8,128]{4,3,2,1,0:T(8,128)S(1)} %shard_map.42), channel_id=1, source_target_pairs={{0,4},{1,5},{2,6},{3,7},{4,0},{5,1},{6,2},{7,3},{8,12},{9,13},{10,... | collective-permute-start | bytes 245768 | tf_op jit(solution)/shard_map/ppermute | solution.py:598
  32.6 4.5 %collective-permute-start.9 = (f32[5,2,2,8,128]{4,3,2,1,0:T(8,128)S(1)}, f32[5,2,2,8,128]{4,3,2,1,0:T(8,128)S(1)}, u32[]{:S(2)}, u32[]{:S(2)}) collective-permute-start(f32[5,2,2,8,128]{4,3,2,1,0:T(8,128)S(1)} %shard_map.43), channel_id=1, source_target_pairs={{0,4},{1,5},{2,6},{3,7},{4,0},{5,1},{6,2},{7,3},{8,12},{9,13},{10,... | collective-permute-start | bytes 245768 | tf_op jit(solution)/shard_map/ppermute | solution.py:598
